TPU v7x, 128 devices: a whole 4x4x4 slice. The times are simulated.
128 devices in a mesh: grp: 2 (over core), vocab: 32 (over x_hi, y, z), seq: 2 (over x_lo).
Axes of the slice: x: 4 (x_hi: 2, x_lo: 2; x = x_hi * 2 + x_lo), y: 4, z: 4, core: 2. Of those that a mesh axis runs over, the one named last changes fastest.
Arguments:
- teacher_rows: bfloat16 [256, 8192], P('vocab', ('grp', 'seq')), may hold values from -104 to 104
- student_rows: bfloat16 [256, 4096], P(('grp', 'vocab')), may hold values from -104 to 104
- teacher_head: bfloat16 [8192, 2, 64128], P(('grp', 'seq'), None, 'vocab'), may hold values from -0.0625 to 0.0625
- student_head: bfloat16 [4096, 128256], P(None, ('grp', 'vocab', 'seq')), may hold values from -0.09375 to 0.09375
- targets: int32 [256], replicated, may hold values from 0 to 128255
- loss_grad: float32 [256], replicated, may hold values from 10 to 100
Outputs:
- hidden_grad: bfloat16 [256, 4096], P(('grp', 'vocab', 'seq'))
- token_loss: float32 [256], replicated
All inputs are finite; a program needn't handle non-finite values.
Results may differ from a plain program's by a relative error of at most 0.014.
Values may be sent and summed in bfloat16 or wider, within the bound.
No kernel may reach another device: no remote copies, remote signals or barrier semaphores. Data moves between devices by JAX's collectives and lax.ppermute only.
A program may use at most 128 MiB of HBM per device.

v0:
```python
import jax
import jax.numpy as jnp
from jax import lax
from jax.sharding import PartitionSpec as P


def body(teacher_rows, student_rows, teacher_head, student_head, targets, loss_grad):
    shards = lax.axis_size("vocab")
    seq_parts = lax.axis_size("seq")
    column_width = student_head.shape[1]
    quarter = teacher_head.shape[0]
    gathered = lax.all_gather(teacher_rows, "vocab", axis=0, tiled=True)
    tokens = gathered.shape[0]
    offset = jnp.int32(0)
    pieces = []
    for turn_index in range(tokens * lax.axis_size(("grp", "seq")) // tokens):
        block_index = offset // tokens + turn_index
        column_half = block_index // seq_parts
        column_part = block_index % seq_parts
        weight = lax.dynamic_slice(
            teacher_head,
            (jnp.int32(0), column_half, column_part * column_width),
            (quarter, 1, column_width),
        )
        pieces.append(jnp.dot(gathered, weight[:, 0, :], preferred_element_type=jnp.float32))
    teacher_logits = lax.psum_scatter(
        jnp.concatenate(pieces, axis=0), ("grp", "seq"), scatter_dimension=0, tiled=True
    )
    student_logits = jnp.dot(
        lax.all_gather(student_rows, ("grp", "vocab"), axis=0, tiled=True),
        student_head,
        preferred_element_type=jnp.float32,
    )
    shard_index = (
        lax.axis_index("grp") * shards + lax.axis_index("vocab")
    ) * seq_parts + lax.axis_index("seq")
    columns = shard_index * column_width + lax.iota(jnp.int32, column_width)
    onehot = targets[:, None] == columns[None, :]
    picked_local = jnp.sum(
        jnp.where(onehot, student_logits, jnp.zeros_like(student_logits)), axis=1
    )
    difference = teacher_logits - student_logits
    teacher_top = jnp.max(teacher_logits, axis=1)
    student_top = jnp.max(student_logits, axis=1)
    teacher_top, student_top = lax.pmax((teacher_top, student_top), ("grp", "vocab", "seq"))
    teacher_exp = jnp.exp(teacher_logits - teacher_top[:, None])
    student_exp = jnp.exp(student_logits - student_top[:, None])
    totals = lax.psum(
        (
            jnp.sum(teacher_exp, axis=1),
            jnp.sum(student_exp, axis=1),
            jnp.sum(teacher_exp * difference, axis=1),
            picked_local,
        ),
        ("grp", "vocab", "seq"),
    )
    teacher_norm = teacher_top + jnp.log(totals[0])
    student_norm = student_top + jnp.log(totals[1])
    weighted = totals[2] / totals[0]
    picked = totals[3]
    teacher_probs = teacher_exp / totals[0][:, None]
    student_probs = student_exp / totals[1][:, None]
    token_loss = weighted - teacher_norm + 2.0 * student_norm - picked
    logit_grad = (
        loss_grad[:, None] * (2.0 * student_probs - teacher_probs - onehot.astype(jnp.float32))
    ).astype(jnp.bfloat16)
    hidden_grad = lax.psum_scatter(
        lax.dot_general(
            logit_grad, student_head, (((1,), (1,)), ((), ())), preferred_element_type=jnp.float32
        ),
        ("grp", "vocab", "seq"),
        scatter_dimension=0,
        tiled=True,
    )
    return (hidden_grad.astype(jnp.bfloat16), token_loss)


def solution(mesh):
    return jax.shard_map(
        body,
        mesh=mesh,
        in_specs=(
            P("vocab", ("grp", "seq")),
            P(("grp", "vocab"), None),
            P(("grp", "seq"), None, "vocab"),
            P(None, ("grp", "vocab", "seq")),
            P(),
            P(),
        ),
        out_specs=(P(("grp", "vocab", "seq"), None), P()),
        check_vma=False,
    )
```

profile of v0, /device:TPU:0, one launch (start us, length us, event | category | flops | bytes accessed | tf_op | source)
XLA Modules:
  0.0 478.8 jit_solution(16317583905134921405)
XLA Ops:
  7.2 0.0 all-gather.4.cloned.1.call-start
  7.2 0.7 all-gather.4.cloned.1.call-update
  7.9 0.0 all-gather.6.cloned.1.call-start
  7.9 0.7 all-gather.6.cloned.1.call-update
  8.6 0.0 reduce-scatter.2.cloned.1.call-start
  8.7 31.8 %fusion.21 = (bf16[2048,1,1002]{0,1,2:T(2,128)(2,1)}, bf16[2048,1,1002]{0,1,2:T(2,128)(2,1)}, bf16[2048,1,1002]{0,1,2:T(2,128)(2,1)}, bf16[2048,1,1002]{0,1,2:T(2,128)(2,1)}) fusion(bf16[2048,2,2004]{0,1,2:T(2,128)(2,1)} %param.8), kind=kLoop, calls=%fused_computation.33 | loop fusion | bytes 32833536 | tf_op jit(solution)/shard_map/dynamic_slice | solution.py:20
  40.5 40.3 %all-gather.4.cloned.1.call-done = bf16[256,2048]{1,0:T(8,128)(2,1)} async-done(((bf16[8,2048]{1,0:T(8,128)(2,1)}), bf16[256,2048]{1,0:T(8,128)(2,1)}) %all-gather.4.cloned.1.call-update) | async-done | bytes 1048592 | tf_op jit(solution)/shard_map/all_gather | solution.py:12
  80.7 0.0 copy-start.1
  80.7 0.0 slice-start.2
  80.7 6.2 %fusion = f32[256,1002]{0,1:T(8,128)S(1)} fusion(bf16[256,2048]{1,0:T(8,128)(2,1)} %all-gather.4.cloned.1.call-done, bf16[2048,1,1002]{0,1,2:T(2,128)(2,1)} %get-tuple-element.16), kind=kOutput, calls=%fused_computation.2 | convolution fusion | flops 1050673152 | bytes 6178816 | tf_op jit(solution)/shard_map/dot_general | solution.py:25
  87.0 0.0 slice-start.3
  87.0 0.0 copy-done.1
  87.0 0.0 slice-start
  87.0 5.9 %fusion.1 = f32[256,1002]{0,1:T(8,128)S(1)} fusion(bf16[256,2048]{1,0:T(8,128)(2,1)S(1)} %copy-done.1, bf16[2048,1,1002]{0,1,2:T(2,128)(2,1)} %get-tuple-element.14), kind=kOutput, calls=%fused_computation.4 | convolution fusion | flops 1050673152 | bytes 6178816 | tf_op jit(solution)/shard_map/dot_general | solution.py:25
  92.9 0.0 slice-done.2
  92.9 0.0 slice-done.3
  92.9 0.0 slice-start.1
  93.0 2.4 fusion.2
  95.4 0.0 slice-done
  95.4 0.0 slice-done.1
  95.4 2.4 fusion.3
  97.9 2.6 pad_maximum_fusion
  100.4 0.0 reduce-scatter.2.cloned.1.call-update
  100.5 48.9 %all-gather.6.cloned.1.call-done = bf16[64,4,4096]{2,1,0:T(4,128)(2,1)} async-done(((bf16[1,4,4096]{2,1,0:T(4,128)(2,1)}), bf16[64,4,4096]{2,1,0:T(4,128)(2,1)}) %all-gather.6.cloned.1.call-update) | async-done | bytes 2097168 | tf_op jit(solution)/shard_map/all_gather | solution.py:30
  149.4 2.7 reshape.15
  152.1 0.0 copy-start
  152.1 0.0 copy-start.2
  152.1 5.7 %fusion.22 = (f32[256]{0:T(256)S(1)}, f32[256,1002]{0,1:T(8,128)S(1)}) fusion(bf16[256,4096]{1,0:T(8,128)(2,1)S(1)} %reshape.15, bf16[4096,1002]{0,1:T(8,128)(2,1)} %param.9), kind=kOutput, calls=%fused_computation.34 | convolution fusion | flops 2101602560 | bytes 11332608 | tf_op jit(solution)/shard_map/dot_general | solution.py:29
  157.8 69.1 %reduce-scatter.2.cloned.1.call-done = f32[256,1002]{0,1:T(8,128)} async-done(((f32[1024,1002]{0,1:T(8,128)}), f32[256,1002]{0,1:T(8,128)}) %reduce-scatter.2.cloned.1.call-update) | async-done | bytes 1026064 | tf_op jit(solution)/shard_map/reduce_scatter | solution.py:26
  227.0 1.4 reduce_max.19
  228.3 66.1 %all-reduce.3 = (f32[256]{0:T(256)S(1)}, f32[256]{0:T(256)S(1)}) all-reduce(f32[256]{0:T(256)S(1)} %reduce_max.19, f32[256]{0:T(256)S(1)} %get-tuple-element.17), channel_id=1, replica_groups=mesh['grp'=2,'vocab'=32,'seq'=2] {'grp','vocab','seq'}, use_global_device_ids=true, to_apply=%region_6.7 | all-reduce | flops 512 | bytes 4096 | tf_op jit(solution)/shard_map/pmax | solution.py:45
  294.5 0.0 copy-done
  294.5 1.7 multiply_reduce_fusion
  296.2 62.4 %all-reduce.2 = (f32[256]{0:T(256)S(1)}, f32[256]{0:T(256)S(1)}) all-reduce(f32[256]{0:T(256)S(1)} %get-tuple-element.3, f32[256]{0:T(256)S(1)} %get-tuple-element.5), channel_id=1, replica_groups=mesh['grp'=2,'vocab'=32,'seq'=2] {'grp','vocab','seq'}, use_global_device_ids=true, to_apply=%region_8.9 | all-reduce | flops 512 | bytes 4096 | tf_op jit(solution)/shard_map/psum | solution.py:48
  358.6 0.0 copy-done.2
  358.6 8.3 %fusion.10 = f32[256,4096]{1,0:T(8,128)} fusion(bf16[4096,1002]{0,1:T(8,128)(2,1)} %param.9, f32[256,1002]{0,1:T(8,128)} %reduce-scatter.2.cloned.1.call-done, f32[256,1002]{0,1:T(8,128)S(1)} %get-tuple-element.18, s32[256]{0:T(256)S(1)} %copy-done, f32[256]{0:T(256)S(1)} %get-tuple-element.9, f32[256]{0:T(256)S(1)} %get-tuple-element.11, ...), kind=kOutput, calls=%fused_computation.20 | convolution fusion | flops 2104167936 | bytes 14464936 | tf_op jit(solution)/shard_map/dot_general | solution.py:68
  366.9 104.1 %all-reduce.5 = (bf16[256,4096]{1,0:T(8,128)(2,1)S(1)}, f32[256]{0:T(256)S(1)}, f32[256]{0:T(256)S(1)}) all-reduce(f32[256,4096]{1,0:T(8,128)} %fusion.10, f32[256]{0:T(256)S(1)} %get-tuple-element.4, f32[256]{0:T(256)S(1)} %get-tuple-element.2), channel_id=3, replica_groups=mesh['grp'=2,'vocab'=32,'seq'=2] {'grp','vocab','seq'}, use_global_device_ids=true, to_apply=%region_9.10.clone | all-reduce | flops 1049088 | bytes 6295552
  471.0 0.6 add_subtract_fusion
  471.6 0.6 dynamic-slice_convert_fusion
  (3 shorter events, 0.0 us)
Async XLA Ops:
  7.2 73.6 %all-gather.4.cloned.1.call-start = ((), (), s32[]{:S(2)}) async-start(), calls=%async_computation.1 | async-start | bytes 1081344 | tf_op jit(solution)/shard_map/all_gather | solution.py:12
  7.9 141.5 %all-gather.6.cloned.1.call-start = ((), (), s32[]{:S(2)}) async-start(), calls=%async_computation.3 | async-start | bytes 2129920 | tf_op jit(solution)/shard_map/all_gather | solution.py:30
  8.6 218.3 %reduce-scatter.2.cloned.1.call-start = ((), (), s32[]{:S(2)}) async-start(), calls=%async_computation.2 | async-start | bytes 5160960 | tf_op jit(solution)/shard_map/reduce_scatter | solution.py:26
  80.7 6.2 %copy-start.1 = (bf16[256,2048]{1,0:T(8,128)(2,1)S(1)}, bf16[256,2048]{1,0:T(8,128)(2,1)}, u32[]{:S(2)}) copy-start(bf16[256,2048]{1,0:T(8,128)(2,1)} %all-gather.4.cloned.1.call-done) | copy-start | bytes 3145732
  80.7 12.2 %slice-start.2 = ((s8[8208384]{0:T(1024)(128)(4,1)}), s8[4194304]{0:T(1024)(128)(4,1)S(1)}, s32[]{:S(2)}) async-start(s8[8208384]{0:T(1024)(128)(4,1)} %bitcast.22), calls=%async_computation.6 | async-start | bytes 8388608
  87.0 6.0 %slice-start.3 = ((s8[8208384]{0:T(1024)(128)(4,1)}), s8[4014080]{0:T(1024)(128)(4,1)S(1)}, s32[]{:S(2)}) async-start(s8[8208384]{0:T(1024)(128)(4,1)} %bitcast.22), calls=%async_computation.7 | async-start | bytes 8028160
  87.0 8.4 %slice-start = ((s8[8208384]{0:T(1024)(128)(4,1)}), s8[4194304]{0:T(1024)(128)(4,1)S(1)}, s32[]{:S(2)}) async-start(s8[8208384]{0:T(1024)(128)(4,1)} %bitcast.20), calls=%async_computation.4 | async-start | bytes 8388608
  92.9 2.5 slice-start.1
  152.1 142.4 %copy-start = (s32[256]{0:T(256)S(1)}, s32[256]{0:T(256)}, u32[]{:S(2)}) copy-start(s32[256]{0:T(256)} %param.10) | copy-start | bytes 3076
  152.1 206.5 %copy-start.2 = (f32[256]{0:T(256)S(1)}, f32[256]{0:T(256)}, u32[]{:S(2)}) copy-start(f32[256]{0:T(256)} %param.11) | copy-start | bytes 3076
Sparse Core Ops, SparseCore 0:
  11.1 69.6 all-gather.3
  84.0 65.3 all-gather.5
  151.8 75.1 reduce-scatter.1
where the time goes:
time: 479 us
  blocking collectives  233 us (49%)
  waiting for transfers between devices  160 us (33%)
  local copies, waits for them, and re-layouts  35.2 us (7%)
  matrix products  31 us (6%)
  between operations  13.9 us (3%)
  other arithmetic  6.21 us (1%)
    unnamed x1, blocking collectives  104 us
    reduce_scatter x1, waiting for transfers between devices, body(): lax.psum_scatter(jnp.concatenate(pieces, axis=0), ('grp', 'seq'), scatter...  69.1 us
    pmax x1, blocking collectives, body(): lax.pmax((teacher_top, student_top), ('grp', 'vocab', 'seq'))  66.1 us
    psum x1, blocking collectives, body(): lax.psum((jnp.sum(teacher_exp, axis=1), jnp.sum(student_exp, axis=1), jnp...  62.4 us
    all_gather x1, waiting for transfers between devices, body(): lax.all_gather(student_rows, ('grp', 'vocab'), axis=0, tiled=True)  48.9 us
    all_gather x1, waiting for transfers between devices, body(): gathered = lax.all_gather(teacher_rows, 'vocab', axis=0, tiled=True)  40.3 us
    dynamic_slice x1, local copies, waits for them, and re-layouts, body(): lax.dynamic_slice(teacher_head, (jnp.int32(0), column_half, column_part *...  31.8 us
    dot_general x4, matrix products, body(): jnp.dot(gathered, weight[:, 0, :], preferred_element_type=jnp.float32)  17 us
  transfers between devices with their start and end apart: 3, of which 3 were waited for; matrix products, arithmetic and copies ran while one was open for 12% of the time, Pallas kernels for 0%

commit v1 on v0

v1 whole, which is shorter than its diff:
```python
import functools

import jax
import jax.numpy as jnp
from jax import lax
from jax.experimental import pallas as pl
from jax.experimental.pallas import tpu as pltpu
from jax.sharding import PartitionSpec as P

F32 = jnp.float32
BF16 = jnp.bfloat16
BLOCKS = 6
VMEM = pl.BlockSpec(memory_space=pltpu.VMEM)
SMEM = pl.BlockSpec(memory_space=pltpu.SMEM)


def params(mib=48):
    return pltpu.CompilerParams(vmem_limit_bytes=mib * 1024 * 1024)


def call(kernel, out_shape, *args, in_specs=None, scratch=(), mib=48):
    return pl.pallas_call(
        kernel,
        out_shape=out_shape,
        in_specs=in_specs or [VMEM] * len(args),
        out_specs=jax.tree.map(lambda _: VMEM, out_shape),
        scratch_shapes=scratch,
        compiler_params=params(mib),
    )(*args)


def swap_xhi(a):
    return lax.ppermute(a, "vocab", [(i, i ^ 16) for i in range(32)])


def from_z(a, k):
    return lax.ppermute(a, "vocab", [((i & ~3) | ((i + k) & 3), i) for i in range(32)])


def from_y(a, k):
    return lax.ppermute(a, "vocab", [((i & ~12) | ((i + 4 * k) & 12), i) for i in range(32)])


def from_x(a, bits):
    flip = (bits & 1) | ((bits >> 1) << 5)
    return lax.ppermute(a, ("vocab", "seq"), [(i ^ flip, i) for i in range(64)])


def swap_core(a):
    return lax.ppermute(a, "grp", [(0, 1), (1, 0)])


def swap_seq(a):
    return lax.ppermute(a, "seq", [(0, 1), (1, 0)])


def place_z(pieces, ids):
    def kernel(ids_ref, *refs):
        z = ids_ref[3]
        for k in range(4):
            zk = lax.rem(z + k, 4)
            for h in range(2):
                refs[4][h, zk] = refs[k][h]

    _, n, w = pieces[0].shape
    return call(
        kernel, jax.ShapeDtypeStruct((2, 4, n, w), BF16), ids, *pieces, in_specs=[SMEM] + [VMEM] * 4
    )


def place_y(pieces, ids):
    _, _, n, w = pieces[0].shape
    rows = 4 * n

    def kernel(ids_ref, *refs):
        y = ids_ref[2]
        for k in range(4):
            yk = lax.rem(y + k, 4)
            for h in range(2):
                start = pl.multiple_of(h * 4 * rows + yk * rows, rows)
                refs[4][pl.ds(start, rows), :] = refs[k][h].reshape(rows, w)

    return call(
        kernel, jax.ShapeDtypeStruct((8 * rows, w), BF16), ids, *pieces, in_specs=[SMEM] + [VMEM] * 4
    )


def teacher_part(head, rows, ids, mine, first, count):
    width, _, depth = head.shape
    step = width // (2 * BLOCKS)
    tokens = rows.shape[0]

    def place(i, ids_ref):
        part = ids_ref[1] if mine else 1 - ids_ref[1]
        return (part * BLOCKS + first + i, 0, 0)

    def kernel(ids_ref, w_ref, x_ref, own_ref, other_ref, acc):
        g = ids_ref[0]
        w = w_ref[...].reshape(2 * step, depth)
        out = lax.dot_general(w, x_ref[...], (((1,), (1,)), ((), ())), preferred_element_type=F32)
        for lane in range(tokens // 128):
            cols = slice(lane * 128, lane * 128 + 128)
            acc[lane, 0 : 2 * step, :] = out[:, cols]
            own_ref[0, :, cols] = acc[lane, pl.ds(g, step, stride=2), :]
            other_ref[0, :, cols] = acc[lane, pl.ds(1 - g, step, stride=2), :]

    out = jax.ShapeDtypeStruct((count, step, tokens), F32)
    block = pl.BlockSpec((1, step, tokens), lambda i, r: (i, 0, 0))
    return pl.pallas_call(
        kernel,
        grid_spec=pltpu.PrefetchScalarGridSpec(
            num_scalar_prefetch=1,
            grid=(count,),
            in_specs=[
                pl.BlockSpec((step, 2, depth), place),
                pl.BlockSpec((tokens, depth), lambda i, r: (0, 0)),
            ],
            out_specs=[block, block],
            scratch_shapes=[pltpu.VMEM((tokens // 128, 2 * step + 18, 128), F32)],
        ),
        out_shape=[out, out],
        compiler_params=params(),
        cost_estimate=pl.CostEstimate(
            flops=4 * count * step * depth * tokens,
            bytes_accessed=count * step * depth * 4 + tokens * depth * 2,
            transcendentals=0,
        ),
    )(ids, head, rows)


def student_product(head, own, other, ids):
    width, depth = head.shape
    half = own.shape[0]
    block = 256

    def kernel(ids_ref, w_ref, own_ref, other_ref, out_ref, xs):
        @pl.when(pl.program_id(0) == 0)
        def _():
            g = ids_ref[0]
            xs[pl.ds(pl.multiple_of(g * half, half), half), :] = own_ref[...]
            xs[pl.ds(pl.multiple_of((1 - g) * half, half), half), :] = other_ref[...]

        out_ref[...] = lax.dot_general(
            w_ref[...], xs[...], (((1,), (1,)), ((), ())), preferred_element_type=F32
        )

    rows = pl.BlockSpec((half, depth), lambda i, r: (0, 0))
    return pl.pallas_call(
        kernel,
        grid_spec=pltpu.PrefetchScalarGridSpec(
            num_scalar_prefetch=1,
            grid=(pl.cdiv(width, block),),
            in_specs=[pl.BlockSpec((block, depth), lambda i, r: (i, 0)), rows, rows],
            out_specs=pl.BlockSpec((block, 2 * half), lambda i, r: (i, 0)),
            scratch_shapes=[pltpu.VMEM((2 * half, depth), BF16)],
        ),
        out_shape=jax.ShapeDtypeStruct((width, 2 * half), F32),
        compiler_params=params(),
        cost_estimate=pl.CostEstimate(
            flops=4 * width * depth * half, bytes_accessed=2 * width * depth, transcendentals=0
        ),
    )(ids, head, own, other)


def hits(ids_ref, targets_ref, shape):
    columns = ids_ref[4] + lax.broadcasted_iota(jnp.int32, shape, 0)
    return columns == targets_ref[...]


def local_stats(mine, core, near, student, targets, ids):
    width, tokens = student.shape
    step = width // BLOCKS

    def kernel(ids_ref, mine_ref, core_ref, *refs):
        near_refs = refs[: len(near)]
        s_ref, t_ref, tl_ref, out_ref = refs[len(near) :]
        b = 0
        for ref in near_refs:
            for i in range(ref.shape[0]):
                tl_ref[b * step : (b + 1) * step, :] = (mine_ref[b] + core_ref[b]) + ref[i]
                b += 1
        t, s = tl_ref[...], s_ref[...]
        t_top = jnp.max(t, axis=0, keepdims=True)
        s_top = jnp.max(s, axis=0, keepdims=True)
        e = jnp.exp(t - t_top)
        out_ref[0:1, :] = t_top
        out_ref[1:2, :] = jnp.sum(e, axis=0, keepdims=True)
        out_ref[2:3, :] = jnp.sum(e * (t - s), axis=0, keepdims=True)
        out_ref[3:4, :] = s_top
        out_ref[4:5, :] = jnp.sum(jnp.exp(s - s_top), axis=0, keepdims=True)
        hit = hits(ids_ref, t_ref, s.shape)
        out_ref[5:6, :] = jnp.sum(jnp.where(hit, s, jnp.zeros_like(s)), axis=0, keepdims=True)
        out_ref[6:8, :] = jnp.zeros((2, tokens), F32)

    return call(
        kernel,
        [jax.ShapeDtypeStruct((width, tokens), F32), jax.ShapeDtypeStruct((8, tokens), F32)],
        ids,
        mine,
        core,
        *near,
        student,
        targets,
        in_specs=[SMEM] + [VMEM] * (4 + len(near)),
    )


def merge(stats):
    def kernel(*refs):
        out_ref = refs[-1]
        values = [r[...] for r in refs[:-1]]

        def row(v, i):
            return v[i : i + 1, :]

        for top_row, sums in ((0, (1, 2)), (3, (4,))):
            top = functools.reduce(jnp.maximum, [row(v, top_row) for v in values])
            scale = [jnp.exp(row(v, top_row) - top) for v in values]
            out_ref[top_row : top_row + 1, :] = top
            for i in sums:
                out_ref[i : i + 1, :] = sum(c * row(v, i) for c, v in zip(scale, values))
        out_ref[5:6, :] = sum(row(v, 5) for v in values)
        out_ref[6:8, :] = values[0][6:8, :]

    return call(kernel, jax.ShapeDtypeStruct(stats[0].shape, F32), *stats)


def hidden_part(head, teacher, student, stats, targets, loss_grad, ids):
    width, depth = head.shape
    tokens = teacher.shape[1]
    half = tokens // 2
    block = 1024

    def kernel(ids_ref, w_ref, tl_ref, sl_ref, st_ref, t_ref, g_ref, own_ref, other_ref, grad):
        @pl.when(pl.program_id(0) == 0)
        def _():
            st = st_ref[...]
            t_probs = jnp.exp(tl_ref[...] - st[0:1, :]) / st[1:2, :]
            s_probs = jnp.exp(sl_ref[...] - st[3:4, :]) / st[4:5, :]
            hit = hits(ids_ref, t_ref, t_probs.shape)
            value = g_ref[...] * (2.0 * s_probs - t_probs - hit.astype(F32))
            first = ids_ref[0] == 0
            low, high = value[:, :half].T, value[:, half:].T
            grad[0:half, :] = jnp.where(first, low, high).astype(BF16)
            grad[half:tokens, :] = jnp.where(first, high, low).astype(BF16)

        out = jnp.dot(grad[...], w_ref[...], preferred_element_type=F32)
        own_ref[...] = out[:half]
        other_ref[...] = out[half:].astype(BF16)

    def whole(*shape):
        return pl.BlockSpec(shape, lambda i, r: (0, 0))

    out_block = pl.BlockSpec((half, block), lambda i, r: (0, i))
    return pl.pallas_call(
        kernel,
        grid_spec=pltpu.PrefetchScalarGridSpec(
            num_scalar_prefetch=1,
            grid=(depth // block,),
            in_specs=[
                pl.BlockSpec((width, block), lambda i, r: (0, i)),
                whole(width, tokens),
                whole(width, tokens),
                whole(8, tokens),
                whole(1, tokens),
                whole(1, tokens),
            ],
            out_specs=[out_block, out_block],
            scratch_shapes=[pltpu.VMEM((tokens, width), BF16)],
        ),
        out_shape=[
            jax.ShapeDtypeStruct((half, depth), F32),
            jax.ShapeDtypeStruct((half, depth), BF16),
        ],
        compiler_params=params(),
        cost_estimate=pl.CostEstimate(
            flops=2 * width * depth * tokens, bytes_accessed=2 * width * depth, transcendentals=0
        ),
    )(ids, head, teacher, student, stats, targets, loss_grad)


def body(teacher_rows, student_rows, teacher_head, student_head, targets, loss_grad):
    t_head = jnp.transpose(teacher_head, (2, 1, 0))
    s_head = jnp.transpose(student_head, (1, 0))
    width = s_head.shape[0]
    grp, vocab, seq = lax.axis_index("grp"), lax.axis_index("vocab"), lax.axis_index("seq")
    shard = (grp * lax.axis_size("vocab") + vocab) * lax.axis_size("seq") + seq
    ids = jnp.stack([grp, seq, (vocab // 4) % 4, vocab % 4, shard * width]).astype(jnp.int32)
    lower = vocab < 16
    targets2, loss_grad2 = targets.reshape(1, -1), loss_grad.reshape(1, -1)

    def pair(a):
        b = swap_xhi(a)
        return jnp.where(lower, jnp.stack([a, b]), jnp.stack([b, a]))

    a, b = pair(teacher_rows), pair(student_rows)
    a = place_z([a] + [from_z(a, k) for k in (1, 2, 3)], ids)
    b = place_z([b] + [from_z(b, k) for k in (1, 2, 3)], ids)
    a = place_y([a] + [from_y(a, k) for k in (1, 2, 3)], ids)
    b, a = lax.optimization_barrier((b, a))
    b = place_y([b] + [from_y(b, k) for k in (1, 2, 3)], ids)

    near = []
    for first in (0, 2, 4):
        own, other = teacher_part(t_head, a, ids, False, first, 2)
        near.append(swap_seq(own + swap_core(other)))
    mine, other = teacher_part(t_head, a, ids, True, 0, BLOCKS)
    core = swap_core(other)

    student = student_product(s_head, b, swap_core(b), ids)
    teacher, stats = local_stats(mine, core, near, student, targets2, ids)
    stats = merge([stats, swap_core(stats)])
    stats = merge([stats] + [from_x(stats, k) for k in (1, 2, 3)])
    stats = merge([stats] + [from_y(stats, k) for k in (1, 2, 3)])
    stats = merge([stats] + [from_z(stats, k) for k in (1, 2, 3)])

    own, other = hidden_part(s_head, teacher, student, stats, targets2, loss_grad2, ids)
    part = (own + swap_core(other).astype(F32)).astype(BF16)
    part = part.reshape(64, 2, -1)
    part = lax.all_to_all(part, ("vocab", "seq"), 0, 0, tiled=True)
    hidden = jnp.sum(part.astype(F32), axis=0).astype(BF16)

    t_norm = stats[0] + jnp.log(stats[1])
    s_norm = stats[3] + jnp.log(stats[4])
    token_loss = stats[2] / stats[1] - t_norm + 2.0 * s_norm - stats[5]
    return hidden, token_loss


def solution(mesh):
    return jax.shard_map(
        body,
        mesh=mesh,
        in_specs=(
            P("vocab", ("grp", "seq")),
            P(("grp", "vocab"), None),
            P(("grp", "seq"), None, "vocab"),
            P(None, ("grp", "vocab", "seq")),
            P(),
            P(),
        ),
        out_specs=(P(("grp", "vocab", "seq"), None), P()),
        check_vma=False,
    )
```

time: 479 us -> 154 us (0.32)
  blocking collectives: 233 us -> 0 us
  waiting for transfers between devices: 160 us -> 69.1 us
  starting transfers between devices: 0.11 us -> 43.3 us
  Pallas kernels: 0 us -> 34.2 us
  local copies, waits for them, and re-layouts: 35.2 us -> 1.6 us
  matrix products: 31 us -> 0 us
  between operations: 13.9 us -> 0.84 us
    unnamed x1 -> x0, blocking collectives: 104 us -> none
    all_gather x2 -> x0, waiting for transfers between devices: 89.2 us -> none  [the longest x1 48.9 us: body(): lax.all_gather(student_rows, ('grp', 'vocab'), axis=0, tiled=True)]
    reduce_scatter x1 -> x0, waiting for transfers between devices: 69.1 us -> none  [body(): lax.psum_scatter(jnp.concatenate(pieces, axis=0), ('grp', 'seq'), scatter...]
    pmax x1 -> x0, blocking collectives: 66.1 us -> none  [body(): lax.pmax((teacher_top, student_top), ('grp', 'vocab', 'seq'))]
    psum x1 -> x0, blocking collectives: 62.4 us -> none  [body(): lax.psum((jnp.sum(teacher_exp, axis=1), jnp.sum(student_exp, axis=1), jnp...]
    ppermute x0 -> x33, waiting for transfers between devices: none -> 51.4 us  [the longest x3 14.9 us: swap_seq(): return lax.ppermute(a, 'seq', [(0, 1), (1, 0)])]
    ppermute x0 -> x33, starting transfers between devices: none -> 38.4 us  [the longest x9 11.5 us: from_y(): lax.ppermute(a, 'vocab', [(i & ~12 | i + 4 * k & 12, i) for i in range(32)])]
    pallas_call x0 -> x15, Pallas kernels: none -> 34.2 us  [the longest x4 16.9 us: teacher_part(): pl.pallas_call(kernel, grid_spec=pltpu.PrefetchScalarGridSpec(num_scalar_...]
  transfers between devices with their start and end apart: 3 -> 34, of which waited for: 3 -> 23; matrix products, arithmetic and copies ran while one was open for 12% -> 1% of each run, Pallas kernels for 0% -> 16%
where the time goes in v1:
time: 154 us; the launch traced here: 153 us
  waiting for transfers between devices  69.1 us (45%)
  starting transfers between devices  43.3 us (28%)
  Pallas kernels  34.2 us (22%)
  other arithmetic  4.2 us (3%)
  local copies, waits for them, and re-layouts  1.6 us (1%)
    all_to_all x1, waiting for transfers between devices, body(): part = lax.all_to_all(part, ('vocab', 'seq'), 0, 0, tiled=True)  17.7 us
    pallas_call x4, Pallas kernels, teacher_part(): pl.pallas_call(kernel, grid_spec=pltpu.PrefetchScalarGridSpec(num_scalar_...  16.9 us
    ppermute x3, waiting for transfers between devices, swap_seq(): return lax.ppermute(a, 'seq', [(0, 1), (1, 0)])  14.9 us
    ppermute x9, waiting for transfers between devices, from_z(): lax.ppermute(a, 'vocab', [(i & ~3 | i + k & 3, i) for i in range(32)])  12.9 us
    ppermute x9, waiting for transfers between devices, from_y(): lax.ppermute(a, 'vocab', [(i & ~12 | i + 4 * k & 12, i) for i in range(32)])  12.8 us
    ppermute x9, starting transfers between devices, from_y(): lax.ppermute(a, 'vocab', [(i & ~12 | i + 4 * k & 12, i) for i in range(32)])  11.5 us
    ppermute x9, starting transfers between devices, from_z(): lax.ppermute(a, 'vocab', [(i & ~3 | i + k & 3, i) for i in range(32)])  10.5 us
    pallas_call x1, Pallas kernels, hidden_part(): pl.pallas_call(kernel, grid_spec=pltpu.PrefetchScalarGridSpec(num_scalar_...  6.8 us
  transfers between devices with their start and end apart: 34, of which 23 were waited for; matrix products, arithmetic and copies ran while one was open for 1% of the time, Pallas kernels for 16%

profile of v1, /device:TPU:0, one launch (start us, length us, event | category | flops | bytes accessed | tf_op | source)
XLA Modules:
  0.0 153.2 jit_solution(13576870318568712596)
XLA Ops:
  0.6 3.2 %collective-permute-start.4 = (bf16[8,2048]{1,0:T(8,128)(2,1)}, bf16[8,2048]{1,0:T(8,128)(2,1)S(1)}, u32[]{:S(2)}, u32[]{:S(2)}) collective-permute-start(bf16[8,2048]{1,0:T(8,128)(2,1)} %param.6), channel_id=1, source_target_pairs={{0,32},{2,34},{4,36},{6,38},{8,40},{10,42},{12,44},{14,46},{16,48}... | collective-permute-start | bytes 98312 | tf_op jit(solution)/shard_map/ppermute | solution.py:33
  3.8 2.5 %collective-permute-done.4 = bf16[8,2048]{1,0:T(8,128)(2,1)S(1)} collective-permute-done((bf16[8,2048]{1,0:T(8,128)(2,1)}, bf16[8,2048]{1,0:T(8,128)(2,1)S(1)}, u32[]{:S(2)}, u32[]{:S(2)}) %collective-permute-start.4) | collective-permute-done | bytes 32800 | tf_op jit(solution)/shard_map/ppermute | solution.py:33
  7.2 4.2 %collective-permute-start.5 = (bf16[2,8,2048]{2,1,0:T(8,128)(2,1)S(1)}, bf16[2,8,2048]{2,1,0:T(8,128)(2,1)S(1)}, u32[]{:S(2)}, u32[]{:S(2)}) collective-permute-start(bf16[2,8,2048]{2,1,0:T(8,128)(2,1)S(1)} %maximum_select_fusion.1.refs_0_), channel_id=1, source_target_pairs={{2,0},{4,2},{6,4},{0,6},{10,8},{12,10},{14,12},{8,14},{18,16},{20,... | collective-permute-start | bytes 196616 | tf_op jit(solution)/shard_map/ppermute | solution.py:37
  11.4 1.3 collective-permute-start.7
  12.6 3.0 %collective-permute-start = (bf16[4,4096]{1,0:T(4,128)(2,1)}, bf16[4,4096]{1,0:T(4,128)(2,1)S(1)}, u32[]{:S(2)}, u32[]{:S(2)}) collective-permute-start(bf16[4,4096]{1,0:T(4,128)(2,1)} %param.7), channel_id=1, source_target_pairs={{0,32},{2,34},{4,36},{6,38},{8,40},{10,42},{12,44},{14,46},{16,48}... | collective-permute-start | bytes 98312 | tf_op jit(solution)/shard_map/ppermute | solution.py:33
  15.7 1.5 collective-permute-done.6.refs_2_
  18.1 1.6 %collective-permute-start.10 = (bf16[2,4,8,2048]{3,2,1,0:T(8,128)(2,1)S(1)}, bf16[2,4,8,2048]{3,2,1,0:T(8,128)(2,1)S(1)}, u32[]{:S(2)}, u32[]{:S(2)}) collective-permute-start(bf16[2,4,8,2048]{3,2,1,0:T(8,128)(2,1)S(1)} %shard_map.78.refs_0_), channel_id=1, source_target_pairs={{24,0},{26,2},{28,4},{30,6},{0,8},{2,10},{4,12},{6,14},{8,16},{10,... | collective-permute-start | bytes 786440 | tf_op jit(solution)/shard_map/ppermute | solution.py:41
  19.8 1.7 %collective-permute-start.8 = (bf16[2,4,8,2048]{3,2,1,0:T(8,128)(2,1)S(1)}, bf16[2,4,8,2048]{3,2,1,0:T(8,128)(2,1)S(1)}, u32[]{:S(2)}, u32[]{:S(2)}) collective-permute-start(bf16[2,4,8,2048]{3,2,1,0:T(8,128)(2,1)S(1)} %shard_map.78.refs_0_), channel_id=1, source_target_pairs={{8,0},{10,2},{12,4},{14,6},{16,8},{18,10},{20,12},{22,14},{24,16},... | collective-permute-start | bytes 786440 | tf_op jit(solution)/shard_map/ppermute | solution.py:41
  21.4 2.0 %collective-permute-start.9 = (bf16[2,4,8,2048]{3,2,1,0:T(8,128)(2,1)S(1)}, bf16[2,4,8,2048]{3,2,1,0:T(8,128)(2,1)S(1)}, u32[]{:S(2)}, u32[]{:S(2)}) collective-permute-start(bf16[2,4,8,2048]{3,2,1,0:T(8,128)(2,1)S(1)} %shard_map.78.refs_0_), channel_id=1, source_target_pairs={{16,0},{18,2},{20,4},{22,6},{24,8},{26,10},{28,12},{30,14},{0,16},... | collective-permute-start | bytes 786440 | tf_op jit(solution)/shard_map/ppermute | solution.py:41
  23.4 0.9 maximum_select_fusion.refs_0_
  24.3 0.9 collective-permute-start.1
  25.2 1.6 %collective-permute-start.2 = (bf16[2,4,4096]{2,1,0:T(4,128)(2,1)S(1)}, bf16[2,4,4096]{2,1,0:T(4,128)(2,1)S(1)}, u32[]{:S(2)}, u32[]{:S(2)}) collective-permute-start(bf16[2,4,4096]{2,1,0:T(4,128)(2,1)S(1)} %maximum_select_fusion.refs_0_), channel_id=1, source_target_pairs={{4,0},{6,2},{0,4},{2,6},{12,8},{14,10},{8,12},{10,14},{20,16},{22,... | collective-permute-start | bytes 196616 | tf_op jit(solution)/shard_map/ppermute | solution.py:37
  26.9 1.8 %collective-permute-done.1.refs_1_ = bf16[2,4,4096]{2,1,0:T(4,128)(2,1)S(1)} collective-permute-done((bf16[2,4,4096]{2,1,0:T(4,128)(2,1)S(1)}, bf16[2,4,4096]{2,1,0:T(4,128)(2,1)S(1)}, u32[]{:S(2)}, u32[]{:S(2)}) %collective-permute-start.1) | collective-permute-done | bytes 65568 | tf_op jit(solution)/shard_map/ppermute | solution.py:37
  29.1 1.9 %collective-permute-done.2.refs_2_ = bf16[2,4,4096]{2,1,0:T(4,128)(2,1)S(1)} collective-permute-done((bf16[2,4,4096]{2,1,0:T(4,128)(2,1)S(1)}, bf16[2,4,4096]{2,1,0:T(4,128)(2,1)S(1)}, u32[]{:S(2)}, u32[]{:S(2)}) %collective-permute-start.2) | collective-permute-done | bytes 65568 | tf_op jit(solution)/shard_map/ppermute | solution.py:37
  31.0 3.1 %collective-permute-done.3.refs_3_ = bf16[2,4,4096]{2,1,0:T(4,128)(2,1)S(1)} collective-permute-done((bf16[2,4,4096]{2,1,0:T(4,128)(2,1)S(1)}, bf16[2,4,4096]{2,1,0:T(4,128)(2,1)S(1)}, u32[]{:S(2)}, u32[]{:S(2)}) %collective-permute-start.3) | collective-permute-done | bytes 65568 | tf_op jit(solution)/shard_map/ppermute | solution.py:37
  35.4 1.1 collective-permute-start.18
  36.5 1.7 %collective-permute-start.19 = (bf16[2,4,4,4096]{3,2,1,0:T(4,128)(2,1)S(1)}, bf16[2,4,4,4096]{3,2,1,0:T(4,128)(2,1)S(1)}, u32[]{:S(2)}, u32[]{:S(2)}) collective-permute-start(bf16[2,4,4,4096]{3,2,1,0:T(4,128)(2,1)S(1)} %shard_map.77.refs_0_), channel_id=1, source_target_pairs={{16,0},{18,2},{20,4},{22,6},{24,8},{26,10},{28,12},{30,14},{0,16},... | collective-permute-start | bytes 786440 | tf_op jit(solution)/shard_map/ppermute | solution.py:41
  38.4 3.4 %collective-permute-done.18.refs_1_ = bf16[2,4,4,4096]{3,2,1,0:T(4,128)(2,1)S(1)} collective-permute-done((bf16[2,4,4,4096]{3,2,1,0:T(4,128)(2,1)S(1)}, bf16[2,4,4,4096]{3,2,1,0:T(4,128)(2,1)S(1)}, u32[]{:S(2)}, u32[]{:S(2)}) %collective-permute-start.18) | collective-permute-done | bytes 262176 | tf_op jit(solution)/shard_map/ppermute | solution.py:41
  41.8 2.7 %collective-permute-done.19.refs_2_ = bf16[2,4,4,4096]{3,2,1,0:T(4,128)(2,1)S(1)} collective-permute-done((bf16[2,4,4,4096]{3,2,1,0:T(4,128)(2,1)S(1)}, bf16[2,4,4,4096]{3,2,1,0:T(4,128)(2,1)S(1)}, u32[]{:S(2)}, u32[]{:S(2)}) %collective-permute-start.19) | collective-permute-done | bytes 262176 | tf_op jit(solution)/shard_map/ppermute | solution.py:41
  44.5 2.7 %collective-permute-done.20.refs_3_ = bf16[2,4,4,4096]{3,2,1,0:T(4,128)(2,1)S(1)} collective-permute-done((bf16[2,4,4,4096]{3,2,1,0:T(4,128)(2,1)S(1)}, bf16[2,4,4,4096]{3,2,1,0:T(4,128)(2,1)S(1)}, u32[]{:S(2)}, u32[]{:S(2)}) %collective-permute-start.20) | collective-permute-done | bytes 262176 | tf_op jit(solution)/shard_map/ppermute | solution.py:41
  47.9 7.3 %shard_map.80 = (f32[6,167,256]{2,1,0:T(8,128)S(1)}, f32[6,167,256]{2,1,0:T(8,128)S(1)}) custom-call(s32[5]{0:T(128)S(1)} %stack.51.ids_ref, bf16[2004,2,2048]{2,1,0:T(2,128)(2,1)} %bitcast.17, bf16[256,2048]{1,0:T(8,128)(2,1)S(1)} %shard_map.79.x_ref), custom_call_target="tpu_custom_call" | custom-call | flops 2101346304 | bytes 9256960 | tf_op jit(solution)/shard_map/pallas_call | solution.py:109
  55.8 3.2 %shard_map.82 = (f32[2,167,256]{2,1,0:T(8,128)S(1)}, f32[2,167,256]{2,1,0:T(8,128)S(1)}) custom-call(s32[5]{0:T(128)S(1)} %stack.51.ids_ref, bf16[2004,2,2048]{2,1,0:T(2,128)(2,1)} %bitcast.18, bf16[256,2048]{1,0:T(8,128)(2,1)S(1)} %shard_map.79.x_ref), custom_call_target="tpu_custom_call" | custom-call | flops 700448768 | bytes 3784704 | tf_op jit(solution)/shard_map/pallas_call | solution.py:109
  59.1 3.2 %shard_map.83 = (f32[2,167,256]{2,1,0:T(8,128)S(1)}, f32[2,167,256]{2,1,0:T(8,128)S(1)}) custom-call(s32[5]{0:T(128)S(1)} %stack.51.ids_ref, bf16[2004,2,2048]{2,1,0:T(2,128)(2,1)} %bitcast.19, bf16[256,2048]{1,0:T(8,128)(2,1)S(1)} %shard_map.79.x_ref), custom_call_target="tpu_custom_call" | custom-call | flops 700448768 | bytes 3784704 | tf_op jit(solution)/shard_map/pallas_call | solution.py:109
  62.9 3.2 %shard_map.81 = (f32[2,167,256]{2,1,0:T(8,128)S(1)}, f32[2,167,256]{2,1,0:T(8,128)S(1)}) custom-call(s32[5]{0:T(128)S(1)} %stack.51.ids_ref, bf16[2004,2,2048]{2,1,0:T(2,128)(2,1)} %bitcast.20, bf16[256,2048]{1,0:T(8,128)(2,1)S(1)} %shard_map.79.x_ref), custom_call_target="tpu_custom_call" | custom-call | flops 700448768 | bytes 3784704 | tf_op jit(solution)/shard_map/pallas_call | solution.py:109
  66.3 1.6 %collective-permute-start.15 = (f32[2,167,256]{2,1,0:T(8,128)S(1)}, f32[2,167,256]{2,1,0:T(8,128)S(1)}, u32[]{:S(2)}, u32[]{:S(2)}) collective-permute-start(f32[2,167,256]{2,1,0:T(8,128)S(1)} %add.45), channel_id=1, source_target_pairs={{0,1},{1,0},{2,3},{3,2},{4,5},{5,4},{6,7},{7,6},{8,9},{9,8},{10,11... | collective-permute-start | bytes 1026056 | tf_op jit(solution)/shard_map/ppermute | solution.py:54
  68.5 1.6 %collective-permute-start.13 = (f32[2,167,256]{2,1,0:T(8,128)S(1)}, f32[2,167,256]{2,1,0:T(8,128)S(1)}, u32[]{:S(2)}, u32[]{:S(2)}) collective-permute-start(f32[2,167,256]{2,1,0:T(8,128)S(1)} %add.44), channel_id=1, source_target_pairs={{0,1},{1,0},{2,3},{3,2},{4,5},{5,4},{6,7},{7,6},{8,9},{9,8},{10,11... | collective-permute-start | bytes 1026056 | tf_op jit(solution)/shard_map/ppermute | solution.py:54
  70.1 6.5 %shard_map.85.refs_3_.sl_ref = f32[1002,256]{1,0:T(8,128)S(1)} custom-call(s32[5]{0:T(128)S(1)} %stack.51.ids_ref, bf16[1002,4096]{1,0:T(8,128)(2,1)} %bitcast.21, bf16[128,4096]{1,0:T(8,128)(2,1)S(1)} %shard_map.84.own_ref, bf16[128,4096]{1,0:T(8,128)(2,1)S(1)} %collective-permute-done.21.other_ref), custom_call_target="tpu_custom_call" | custom-call | flops 2101346304 | bytes 8208384 | tf_op jit(solution)/shard_map/pallas_call | solution.py:148
  77.2 7.4 %collective-permute-done.17.refs_2_ = f32[2,167,256]{2,1,0:T(8,128)S(1)} collective-permute-done((f32[2,167,256]{2,1,0:T(8,128)S(1)}, f32[2,167,256]{2,1,0:T(8,128)S(1)}, u32[]{:S(2)}, u32[]{:S(2)}) %collective-permute-start.17) | collective-permute-done | bytes 342048 | tf_op jit(solution)/shard_map/ppermute | solution.py:54
  84.6 7.0 %collective-permute-done.13.refs_0_ = f32[2,167,256]{2,1,0:T(8,128)S(1)} collective-permute-done((f32[2,167,256]{2,1,0:T(8,128)S(1)}, f32[2,167,256]{2,1,0:T(8,128)S(1)}, u32[]{:S(2)}, u32[]{:S(2)}) %collective-permute-start.13) | collective-permute-done | bytes 342048 | tf_op jit(solution)/shard_map/ppermute | solution.py:54
  91.5 1.5 shard_map.86
  93.1 1.2 collective-permute-done.22.refs_1_
  94.3 1.6 %collective-permute-start.23 = (f32[8,256]{1,0:T(8,128)S(1)}, f32[8,256]{1,0:T(8,128)S(1)}, u32[]{:S(2)}, u32[]{:S(2)}) collective-permute-start(f32[8,256]{1,0:T(8,128)S(1)} %shard_map.87.refs_0_), channel_id=1, source_target_pairs={{1,0},{0,1},{3,2},{2,3},{5,4},{4,5},{7,6},{6,7},{9,8},{8,9},{11,10... | collective-permute-start | bytes 24584 | tf_op jit(solution)/shard_map/ppermute | solution.py:46
  95.9 2.7 %collective-permute-start.24 = (f32[8,256]{1,0:T(8,128)S(1)}, f32[8,256]{1,0:T(8,128)S(1)}, u32[]{:S(2)}, u32[]{:S(2)}) collective-permute-start(f32[8,256]{1,0:T(8,128)S(1)} %shard_map.87.refs_0_), channel_id=1, source_target_pairs={{32,0},{33,1},{34,2},{35,3},{36,4},{37,5},{38,6},{39,7},{40,8},{41... | collective-permute-start | bytes 24584 | tf_op jit(solution)/shard_map/ppermute | solution.py:46
  99.1 2.0 %collective-permute-done.24.refs_2_ = f32[8,256]{1,0:T(8,128)S(1)} collective-permute-done((f32[8,256]{1,0:T(8,128)S(1)}, f32[8,256]{1,0:T(8,128)S(1)}, u32[]{:S(2)}, u32[]{:S(2)}) %collective-permute-start.24) | collective-permute-done | bytes 8224 | tf_op jit(solution)/shard_map/ppermute | solution.py:46
  101.0 2.4 %collective-permute-done.25.refs_3_ = f32[8,256]{1,0:T(8,128)S(1)} collective-permute-done((f32[8,256]{1,0:T(8,128)S(1)}, f32[8,256]{1,0:T(8,128)S(1)}, u32[]{:S(2)}, u32[]{:S(2)}) %collective-permute-start.25) | collective-permute-done | bytes 8224 | tf_op jit(solution)/shard_map/ppermute | solution.py:46
  104.2 1.7 %collective-permute-start.27 = (f32[8,256]{1,0:T(8,128)S(1)}, f32[8,256]{1,0:T(8,128)S(1)}, u32[]{:S(2)}, u32[]{:S(2)}) collective-permute-start(f32[8,256]{1,0:T(8,128)S(1)} %shard_map.88.refs_0_), channel_id=1, source_target_pairs={{16,0},{18,2},{20,4},{22,6},{24,8},{26,10},{28,12},{30,14},{0,16},... | collective-permute-start | bytes 24584 | tf_op jit(solution)/shard_map/ppermute | solution.py:41
  107.2 2.1 %collective-permute-done.27.refs_2_ = f32[8,256]{1,0:T(8,128)S(1)} collective-permute-done((f32[8,256]{1,0:T(8,128)S(1)}, f32[8,256]{1,0:T(8,128)S(1)}, u32[]{:S(2)}, u32[]{:S(2)}) %collective-permute-start.27) | collective-permute-done | bytes 8224 | tf_op jit(solution)/shard_map/ppermute | solution.py:41
  109.3 1.4 collective-permute-done.28.refs_3_
  110.8 0.9 collective-permute-start.29
  111.7 1.2 collective-permute-start.31
  112.9 1.6 %collective-permute-done.29.refs_1_ = f32[8,256]{1,0:T(8,128)S(1)} collective-permute-done((f32[8,256]{1,0:T(8,128)S(1)}, f32[8,256]{1,0:T(8,128)S(1)}, u32[]{:S(2)}, u32[]{:S(2)}) %collective-permute-start.29) | collective-permute-done | bytes 8224 | tf_op jit(solution)/shard_map/ppermute | solution.py:37
  114.5 2.4 %collective-permute-done.30.refs_2_ = f32[8,256]{1,0:T(8,128)S(1)} collective-permute-done((f32[8,256]{1,0:T(8,128)S(1)}, f32[8,256]{1,0:T(8,128)S(1)}, u32[]{:S(2)}, u32[]{:S(2)}) %collective-permute-start.30) | collective-permute-done | bytes 8224 | tf_op jit(solution)/shard_map/ppermute | solution.py:37
  117.2 6.8 %shard_map.91 = (f32[128,4096]{1,0:T(8,128)S(1)}, bf16[128,4096]{1,0:T(8,128)(2,1)S(1)}) custom-call(s32[5]{0:T(128)S(1)} %stack.51.ids_ref, bf16[1002,4096]{1,0:T(8,128)(2,1)} %bitcast.22, f32[1002,256]{1,0:T(8,128)S(1)} %get-tuple-element.26.tl_ref, f32[1002,256]{1,0:T(8,128)S(1)} %shard_map.85.refs_3_.sl_ref, f32[8,256]{1,0:T(8,128)S(1)} %shard_map.90.st_ref, ...), custom_call_target="tpu_custom_call" | custom-call | flops 2101346304 | bytes 8208384 | tf_op jit(solution)/shard_map/pallas_call | solution.py:255
  124.1 2.6 %collective-permute-done.32 = bf16[128,4096]{1,0:T(8,128)(2,1)S(1)} collective-permute-done((bf16[128,4096]{1,0:T(8,128)(2,1)S(1)}, bf16[128,4096]{1,0:T(8,128)(2,1)S(1)}, u32[]{:S(2)}, u32[]{:S(2)}) %collective-permute-start.32) | collective-permute-done | bytes 1048608 | tf_op jit(solution)/shard_map/ppermute | solution.py:50
  127.0 1.5 reshape.24
  128.5 4.9 %all-to-all-start = ((bf16[64,2,4096]{2,1,0:T(2,128)(2,1)}), bf16[64,2,4096]{2,1,0:T(2,128)(2,1)S(1)}, u32[]{:S(2)}, u32[]{:S(2)}) async-start(bf16[64,2,4096]{2,1,0:T(2,128)(2,1)} %reshape.24), calls=%async_computation | async-start | bytes 2097152 | tf_op jit(solution)/shard_map/all_to_all | solution.py:320
  134.0 17.7 %all-to-all-done = bf16[64,2,4096]{2,1,0:T(2,128)(2,1)S(1)} async-done(((bf16[64,2,4096]{2,1,0:T(2,128)(2,1)}), bf16[64,2,4096]{2,1,0:T(2,128)(2,1)S(1)}, u32[]{:S(2)}, u32[]{:S(2)}) %all-to-all-start) | async-done | bytes 1048608 | tf_op jit(solution)/shard_map/all_to_all | solution.py:320
  151.7 1.5 reduce_sum.12
  (49 shorter events, 10.9 us)
Async XLA Ops:
  0.6 5.7 %collective-permute-start.4 = (bf16[8,2048]{1,0:T(8,128)(2,1)}, bf16[8,2048]{1,0:T(8,128)(2,1)S(1)}, u32[]{:S(2)}, u32[]{:S(2)}) collective-permute-start(bf16[8,2048]{1,0:T(8,128)(2,1)} %param.6), channel_id=1, source_target_pairs={{0,32},{2,34},{4,36},{6,38},{8,40},{10,42},{12,44},{14,46},{16,48}... | collective-permute-start | bytes 98312 | tf_op jit(solution)/shard_map/ppermute | solution.py:33
  7.2 8.6 %collective-permute-start.5 = (bf16[2,8,2048]{2,1,0:T(8,128)(2,1)S(1)}, bf16[2,8,2048]{2,1,0:T(8,128)(2,1)S(1)}, u32[]{:S(2)}, u32[]{:S(2)}) collective-permute-start(bf16[2,8,2048]{2,1,0:T(8,128)(2,1)S(1)} %maximum_select_fusion.1.refs_0_), channel_id=1, source_target_pairs={{2,0},{4,2},{6,4},{0,6},{10,8},{12,10},{14,12},{8,14},{18,16},{20,... | collective-permute-start | bytes 196616 | tf_op jit(solution)/shard_map/ppermute | solution.py:37
  11.4 5.9 %collective-permute-start.6 = (bf16[2,8,2048]{2,1,0:T(8,128)(2,1)S(1)}, bf16[2,8,2048]{2,1,0:T(8,128)(2,1)S(1)}, u32[]{:S(2)}, u32[]{:S(2)}) collective-permute-start(bf16[2,8,2048]{2,1,0:T(8,128)(2,1)S(1)} %maximum_select_fusion.1.refs_0_), channel_id=1, source_target_pairs={{4,0},{6,2},{0,4},{2,6},{12,8},{14,10},{8,12},{10,14},{20,16},{22,... | collective-permute-start | bytes 196616 | tf_op jit(solution)/shard_map/ppermute | solution.py:37
  11.4 6.2 %collective-permute-start.7 = (bf16[2,8,2048]{2,1,0:T(8,128)(2,1)S(1)}, bf16[2,8,2048]{2,1,0:T(8,128)(2,1)S(1)}, u32[]{:S(2)}, u32[]{:S(2)}) collective-permute-start(bf16[2,8,2048]{2,1,0:T(8,128)(2,1)S(1)} %maximum_select_fusion.1.refs_0_), channel_id=1, source_target_pairs={{6,0},{0,2},{2,4},{4,6},{14,8},{8,10},{10,12},{12,14},{22,16},{16,... | collective-permute-start | bytes 196616 | tf_op jit(solution)/shard_map/ppermute | solution.py:37
  12.6 10.8 %collective-permute-start = (bf16[4,4096]{1,0:T(4,128)(2,1)}, bf16[4,4096]{1,0:T(4,128)(2,1)S(1)}, u32[]{:S(2)}, u32[]{:S(2)}) collective-permute-start(bf16[4,4096]{1,0:T(4,128)(2,1)} %param.7), channel_id=1, source_target_pairs={{0,32},{2,34},{4,36},{6,38},{8,40},{10,42},{12,44},{14,46},{16,48}... | collective-permute-start | bytes 98312 | tf_op jit(solution)/shard_map/ppermute | solution.py:33
  18.1 16.6 %collective-permute-start.10 = (bf16[2,4,8,2048]{3,2,1,0:T(8,128)(2,1)S(1)}, bf16[2,4,8,2048]{3,2,1,0:T(8,128)(2,1)S(1)}, u32[]{:S(2)}, u32[]{:S(2)}) collective-permute-start(bf16[2,4,8,2048]{3,2,1,0:T(8,128)(2,1)S(1)} %shard_map.78.refs_0_), channel_id=1, source_target_pairs={{24,0},{26,2},{28,4},{30,6},{0,8},{2,10},{4,12},{6,14},{8,16},{10,... | collective-permute-start | bytes 786440 | tf_op jit(solution)/shard_map/ppermute | solution.py:41
  19.8 14.9 %collective-permute-start.8 = (bf16[2,4,8,2048]{3,2,1,0:T(8,128)(2,1)S(1)}, bf16[2,4,8,2048]{3,2,1,0:T(8,128)(2,1)S(1)}, u32[]{:S(2)}, u32[]{:S(2)}) collective-permute-start(bf16[2,4,8,2048]{3,2,1,0:T(8,128)(2,1)S(1)} %shard_map.78.refs_0_), channel_id=1, source_target_pairs={{8,0},{10,2},{12,4},{14,6},{16,8},{18,10},{20,12},{22,14},{24,16},... | collective-permute-start | bytes 786440 | tf_op jit(solution)/shard_map/ppermute | solution.py:41
  21.4 13.3 %collective-permute-start.9 = (bf16[2,4,8,2048]{3,2,1,0:T(8,128)(2,1)S(1)}, bf16[2,4,8,2048]{3,2,1,0:T(8,128)(2,1)S(1)}, u32[]{:S(2)}, u32[]{:S(2)}) collective-permute-start(bf16[2,4,8,2048]{3,2,1,0:T(8,128)(2,1)S(1)} %shard_map.78.refs_0_), channel_id=1, source_target_pairs={{16,0},{18,2},{20,4},{22,6},{24,8},{26,10},{28,12},{30,14},{0,16},... | collective-permute-start | bytes 786440 | tf_op jit(solution)/shard_map/ppermute | solution.py:41
  24.3 4.3 %collective-permute-start.1 = (bf16[2,4,4096]{2,1,0:T(4,128)(2,1)S(1)}, bf16[2,4,4096]{2,1,0:T(4,128)(2,1)S(1)}, u32[]{:S(2)}, u32[]{:S(2)}) collective-permute-start(bf16[2,4,4096]{2,1,0:T(4,128)(2,1)S(1)} %maximum_select_fusion.refs_0_), channel_id=1, source_target_pairs={{2,0},{4,2},{6,4},{0,6},{10,8},{12,10},{14,12},{8,14},{18,16},{20,... | collective-permute-start | bytes 196616 | tf_op jit(solution)/shard_map/ppermute | solution.py:37
  25.2 5.8 %collective-permute-start.2 = (bf16[2,4,4096]{2,1,0:T(4,128)(2,1)S(1)}, bf16[2,4,4096]{2,1,0:T(4,128)(2,1)S(1)}, u32[]{:S(2)}, u32[]{:S(2)}) collective-permute-start(bf16[2,4,4096]{2,1,0:T(4,128)(2,1)S(1)} %maximum_select_fusion.refs_0_), channel_id=1, source_target_pairs={{4,0},{6,2},{0,4},{2,6},{12,8},{14,10},{8,12},{10,14},{20,16},{22,... | collective-permute-start | bytes 196616 | tf_op jit(solution)/shard_map/ppermute | solution.py:37
  28.7 5.5 %collective-permute-start.3 = (bf16[2,4,4096]{2,1,0:T(4,128)(2,1)S(1)}, bf16[2,4,4096]{2,1,0:T(4,128)(2,1)S(1)}, u32[]{:S(2)}, u32[]{:S(2)}) collective-permute-start(bf16[2,4,4096]{2,1,0:T(4,128)(2,1)S(1)} %maximum_select_fusion.refs_0_), channel_id=1, source_target_pairs={{6,0},{0,2},{2,4},{4,6},{14,8},{8,10},{10,12},{12,14},{22,16},{16,... | collective-permute-start | bytes 196616 | tf_op jit(solution)/shard_map/ppermute | solution.py:37
  35.4 6.4 %collective-permute-start.18 = (bf16[2,4,4,4096]{3,2,1,0:T(4,128)(2,1)S(1)}, bf16[2,4,4,4096]{3,2,1,0:T(4,128)(2,1)S(1)}, u32[]{:S(2)}, u32[]{:S(2)}) collective-permute-start(bf16[2,4,4,4096]{3,2,1,0:T(4,128)(2,1)S(1)} %shard_map.77.refs_0_), channel_id=1, source_target_pairs={{8,0},{10,2},{12,4},{14,6},{16,8},{18,10},{20,12},{22,14},{24,16},... | collective-permute-start | bytes 786440 | tf_op jit(solution)/shard_map/ppermute | solution.py:41
  36.5 8.0 %collective-permute-start.19 = (bf16[2,4,4,4096]{3,2,1,0:T(4,128)(2,1)S(1)}, bf16[2,4,4,4096]{3,2,1,0:T(4,128)(2,1)S(1)}, u32[]{:S(2)}, u32[]{:S(2)}) collective-permute-start(bf16[2,4,4,4096]{3,2,1,0:T(4,128)(2,1)S(1)} %shard_map.77.refs_0_), channel_id=1, source_target_pairs={{16,0},{18,2},{20,4},{22,6},{24,8},{26,10},{28,12},{30,14},{0,16},... | collective-permute-start | bytes 786440 | tf_op jit(solution)/shard_map/ppermute | solution.py:41
  38.2 9.0 %collective-permute-start.20 = (bf16[2,4,4,4096]{3,2,1,0:T(4,128)(2,1)S(1)}, bf16[2,4,4,4096]{3,2,1,0:T(4,128)(2,1)S(1)}, u32[]{:S(2)}, u32[]{:S(2)}) collective-permute-start(bf16[2,4,4,4096]{3,2,1,0:T(4,128)(2,1)S(1)} %shard_map.77.refs_0_), channel_id=1, source_target_pairs={{24,0},{26,2},{28,4},{30,6},{0,8},{2,10},{4,12},{6,14},{8,16},{10,... | collective-permute-start | bytes 786440 | tf_op jit(solution)/shard_map/ppermute | solution.py:41
  47.8 22.3 %collective-permute-start.21 = (bf16[128,4096]{1,0:T(8,128)(2,1)S(1)}, bf16[128,4096]{1,0:T(8,128)(2,1)S(1)}, u32[]{:S(2)}, u32[]{:S(2)}) collective-permute-start(bf16[128,4096]{1,0:T(8,128)(2,1)S(1)} %shard_map.84.own_ref), channel_id=1, source_target_pairs={{0,64},{64,0},{1,65},{65,1},{2,66},{66,2},{3,67},{67,3},{4,68},{68... | collective-permute-start | bytes 3145736 | tf_op jit(solution)/shard_map/ppermute | solution.py:50
  55.3 36.3 %collective-permute-start.11 = (f32[6,167,256]{2,1,0:T(8,128)S(1)}, f32[6,167,256]{2,1,0:T(8,128)S(1)}, u32[]{:S(2)}, u32[]{:S(2)}) collective-permute-start(f32[6,167,256]{2,1,0:T(8,128)S(1)} %get-tuple-element.18), channel_id=1, source_target_pairs={{0,64},{64,0},{1,65},{65,1},{2,66},{66,2},{3,67},{67,3},{4,68},{68... | collective-permute-start | bytes 3078152 | tf_op jit(solution)/shard_map/ppermute | solution.py:50
  59.0 7.2 %collective-permute-start.14 = (f32[2,167,256]{2,1,0:T(8,128)S(1)}, f32[2,167,256]{2,1,0:T(8,128)S(1)}, u32[]{:S(2)}, u32[]{:S(2)}) collective-permute-start(f32[2,167,256]{2,1,0:T(8,128)S(1)} %get-tuple-element.22), channel_id=1, source_target_pairs={{0,64},{64,0},{1,65},{65,1},{2,66},{66,2},{3,67},{67,3},{4,68},{68... | collective-permute-start | bytes 1026056 | tf_op jit(solution)/shard_map/ppermute | solution.py:50
  62.3 5.5 %collective-permute-start.16 = (f32[2,167,256]{2,1,0:T(8,128)S(1)}, f32[2,167,256]{2,1,0:T(8,128)S(1)}, u32[]{:S(2)}, u32[]{:S(2)}) collective-permute-start(f32[2,167,256]{2,1,0:T(8,128)S(1)} %get-tuple-element.24), channel_id=1, source_target_pairs={{0,64},{64,0},{1,65},{65,1},{2,66},{66,2},{3,67},{67,3},{4,68},{68... | collective-permute-start | bytes 1026056 | tf_op jit(solution)/shard_map/ppermute | solution.py:50
  66.1 2.4 %collective-permute-start.12 = (f32[2,167,256]{2,1,0:T(8,128)S(1)}, f32[2,167,256]{2,1,0:T(8,128)S(1)}, u32[]{:S(2)}, u32[]{:S(2)}) collective-permute-start(f32[2,167,256]{2,1,0:T(8,128)S(1)} %get-tuple-element.20), channel_id=1, source_target_pairs={{0,64},{64,0},{1,65},{65,1},{2,66},{66,2},{3,67},{67,3},{4,68},{68... | collective-permute-start | bytes 1026056 | tf_op jit(solution)/shard_map/ppermute | solution.py:50
  66.3 10.9 %collective-permute-start.15 = (f32[2,167,256]{2,1,0:T(8,128)S(1)}, f32[2,167,256]{2,1,0:T(8,128)S(1)}, u32[]{:S(2)}, u32[]{:S(2)}) collective-permute-start(f32[2,167,256]{2,1,0:T(8,128)S(1)} %add.45), channel_id=1, source_target_pairs={{0,1},{1,0},{2,3},{3,2},{4,5},{5,4},{6,7},{7,6},{8,9},{9,8},{10,11... | collective-permute-start | bytes 1026056 | tf_op jit(solution)/shard_map/ppermute | solution.py:54
  67.9 16.7 %collective-permute-start.17 = (f32[2,167,256]{2,1,0:T(8,128)S(1)}, f32[2,167,256]{2,1,0:T(8,128)S(1)}, u32[]{:S(2)}, u32[]{:S(2)}) collective-permute-start(f32[2,167,256]{2,1,0:T(8,128)S(1)} %add.46), channel_id=1, source_target_pairs={{0,1},{1,0},{2,3},{3,2},{4,5},{5,4},{6,7},{7,6},{8,9},{9,8},{10,11... | collective-permute-start | bytes 1026056 | tf_op jit(solution)/shard_map/ppermute | solution.py:54
  68.5 23.0 %collective-permute-start.13 = (f32[2,167,256]{2,1,0:T(8,128)S(1)}, f32[2,167,256]{2,1,0:T(8,128)S(1)}, u32[]{:S(2)}, u32[]{:S(2)}) collective-permute-start(f32[2,167,256]{2,1,0:T(8,128)S(1)} %add.44), channel_id=1, source_target_pairs={{0,1},{1,0},{2,3},{3,2},{4,5},{5,4},{6,7},{7,6},{8,9},{9,8},{10,11... | collective-permute-start | bytes 1026056 | tf_op jit(solution)/shard_map/ppermute | solution.py:54
  70.1 21.4 %copy-start = (s32[256]{0:T(256)S(1)}, s32[256]{0:T(256)}, u32[]{:S(2)}) copy-start(s32[256]{0:T(256)} %param.10) | copy-start | bytes 3076
  91.5 25.6 %copy-start.1 = (f32[256]{0:T(256)S(1)}, f32[256]{0:T(256)}, u32[]{:S(2)}) copy-start(f32[256]{0:T(256)} %param.11) | copy-start | bytes 3076
  93.0 1.2 collective-permute-start.22
  94.3 4.8 %collective-permute-start.23 = (f32[8,256]{1,0:T(8,128)S(1)}, f32[8,256]{1,0:T(8,128)S(1)}, u32[]{:S(2)}, u32[]{:S(2)}) collective-permute-start(f32[8,256]{1,0:T(8,128)S(1)} %shard_map.87.refs_0_), channel_id=1, source_target_pairs={{1,0},{0,1},{3,2},{2,3},{5,4},{4,5},{7,6},{6,7},{9,8},{8,9},{11,10... | collective-permute-start | bytes 24584 | tf_op jit(solution)/shard_map/ppermute | solution.py:46
  95.9 5.2 %collective-permute-start.24 = (f32[8,256]{1,0:T(8,128)S(1)}, f32[8,256]{1,0:T(8,128)S(1)}, u32[]{:S(2)}, u32[]{:S(2)}) collective-permute-start(f32[8,256]{1,0:T(8,128)S(1)} %shard_map.87.refs_0_), channel_id=1, source_target_pairs={{32,0},{33,1},{34,2},{35,3},{36,4},{37,5},{38,6},{39,7},{40,8},{41... | collective-permute-start | bytes 24584 | tf_op jit(solution)/shard_map/ppermute | solution.py:46
  98.6 4.9 %collective-permute-start.25 = (f32[8,256]{1,0:T(8,128)S(1)}, f32[8,256]{1,0:T(8,128)S(1)}, u32[]{:S(2)}, u32[]{:S(2)}) collective-permute-start(f32[8,256]{1,0:T(8,128)S(1)} %shard_map.87.refs_0_), channel_id=1, source_target_pairs={{33,0},{32,1},{35,2},{34,3},{37,4},{36,5},{39,6},{38,7},{41,8},{40... | collective-permute-start | bytes 24584 | tf_op jit(solution)/shard_map/ppermute | solution.py:46
  103.5 3.7 %collective-permute-start.26 = (f32[8,256]{1,0:T(8,128)S(1)}, f32[8,256]{1,0:T(8,128)S(1)}, u32[]{:S(2)}, u32[]{:S(2)}) collective-permute-start(f32[8,256]{1,0:T(8,128)S(1)} %shard_map.88.refs_0_), channel_id=1, source_target_pairs={{8,0},{10,2},{12,4},{14,6},{16,8},{18,10},{20,12},{22,14},{24,16},... | collective-permute-start | bytes 24584 | tf_op jit(solution)/shard_map/ppermute | solution.py:41
  104.2 5.2 %collective-permute-start.27 = (f32[8,256]{1,0:T(8,128)S(1)}, f32[8,256]{1,0:T(8,128)S(1)}, u32[]{:S(2)}, u32[]{:S(2)}) collective-permute-start(f32[8,256]{1,0:T(8,128)S(1)} %shard_map.88.refs_0_), channel_id=1, source_target_pairs={{16,0},{18,2},{20,4},{22,6},{24,8},{26,10},{28,12},{30,14},{0,16},... | collective-permute-start | bytes 24584 | tf_op jit(solution)/shard_map/ppermute | solution.py:41
  105.9 4.9 %collective-permute-start.28 = (f32[8,256]{1,0:T(8,128)S(1)}, f32[8,256]{1,0:T(8,128)S(1)}, u32[]{:S(2)}, u32[]{:S(2)}) collective-permute-start(f32[8,256]{1,0:T(8,128)S(1)} %shard_map.88.refs_0_), channel_id=1, source_target_pairs={{24,0},{26,2},{28,4},{30,6},{0,8},{2,10},{4,12},{6,14},{8,16},{10,... | collective-permute-start | bytes 24584 | tf_op jit(solution)/shard_map/ppermute | solution.py:41
  110.8 3.7 %collective-permute-start.29 = (f32[8,256]{1,0:T(8,128)S(1)}, f32[8,256]{1,0:T(8,128)S(1)}, u32[]{:S(2)}, u32[]{:S(2)}) collective-permute-start(f32[8,256]{1,0:T(8,128)S(1)} %shard_map.89.refs_0_), channel_id=1, source_target_pairs={{2,0},{4,2},{6,4},{0,6},{10,8},{12,10},{14,12},{8,14},{18,16},{20,... | collective-permute-start | bytes 24584 | tf_op jit(solution)/shard_map/ppermute | solution.py:37
  111.7 5.2 %collective-permute-start.30 = (f32[8,256]{1,0:T(8,128)S(1)}, f32[8,256]{1,0:T(8,128)S(1)}, u32[]{:S(2)}, u32[]{:S(2)}) collective-permute-start(f32[8,256]{1,0:T(8,128)S(1)} %shard_map.89.refs_0_), channel_id=1, source_target_pairs={{4,0},{6,2},{0,4},{2,6},{12,8},{14,10},{8,12},{10,14},{20,16},{22,... | collective-permute-start | bytes 24584 | tf_op jit(solution)/shard_map/ppermute | solution.py:37
  111.7 5.5 %collective-permute-start.31 = (f32[8,256]{1,0:T(8,128)S(1)}, f32[8,256]{1,0:T(8,128)S(1)}, u32[]{:S(2)}, u32[]{:S(2)}) collective-permute-start(f32[8,256]{1,0:T(8,128)S(1)} %shard_map.89.refs_0_), channel_id=1, source_target_pairs={{6,0},{0,2},{2,4},{4,6},{14,8},{8,10},{10,12},{12,14},{22,16},{16,... | collective-permute-start | bytes 24584 | tf_op jit(solution)/shard_map/ppermute | solution.py:37
  124.0 2.7 %collective-permute-start.32 = (bf16[128,4096]{1,0:T(8,128)(2,1)S(1)}, bf16[128,4096]{1,0:T(8,128)(2,1)S(1)}, u32[]{:S(2)}, u32[]{:S(2)}) collective-permute-start(bf16[128,4096]{1,0:T(8,128)(2,1)S(1)} %get-tuple-element.29), channel_id=1, source_target_pairs={{0,64},{64,0},{1,65},{65,1},{2,66},{66,2},{3,67},{67,3},{4,68},{68... | collective-permute-start | bytes 3145736 | tf_op jit(solution)/shard_map/ppermute | solution.py:50
  128.5 23.2 %all-to-all-start = ((bf16[64,2,4096]{2,1,0:T(2,128)(2,1)}), bf16[64,2,4096]{2,1,0:T(2,128)(2,1)S(1)}, u32[]{:S(2)}, u32[]{:S(2)}) async-start(bf16[64,2,4096]{2,1,0:T(2,128)(2,1)} %reshape.24), calls=%async_computation | async-start | bytes 2097152 | tf_op jit(solution)/shard_map/all_to_all | solution.py:320

commit v2 on v1

v2 whole, which is shorter than its diff:
```python
import functools

import jax
import jax.numpy as jnp
from jax import lax
from jax.experimental import pallas as pl
from jax.experimental.pallas import tpu as pltpu
from jax.sharding import PartitionSpec as P

F32 = jnp.float32
BF16 = jnp.bfloat16
BLOCKS = 6
TINY = pl.CostEstimate(flops=1000, bytes_accessed=1000, transcendentals=0)
VMEM = pl.BlockSpec(memory_space=pltpu.VMEM)
SMEM = pl.BlockSpec(memory_space=pltpu.SMEM)


def params(mib=20):
    return pltpu.CompilerParams(vmem_limit_bytes=mib * 1024 * 1024)


def call(kernel, out_shape, *args, in_specs=None, scratch=(), mib=20):
    return pl.pallas_call(
        kernel,
        out_shape=out_shape,
        in_specs=in_specs or [VMEM] * len(args),
        out_specs=jax.tree.map(lambda _: VMEM, out_shape),
        scratch_shapes=scratch,
        compiler_params=params(mib),
        cost_estimate=TINY,
    )(*args)


def swap_xhi(a):
    return lax.ppermute(a, "vocab", [(i, i ^ 16) for i in range(32)])


def swap_core(a):
    return lax.ppermute(a, "grp", [(0, 1), (1, 0)])


def swap_seq(a):
    return lax.ppermute(a, "seq", [(0, 1), (1, 0)])


def place(a):
    n, two, m, w = a.shape

    def kernel(in_ref, out_ref):
        for h in range(two):
            out_ref[h * n * m : (h + 1) * n * m, :] = in_ref[:, h].reshape(n * m, w)

    return call(kernel, jax.ShapeDtypeStruct((two * n * m, w), BF16), a)


def teacher_part(head, rows, ids, mine, first, count):
    width, _, depth = head.shape
    step = width // (2 * BLOCKS)
    tokens = rows.shape[0]
    padded = -(-step // 8) * 8

    def kernel(ids_ref, w_hbm, x_ref, own_ref, other_ref, w_buf, acc, sems):
        g = ids_ref[0]
        part = ids_ref[1] if mine else 1 - ids_ref[1]
        copies = []
        for i in range(count):
            start = (part * BLOCKS + first + i) * step
            copies.append(
                pltpu.make_async_copy(w_hbm.at[pl.ds(start, step)], w_buf.at[i], sems.at[i])
            )
        for c in copies:
            c.start()
        for i in range(count):
            copies[i].wait()
            w = w_buf[i].reshape(2 * step, depth)
            out = lax.dot_general(
                w, x_ref[...], (((1,), (1,)), ((), ())), preferred_element_type=F32
            )
            for lane in range(tokens // 128):
                cols = slice(lane * 128, lane * 128 + 128)
                acc[lane, 0 : 2 * step, :] = out[:, cols]
                rows = slice(i * padded, i * padded + step)
                own_ref[rows, cols] = acc[lane, pl.ds(g, step, stride=2), :]
                other_ref[rows, cols] = acc[lane, pl.ds(1 - g, step, stride=2), :]

    out = jax.ShapeDtypeStruct((count * padded, tokens), F32)
    return call(
        kernel,
        [out, out],
        ids,
        head,
        rows,
        in_specs=[SMEM, pl.BlockSpec(memory_space=pl.ANY), VMEM],
        scratch=[
            pltpu.VMEM((count, step, 2, depth), BF16),
            pltpu.VMEM((tokens // 128, 2 * step + 18, 128), F32),
            pltpu.SemaphoreType.DMA((count,)),
        ],
        mib=50,
    )


def student_product(head, own, other, ids):
    width, depth = head.shape
    half = own.shape[0]
    block = 256

    def kernel(ids_ref, w_ref, own_ref, other_ref, out_ref, xs):
        g = ids_ref[0]
        xs[pl.ds(pl.multiple_of(g * half, half), half), :] = own_ref[...]
        xs[pl.ds(pl.multiple_of((1 - g) * half, half), half), :] = other_ref[...]
        for start in range(0, width, block):
            rows = slice(start, min(start + block, width))
            out_ref[rows, :] = lax.dot_general(
                w_ref[rows, :], xs[...], (((1,), (1,)), ((), ())), preferred_element_type=F32
            )

    return call(
        kernel,
        jax.ShapeDtypeStruct((width, 2 * half), F32),
        ids,
        head,
        own,
        other,
        in_specs=[SMEM, VMEM, VMEM, VMEM],
        scratch=[pltpu.VMEM((2 * half, depth), BF16)],
    )


def hits(ids_ref, targets_ref, shape):
    columns = ids_ref[4] + lax.broadcasted_iota(jnp.int32, shape, 0)
    return columns == targets_ref[...]


def local_stats(mine, core, near, student, targets, ids):
    width, tokens = student.shape
    step = width // BLOCKS
    padded = -(-step // 8) * 8

    def kernel(ids_ref, mine_ref, core_ref, *refs):
        near_refs = refs[: len(near)]
        s_ref, t_ref, tl_ref, out_ref = refs[len(near) :]
        b = 0
        for ref in near_refs:
            for i in range(ref.shape[0] // padded):
                here = slice(b * padded, b * padded + step)
                there = slice(i * padded, i * padded + step)
                own = mine_ref[here, :] + core_ref[here, :]
                tl_ref[b * step : (b + 1) * step, :] = own + ref[there, :]
                b += 1
        t, s = tl_ref[...], s_ref[...]
        t_top = jnp.max(t, axis=0, keepdims=True)
        s_top = jnp.max(s, axis=0, keepdims=True)
        e = jnp.exp(t - t_top)
        out_ref[0:1, :] = t_top
        out_ref[1:2, :] = jnp.sum(e, axis=0, keepdims=True)
        out_ref[2:3, :] = jnp.sum(e * (t - s), axis=0, keepdims=True)
        out_ref[3:4, :] = s_top
        out_ref[4:5, :] = jnp.sum(jnp.exp(s - s_top), axis=0, keepdims=True)
        hit = hits(ids_ref, t_ref, s.shape)
        out_ref[5:6, :] = jnp.sum(jnp.where(hit, s, jnp.zeros_like(s)), axis=0, keepdims=True)
        out_ref[6:8, :] = jnp.zeros((2, tokens), F32)

    return call(
        kernel,
        [jax.ShapeDtypeStruct((width, tokens), F32), jax.ShapeDtypeStruct((8, tokens), F32)],
        ids,
        mine,
        core,
        *near,
        student,
        targets,
        in_specs=[SMEM] + [VMEM] * (4 + len(near)),
    )


def merge(stats):
    def kernel(*refs):
        out_ref = refs[-1]
        values = [r[...] for r in refs[:-1]]

        def row(v, i):
            return v[i : i + 1, :]

        for top_row, sums in ((0, (1, 2)), (3, (4,))):
            top = functools.reduce(jnp.maximum, [row(v, top_row) for v in values])
            scale = [jnp.exp(row(v, top_row) - top) for v in values]
            out_ref[top_row : top_row + 1, :] = top
            for i in sums:
                out_ref[i : i + 1, :] = sum(c * row(v, i) for c, v in zip(scale, values))
        out_ref[5:6, :] = sum(row(v, 5) for v in values)
        out_ref[6:8, :] = values[0][6:8, :]

    return call(kernel, jax.ShapeDtypeStruct(stats[0].shape, F32), *stats)


def merge_all(stats):
    def kernel(in_ref, out_ref):
        for top_row, sums in ((0, (1, 2)), (3, (4,))):
            tops = in_ref[:, top_row, :]
            top = jnp.max(tops, axis=0, keepdims=True)
            scale = jnp.exp(tops - top)
            out_ref[top_row : top_row + 1, :] = top
            for i in sums:
                out_ref[i : i + 1, :] = jnp.sum(scale * in_ref[:, i, :], axis=0, keepdims=True)
        out_ref[5:6, :] = jnp.sum(in_ref[:, 5, :], axis=0, keepdims=True)
        out_ref[6:8, :] = jnp.zeros((2, in_ref.shape[2]), F32)

    return call(kernel, jax.ShapeDtypeStruct(stats.shape[1:], F32), stats)


def hidden_part(head, teacher, student, stats, targets, loss_grad, ids):
    width, depth = head.shape
    tokens = teacher.shape[1]
    half = tokens // 2
    block = 1024

    def kernel(ids_ref, w_ref, tl_ref, sl_ref, st_ref, t_ref, g_ref, own_ref, other_ref, grad):
        st = st_ref[...]
        t_probs = jnp.exp(tl_ref[...] - st[0:1, :]) / st[1:2, :]
        s_probs = jnp.exp(sl_ref[...] - st[3:4, :]) / st[4:5, :]
        hit = hits(ids_ref, t_ref, t_probs.shape)
        value = g_ref[...] * (2.0 * s_probs - t_probs - hit.astype(F32))
        first = ids_ref[0] == 0
        low, high = value[:, :half].T, value[:, half:].T
        grad[0:half, :] = jnp.where(first, low, high).astype(BF16)
        grad[half:tokens, :] = jnp.where(first, high, low).astype(BF16)
        for start in range(0, depth, block):
            cols = slice(start, start + block)
            out = jnp.dot(grad[...], w_ref[:, cols], preferred_element_type=F32)
            own_ref[:, cols] = out[:half]
            other_ref[:, cols] = out[half:].astype(BF16)

    return call(
        kernel,
        [jax.ShapeDtypeStruct((half, depth), F32), jax.ShapeDtypeStruct((half, depth), BF16)],
        ids,
        head,
        teacher,
        student,
        stats,
        targets,
        loss_grad,
        in_specs=[SMEM] + [VMEM] * 6,
        scratch=[pltpu.VMEM((tokens, width), BF16)],
    )


def body(teacher_rows, student_rows, teacher_head, student_head, targets, loss_grad):
    t_head = jnp.transpose(teacher_head, (2, 1, 0))
    s_head = jnp.transpose(student_head, (1, 0))
    width = s_head.shape[0]
    grp, vocab, seq = lax.axis_index("grp"), lax.axis_index("vocab"), lax.axis_index("seq")
    shard = (grp * lax.axis_size("vocab") + vocab) * lax.axis_size("seq") + seq
    ids = jnp.stack([grp, seq, (vocab // 4) % 4, vocab % 4, shard * width]).astype(jnp.int32)
    lower = vocab < 16
    targets2, loss_grad2 = targets.reshape(1, -1), loss_grad.reshape(1, -1)

    def pair(a):
        b = swap_xhi(a)
        return jnp.where(lower, jnp.stack([a, b]), jnp.stack([b, a]))

    after = lax.optimization_barrier
    a = jnp.broadcast_to(teacher_rows[None], (32,) + teacher_rows.shape)
    a = lax.all_to_all(a, "vocab", 0, 0, tiled=True).reshape(-1, teacher_rows.shape[1])
    planes = [[x * 16 + i for i in range(16)] for x in range(2)]
    b = pair(student_rows)
    b = jnp.broadcast_to(b[None], (16,) + b.shape)
    a, b = after((a, b))
    b = lax.all_to_all(b, "vocab", 0, 0, axis_index_groups=planes, tiled=True)

    def send(first, count):
        own, other = teacher_part(t_head, a, ids, False, first, count)
        return own, swap_core(other)

    own0, got0 = send(0, 4)
    a, own0 = after((a, own0))
    own1, other1 = teacher_part(t_head, a, ids, False, 4, 2)
    a, own1, other1, sum0 = after((a, own1, other1, own0 + got0))
    near0 = swap_seq(sum0)
    sum1 = own1 + swap_core(other1)
    mine, other = teacher_part(t_head, a, ids, True, 0, BLOCKS)
    mine, other, b, sum1, near0 = after((mine, other, b, sum1, near0))
    near1 = swap_seq(sum1)
    core = swap_core(other)
    b = place(b)
    student = student_product(s_head, b, swap_core(b), ids)
    near = [near0, near1]
    teacher, stats = local_stats(mine, core, near, student, targets2, ids)
    stats = merge([stats, swap_core(stats)])
    stats = jnp.broadcast_to(stats[None], (64,) + stats.shape)
    stats = merge_all(lax.all_to_all(stats, ("vocab", "seq"), 0, 0, tiled=True))

    own, other = hidden_part(s_head, teacher, student, stats, targets2, loss_grad2, ids)
    part = (own + swap_core(other).astype(F32)).astype(BF16)
    part = part.reshape(64, 2, -1)
    part = lax.all_to_all(part, ("vocab", "seq"), 0, 0, tiled=True)
    hidden = jnp.sum(part.astype(F32), axis=0).astype(BF16)

    t_norm = stats[0] + jnp.log(stats[1])
    s_norm = stats[3] + jnp.log(stats[4])
    token_loss = stats[2] / stats[1] - t_norm + 2.0 * s_norm - stats[5]
    return hidden, token_loss


def solution(mesh):
    return jax.shard_map(
        body,
        mesh=mesh,
        in_specs=(
            P("vocab", ("grp", "seq")),
            P(("grp", "vocab"), None),
            P(("grp", "seq"), None, "vocab"),
            P(None, ("grp", "vocab", "seq")),
            P(),
            P(),
        ),
        out_specs=(P(("grp", "vocab", "seq"), None), P()),
        check_vma=False,
    )
```

time: 154 us -> 140 us (0.909)
  waiting for transfers between devices: 69.1 us -> 47.9 us
  blocking collectives: 0 us -> 21.1 us
  starting transfers between devices: 43.3 us -> 25.9 us
  local copies, waits for them, and re-layouts: 1.6 us -> 12.6 us
  Pallas kernels: 34.2 us -> 26.7 us
    pallas_call x6 -> x0, Pallas kernels: 30.2 us -> none  [the longest x4 16.9 us: teacher_part(): pl.pallas_call(kernel, grid_spec=pltpu.PrefetchScalarGridSpec(num_scalar_...]
    ppermute x21 -> x0, waiting for transfers between devices: 30.2 us -> none  [the longest x9 12.9 us: from_z(): lax.ppermute(a, 'vocab', [(i & ~3 | i + k & 3, i) for i in range(32)])]
    ppermute x21 -> x0, starting transfers between devices: 26.8 us -> none  [the longest x9 11.5 us: from_y(): lax.ppermute(a, 'vocab', [(i & ~12 | i + 4 * k & 12, i) for i in range(32)])]
    pallas_call x9, Pallas kernels: 3.96 us -> 26.7 us  [call(): pl.pallas_call(kernel, out_shape=out_shape, in_specs=in_specs or [VMEM] *...]
    all_to_all x0 -> x1, blocking collectives: none -> 21.1 us  [body(): stats = merge_all(lax.all_to_all(stats, ('vocab', 'seq'), 0, 0, tiled=True))]
    all_to_all x0 -> x2, starting transfers between devices: none -> 15.2 us  [the longest x1 10.9 us: body(): lax.all_to_all(a, 'vocab', 0, 0, tiled=True)]
    ppermute x2 -> x1, waiting for transfers between devices: 2.52 us -> 12 us  [swap_xhi(): return lax.ppermute(a, 'vocab', [(i, i ^ 16) for i in range(32)])]
    ppermute x3 -> x2, waiting for transfers between devices: 14.9 us -> 6.74 us  [swap_seq(): return lax.ppermute(a, 'seq', [(0, 1), (1, 0)])]
  transfers between devices with their start and end apart: 34 -> 12, of which waited for: 23 -> 9; matrix products, arithmetic and copies ran while one was open for 1% -> 2% of each run, Pallas kernels for 16% -> 10%
where the time goes in v2:
time: 140 us; the launch traced here: 139 us
  waiting for transfers between devices  47.9 us (34%)
  Pallas kernels  26.7 us (19%)
  starting transfers between devices  25.9 us (18%)
  blocking collectives  21.1 us (15%)
  local copies, waits for them, and re-layouts  12.6 us (9%)
  other arithmetic  4.48 us (3%)
    pallas_call x9, Pallas kernels, call(): pl.pallas_call(kernel, out_shape=out_shape, in_specs=in_specs or [VMEM] *...  26.7 us
    all_to_all x1, blocking collectives, body(): stats = merge_all(lax.all_to_all(stats, ('vocab', 'seq'), 0, 0, tiled=True))  21.1 us
    all_to_all x1, waiting for transfers between devices, body(): part = lax.all_to_all(part, ('vocab', 'seq'), 0, 0, tiled=True)  17.7 us
    ppermute x1, waiting for transfers between devices, swap_xhi(): return lax.ppermute(a, 'vocab', [(i, i ^ 16) for i in range(32)])  12 us
    all_to_all x1, starting transfers between devices, body(): lax.all_to_all(a, 'vocab', 0, 0, tiled=True)  10.9 us
    unnamed x14, local copies, waits for them, and re-layouts  7.65 us
    ppermute x2, waiting for transfers between devices, swap_seq(): return lax.ppermute(a, 'seq', [(0, 1), (1, 0)])  6.74 us
    ppermute x6, waiting for transfers between devices, swap_core(): return lax.ppermute(a, 'grp', [(0, 1), (1, 0)])  5.37 us
  transfers between devices with their start and end apart: 12, of which 9 were waited for; matrix products, arithmetic and copies ran while one was open for 2% of the time, Pallas kernels for 10%

profile of v2, /device:TPU:0, one launch (start us, length us, event | category | flops | bytes accessed | tf_op | source)
XLA Modules:
  0.0 139.4 jit_solution(52557988583491853)
XLA Ops:
  0.6 1.9 %broadcast_in_dim.6 = bf16[32,8,2048]{2,1,0:T(8,128)(2,1)} broadcast(bf16[8,2048]{1,0:T(8,128)(2,1)} %param.6), dimensions={1,2} | broadcast | bytes 1081344 | tf_op jit(solution)/shard_map/broadcast_in_dim | solution.py:264
  2.5 10.9 %all-to-all-start = ((bf16[32,8,2048]{2,1,0:T(8,128)(2,1)}), bf16[32,8,2048]{2,1,0:T(8,128)(2,1)S(1)}, u32[]{:S(2)}, u32[]{:S(2)}) async-start(bf16[32,8,2048]{2,1,0:T(8,128)(2,1)} %broadcast_in_dim.6), calls=%async_computation | async-start | bytes 2097152 | tf_op jit(solution)/shard_map/all_to_all | solution.py:265
  13.4 3.4 %collective-permute-start = (bf16[4,4096]{1,0:T(4,128)(2,1)S(1)}, bf16[4,4096]{1,0:T(4,128)(2,1)S(1)}, u32[]{:S(2)}, u32[]{:S(2)}) collective-permute-start(bf16[4,4096]{1,0:T(4,128)(2,1)S(1)} %copy-done.6), channel_id=1, source_target_pairs={{0,32},{2,34},{4,36},{6,38},{8,40},{10,42},{12,44},{14,46},{16,48}... | collective-permute-start | bytes 98312 | tf_op jit(solution)/shard_map/ppermute | solution.py:35
  16.8 0.1 stack.37.ids_ref
  16.9 12.0 %collective-permute-done = bf16[4,4096]{1,0:T(4,128)(2,1)S(1)} collective-permute-done((bf16[4,4096]{1,0:T(4,128)(2,1)S(1)}, bf16[4,4096]{1,0:T(4,128)(2,1)S(1)}, u32[]{:S(2)}, u32[]{:S(2)}) %collective-permute-start) | collective-permute-done | bytes 32800 | tf_op jit(solution)/shard_map/ppermute | solution.py:35
  28.9 0.1 maximum_select_fusion
  28.9 2.6 %all-to-all-done = bf16[32,8,2048]{2,1,0:T(8,128)(2,1)S(1)} async-done(((bf16[32,8,2048]{2,1,0:T(8,128)(2,1)}), bf16[32,8,2048]{2,1,0:T(8,128)(2,1)S(1)}, u32[]{:S(2)}, u32[]{:S(2)}) %all-to-all-start) | async-done | bytes 1048608 | tf_op jit(solution)/shard_map/all_to_all | solution.py:265
  31.5 1.5 %broadcast_in_dim.7 = bf16[16,2,4,4096]{3,2,1,0:T(4,128)(2,1)} broadcast(bf16[2,4,4096]{2,1,0:T(4,128)(2,1)S(1)} %maximum_select_fusion), dimensions={1,2,3} | broadcast | bytes 1114112 | tf_op jit(solution)/shard_map/broadcast_in_dim | solution.py:268
  33.0 6.5 %shard_map.77 = (f32[672,256]{1,0:T(8,128)S(1)}, f32[672,256]{1,0:T(8,128)}) custom-call(s32[5]{0:T(128)S(1)} %stack.37.ids_ref, bf16[2004,2,2048]{2,1,0:T(2,128)(2,1)} %bitcast.21, bf16[256,2048]{1,0:T(8,128)(2,1)S(1)} %bitcast.15), custom_call_target="tpu_custom_call" | custom-call | flops 1000 | bytes 1000 | tf_op jit(solution)/shard_map/pallas_call | solution.py:23
  39.5 0.1 collective-permute-start.1
  39.6 4.3 %all-to-all-start.1 = ((bf16[16,2,4,4096]{3,2,1,0:T(4,128)(2,1)}), bf16[16,2,4,4096]{3,2,1,0:T(4,128)(2,1)S(1)}, u32[]{:S(2)}, u32[]{:S(2)}) async-start(bf16[16,2,4,4096]{3,2,1,0:T(4,128)(2,1)} %broadcast_in_dim.7), calls=%async_computation.1 | async-start | bytes 2097152 | tf_op jit(solution)/shard_map/all_to_all | solution.py:270
  43.9 3.8 %shard_map.78 = (f32[336,256]{1,0:T(8,128)S(1)}, f32[336,256]{1,0:T(8,128)S(1)}) custom-call(s32[5]{0:T(128)S(1)} %stack.37.ids_ref, bf16[2004,2,2048]{2,1,0:T(2,128)(2,1)} %bitcast.22, bf16[256,2048]{1,0:T(8,128)(2,1)S(1)} %bitcast.16), custom_call_target="tpu_custom_call" | custom-call | flops 1000 | bytes 1000 | tf_op jit(solution)/shard_map/pallas_call | solution.py:23
  47.6 0.0 collective-permute-done.1
  47.6 2.0 %add.41 = f32[672,256]{1,0:T(8,128)} add(f32[672,256]{1,0:T(8,128)S(1)} %get-tuple-element.30, f32[672,256]{1,0:T(8,128)} %collective-permute-done.1) | non-fusion elementwise | flops 172032 | bytes 2064384 | tf_op jit(solution)/shard_map/add | solution.py:279
  49.7 0.6 collective-permute-start.3
  50.3 0.0 collective-permute-start.2
  50.3 7.5 %shard_map.79 = (f32[1008,256]{1,0:T(8,128)S(1)}, f32[1008,256]{1,0:T(8,128)S(1)}) custom-call(s32[5]{0:T(128)S(1)} %stack.37.ids_ref, bf16[2004,2,2048]{2,1,0:T(2,128)(2,1)} %bitcast.23, bf16[256,2048]{1,0:T(8,128)(2,1)S(1)} %bitcast.17), custom_call_target="tpu_custom_call" | custom-call | flops 1000 | bytes 1000 | tf_op jit(solution)/shard_map/pallas_call | solution.py:23
  57.8 0.0 copy-start.4
  57.8 1.0 copy-done.4
  58.7 0.0 collective-permute-done.2
  58.8 3.5 %all-to-all-done.1.in_ref = bf16[16,2,4,4096]{3,2,1,0:T(4,128)(2,1)S(1)} async-done(((bf16[16,2,4,4096]{3,2,1,0:T(4,128)(2,1)}), bf16[16,2,4,4096]{3,2,1,0:T(4,128)(2,1)S(1)}, u32[]{:S(2)}, u32[]{:S(2)}) %all-to-all-start.1) | async-done | bytes 1048608 | tf_op jit(solution)/shard_map/all_to_all | solution.py:270
  62.3 5.2 %collective-permute-done.3.refs_0_ = f32[672,256]{1,0:T(8,128)} collective-permute-done((f32[672,256]{1,0:T(8,128)}, f32[672,256]{1,0:T(8,128)}, u32[]{:S(2)}, u32[]{:S(2)}) %collective-permute-start.3) | collective-permute-done | bytes 688160 | tf_op jit(solution)/shard_map/ppermute | solution.py:43
  67.5 0.1 shard_map.80.own_ref
  67.6 0.1 collective-permute-start.6
  67.7 0.5 collective-permute-start.4
  68.2 0.6 collective-permute-start.5
  68.8 1.6 %collective-permute-done.6.other_ref = bf16[128,4096]{1,0:T(8,128)(2,1)S(1)} collective-permute-done((bf16[128,4096]{1,0:T(8,128)(2,1)S(1)}, bf16[128,4096]{1,0:T(8,128)(2,1)S(1)}, u32[]{:S(2)}, u32[]{:S(2)}) %collective-permute-start.6) | collective-permute-done | bytes 1048608 | tf_op jit(solution)/shard_map/ppermute | solution.py:39
  70.4 3.3 %copy-done = bf16[4096,1002]{0,1:T(8,128)(2,1)S(1)} copy-done((bf16[4096,1002]{0,1:T(8,128)(2,1)S(1)}, bf16[4096,1002]{0,1:T(8,128)(2,1)}, u32[]{:S(2)}) %copy-start) | copy-done | bytes 8208408
  73.7 3.1 %shard_map.81.refs_2_.sl_ref = f32[1002,256]{1,0:T(8,128)S(1)} custom-call(s32[5]{0:T(128)S(1)} %stack.37.ids_ref, bf16[1002,4096]{1,0:T(8,128)(2,1)S(1)} %bitcast.13, bf16[128,4096]{1,0:T(8,128)(2,1)S(1)} %shard_map.80.own_ref, bf16[128,4096]{1,0:T(8,128)(2,1)S(1)} %collective-permute-done.6.other_ref), custom_call_target="tpu_custom_call" | custom-call | flops 1000 | bytes 1000 | tf_op jit(solution)/shard_map/pallas_call | solution.py:23
  76.8 1.5 %collective-permute-done.5.refs_1_ = f32[336,256]{1,0:T(8,128)S(1)} collective-permute-done((f32[336,256]{1,0:T(8,128)S(1)}, f32[336,256]{1,0:T(8,128)S(1)}, u32[]{:S(2)}, u32[]{:S(2)}) %collective-permute-start.5) | collective-permute-done | bytes 344096 | tf_op jit(solution)/shard_map/ppermute | solution.py:43
  78.3 0.0 collective-permute-done.4.core_ref
  78.3 0.0 copy-done.2
  78.3 2.1 %shard_map.82 = (f32[1002,256]{1,0:T(8,128)S(1)}, f32[8,256]{1,0:T(8,128)S(1)}) custom-call(s32[5]{0:T(128)S(1)} %stack.37.ids_ref, f32[1008,256]{1,0:T(8,128)S(1)} %get-tuple-element.39.mine_ref, f32[1008,256]{1,0:T(8,128)S(1)} %collective-permute-done.4.core_ref, f32[672,256]{1,0:T(8,128)} %collective-permute-done.3.refs_0_, ...), custom_call_target="tpu_custom_call" | custom-call | flops 1000 | bytes 1000 | tf_op jit(solution)/shard_map/pallas_call | solution.py:23
  80.4 0.1 collective-permute-start.7
  80.5 1.2 collective-permute-done.7.refs_1_
  81.7 21.1 %all_to_all.20.in_ref = f32[64,8,256]{2,1,0:T(8,128)S(1)} all-to-all(f32[64,8,256]{2,1,0:T(8,128)S(1)} %broadcast_in_dim.8), channel_id=1, replica_groups=mesh['grp'=2,'vocab'=32,'seq'=2] {'vocab','seq'}, dimensions={0} | all-to-all | bytes 1048576 | tf_op jit(solution)/shard_map/all_to_all | solution.py:292
  102.8 0.2 shard_map.84.st_ref
  103.0 0.0 copy-start.1
  103.1 3.3 %copy-done.1 = bf16[4096,1002]{0,1:T(8,128)(2,1)S(1)} copy-done((bf16[4096,1002]{0,1:T(8,128)(2,1)S(1)}, bf16[4096,1002]{0,1:T(8,128)(2,1)}, u32[]{:S(2)}) %copy-start.1) | copy-done | bytes 8208408
  106.4 3.4 %shard_map.85 = (f32[128,4096]{1,0:T(8,128)S(1)}, bf16[128,4096]{1,0:T(8,128)(2,1)S(1)}) custom-call(s32[5]{0:T(128)S(1)} %stack.37.ids_ref, bf16[1002,4096]{1,0:T(8,128)(2,1)S(1)} %bitcast.14, f32[1002,256]{1,0:T(8,128)S(1)} %get-tuple-element.44.tl_ref, f32[1002,256]{1,0:T(8,128)S(1)} %shard_map.81.refs_2_.sl_ref, f32[8,256]{1,0:T(8,128)S(1)} %shard_map.84.st_ref, ...), custom_call_target="tpu_custom_call" | custom-call | flops 1000 | bytes 1000 | tf_op jit(solution)/shard_map/pallas_call | solution.py:23
  109.8 0.1 collective-permute-start.8
  109.9 2.6 %collective-permute-done.8 = bf16[128,4096]{1,0:T(8,128)(2,1)S(1)} collective-permute-done((bf16[128,4096]{1,0:T(8,128)(2,1)S(1)}, bf16[128,4096]{1,0:T(8,128)(2,1)S(1)}, u32[]{:S(2)}, u32[]{:S(2)}) %collective-permute-start.8) | collective-permute-done | bytes 1048608 | tf_op jit(solution)/shard_map/ppermute | solution.py:39
  112.6 0.2 add_convert_fusion
  112.8 1.5 %reshape.63 = bf16[64,2,4096]{2,1,0:T(2,128)(2,1)} reshape(bf16[128,4096]{1,0:T(8,128)(2,1)S(1)} %add_convert_fusion) | data formatting | bytes 2097152 | tf_op jit(solution)/shard_map/reshape | solution.py:296
  114.4 5.3 %all-to-all-start.3 = ((bf16[64,2,4096]{2,1,0:T(2,128)(2,1)}), bf16[64,2,4096]{2,1,0:T(2,128)(2,1)S(1)}, u32[]{:S(2)}, u32[]{:S(2)}) async-start(bf16[64,2,4096]{2,1,0:T(2,128)(2,1)} %reshape.63), calls=%async_computation.3 | async-start | bytes 2097152 | tf_op jit(solution)/shard_map/all_to_all | solution.py:297
  119.6 0.6 slice_subtract_fusion
  120.2 17.7 %all-to-all-done.3 = bf16[64,2,4096]{2,1,0:T(2,128)(2,1)S(1)} async-done(((bf16[64,2,4096]{2,1,0:T(2,128)(2,1)}), bf16[64,2,4096]{2,1,0:T(2,128)(2,1)S(1)}, u32[]{:S(2)}, u32[]{:S(2)}) %all-to-all-start.3) | async-done | bytes 1048608 | tf_op jit(solution)/shard_map/all_to_all | solution.py:297
  137.9 1.5 %reduce_sum.12 = bf16[2,4096]{1,0:T(2,128)(2,1)} reduce(bf16[64,2,4096]{2,1,0:T(2,128)(2,1)S(1)} %all-to-all-done.3, bf16[]{:T(256)} %constant.52.clone.1), dimensions={0}, to_apply=%region_0.1 | reduce | flops 516096 | bytes 1064962 | tf_op jit(solution)/shard_map/reduce_sum | solution.py:298
  (11 shorter events, 0.1 us)
Async XLA Ops:
  0.6 12.8 %copy-start.6 = (bf16[4,4096]{1,0:T(4,128)(2,1)S(1)}, bf16[4,4096]{1,0:T(4,128)(2,1)}, u32[]{:S(2)}) copy-start(bf16[4,4096]{1,0:T(4,128)(2,1)} %param.7) | copy-start | bytes 98308
  2.5 29.0 %all-to-all-start = ((bf16[32,8,2048]{2,1,0:T(8,128)(2,1)}), bf16[32,8,2048]{2,1,0:T(8,128)(2,1)S(1)}, u32[]{:S(2)}, u32[]{:S(2)}) async-start(bf16[32,8,2048]{2,1,0:T(8,128)(2,1)} %broadcast_in_dim.6), calls=%async_computation | async-start | bytes 2097152 | tf_op jit(solution)/shard_map/all_to_all | solution.py:265
  13.4 15.4 %collective-permute-start = (bf16[4,4096]{1,0:T(4,128)(2,1)S(1)}, bf16[4,4096]{1,0:T(4,128)(2,1)S(1)}, u32[]{:S(2)}, u32[]{:S(2)}) collective-permute-start(bf16[4,4096]{1,0:T(4,128)(2,1)S(1)} %copy-done.6), channel_id=1, source_target_pairs={{0,32},{2,34},{4,36},{6,38},{8,40},{10,42},{12,44},{14,46},{16,48}... | collective-permute-start | bytes 98312 | tf_op jit(solution)/shard_map/ppermute | solution.py:35
  39.5 8.2 %collective-permute-start.1 = (f32[672,256]{1,0:T(8,128)}, f32[672,256]{1,0:T(8,128)}, u32[]{:S(2)}, u32[]{:S(2)}) collective-permute-start(f32[672,256]{1,0:T(8,128)} %get-tuple-element.31), channel_id=1, source_target_pairs={{0,64},{64,0},{1,65},{65,1},{2,66},{66,2},{3,67},{67,3},{4,68},{68... | collective-permute-start | bytes 2064392 | tf_op jit(solution)/shard_map/ppermute | solution.py:39
  39.6 22.8 %all-to-all-start.1 = ((bf16[16,2,4,4096]{3,2,1,0:T(4,128)(2,1)}), bf16[16,2,4,4096]{3,2,1,0:T(4,128)(2,1)S(1)}, u32[]{:S(2)}, u32[]{:S(2)}) async-start(bf16[16,2,4,4096]{3,2,1,0:T(4,128)(2,1)} %broadcast_in_dim.7), calls=%async_computation.1 | async-start | bytes 2097152 | tf_op jit(solution)/shard_map/all_to_all | solution.py:270
  49.7 17.9 %collective-permute-start.3 = (f32[672,256]{1,0:T(8,128)}, f32[672,256]{1,0:T(8,128)}, u32[]{:S(2)}, u32[]{:S(2)}) collective-permute-start(f32[672,256]{1,0:T(8,128)} %add.41), channel_id=1, source_target_pairs={{0,1},{1,0},{2,3},{3,2},{4,5},{5,4},{6,7},{7,6},{8,9},{9,8},{10,11... | collective-permute-start | bytes 2064392 | tf_op jit(solution)/shard_map/ppermute | solution.py:43
  50.3 8.5 %collective-permute-start.2 = (f32[336,256]{1,0:T(8,128)S(1)}, f32[336,256]{1,0:T(8,128)S(1)}, u32[]{:S(2)}, u32[]{:S(2)}) collective-permute-start(f32[336,256]{1,0:T(8,128)S(1)} %get-tuple-element.37), channel_id=1, source_target_pairs={{0,64},{64,0},{1,65},{65,1},{2,66},{66,2},{3,67},{67,3},{4,68},{68... | collective-permute-start | bytes 1032200 | tf_op jit(solution)/shard_map/ppermute | solution.py:39
  57.8 1.0 copy-start.4
  58.7 9.0 %copy-start.5 = (f32[1008,256]{1,0:T(8,128)S(1)}, f32[1008,256]{1,0:T(8,128)}, u32[]{:S(2)}) copy-start(f32[1008,256]{1,0:T(8,128)} %copy-done.4) | copy-start | bytes 3096580
  67.6 2.7 %collective-permute-start.6 = (bf16[128,4096]{1,0:T(8,128)(2,1)S(1)}, bf16[128,4096]{1,0:T(8,128)(2,1)S(1)}, u32[]{:S(2)}, u32[]{:S(2)}) collective-permute-start(bf16[128,4096]{1,0:T(8,128)(2,1)S(1)} %shard_map.80.own_ref), channel_id=1, source_target_pairs={{0,64},{64,0},{1,65},{65,1},{2,66},{66,2},{3,67},{67,3},{4,68},{68... | collective-permute-start | bytes 3145736 | tf_op jit(solution)/shard_map/ppermute | solution.py:39
  67.7 10.6 %collective-permute-start.4 = (f32[1008,256]{1,0:T(8,128)S(1)}, f32[1008,256]{1,0:T(8,128)S(1)}, u32[]{:S(2)}, u32[]{:S(2)}) collective-permute-start(f32[1008,256]{1,0:T(8,128)S(1)} %copy-done.5), channel_id=1, source_target_pairs={{0,64},{64,0},{1,65},{65,1},{2,66},{66,2},{3,67},{67,3},{4,68},{68... | collective-permute-start | bytes 3096584 | tf_op jit(solution)/shard_map/ppermute | solution.py:39
  68.2 10.1 %collective-permute-start.5 = (f32[336,256]{1,0:T(8,128)S(1)}, f32[336,256]{1,0:T(8,128)S(1)}, u32[]{:S(2)}, u32[]{:S(2)}) collective-permute-start(f32[336,256]{1,0:T(8,128)S(1)} %add.42), channel_id=1, source_target_pairs={{0,1},{1,0},{2,3},{3,2},{4,5},{5,4},{6,7},{7,6},{8,9},{9,8},{10,11... | collective-permute-start | bytes 1032200 | tf_op jit(solution)/shard_map/ppermute | solution.py:43
  70.4 3.3 %copy-start = (bf16[4096,1002]{0,1:T(8,128)(2,1)S(1)}, bf16[4096,1002]{0,1:T(8,128)(2,1)}, u32[]{:S(2)}) copy-start(bf16[4096,1002]{0,1:T(8,128)(2,1)} %param.9) | copy-start | bytes 24625156
  73.7 4.6 %copy-start.2 = (s32[256]{0:T(256)S(1)}, s32[256]{0:T(256)}, u32[]{:S(2)}) copy-start(s32[256]{0:T(256)} %param.10) | copy-start | bytes 3076
  80.4 22.6 %copy-start.3 = (f32[256]{0:T(256)S(1)}, f32[256]{0:T(256)}, u32[]{:S(2)}) copy-start(f32[256]{0:T(256)} %param.11) | copy-start | bytes 3076
  80.4 1.3 collective-permute-start.7
  103.0 3.3 %copy-start.1 = (bf16[4096,1002]{0,1:T(8,128)(2,1)S(1)}, bf16[4096,1002]{0,1:T(8,128)(2,1)}, u32[]{:S(2)}) copy-start(bf16[4096,1002]{0,1:T(8,128)(2,1)} %param.9) | copy-start | bytes 24625156
  109.8 2.7 %collective-permute-start.8 = (bf16[128,4096]{1,0:T(8,128)(2,1)S(1)}, bf16[128,4096]{1,0:T(8,128)(2,1)S(1)}, u32[]{:S(2)}, u32[]{:S(2)}) collective-permute-start(bf16[128,4096]{1,0:T(8,128)(2,1)S(1)} %get-tuple-element.47), channel_id=1, source_target_pairs={{0,64},{64,0},{1,65},{65,1},{2,66},{66,2},{3,67},{67,3},{4,68},{68... | collective-permute-start | bytes 3145736 | tf_op jit(solution)/shard_map/ppermute | solution.py:39
  114.4 23.6 %all-to-all-start.3 = ((bf16[64,2,4096]{2,1,0:T(2,128)(2,1)}), bf16[64,2,4096]{2,1,0:T(2,128)(2,1)S(1)}, u32[]{:S(2)}, u32[]{:S(2)}) async-start(bf16[64,2,4096]{2,1,0:T(2,128)(2,1)} %reshape.63), calls=%async_computation.3 | async-start | bytes 2097152 | tf_op jit(solution)/shard_map/all_to_all | solution.py:297

commit v3 on v2

--- a/solution.py
+++ b/solution.py
@@ -43,6 +43,14 @@
     return lax.ppermute(a, "seq", [(0, 1), (1, 0)])
 
 
+def spread_rows(rows, copies):
+    def kernel(in_ref, out_ref):
+        for i in range(copies):
+            out_ref[i] = in_ref[...]
+
+    return call(kernel, jax.ShapeDtypeStruct((copies,) + rows.shape, rows.dtype), rows)
+
+
 def place(a):
     n, two, m, w = a.shape
 
@@ -58,46 +66,43 @@
     step = width // (2 * BLOCKS)
     tokens = rows.shape[0]
     padded = -(-step // 8) * 8
-
-    def kernel(ids_ref, w_hbm, x_ref, own_ref, other_ref, w_buf, acc, sems):
+    pair = 2
+
+    def place(i, ids_ref):
+        part = ids_ref[1] if mine else 1 - ids_ref[1]
+        return ((part * BLOCKS + first) // pair + i, 0, 0)
+
+    def kernel(ids_ref, w_ref, x_ref, own_ref, other_ref, acc):
         g = ids_ref[0]
-        part = ids_ref[1] if mine else 1 - ids_ref[1]
-        copies = []
-        for i in range(count):
-            start = (part * BLOCKS + first + i) * step
-            copies.append(
-                pltpu.make_async_copy(w_hbm.at[pl.ds(start, step)], w_buf.at[i], sems.at[i])
-            )
-        for c in copies:
-            c.start()
-        for i in range(count):
-            copies[i].wait()
-            w = w_buf[i].reshape(2 * step, depth)
-            out = lax.dot_general(
-                w, x_ref[...], (((1,), (1,)), ((), ())), preferred_element_type=F32
-            )
-            for lane in range(tokens // 128):
-                cols = slice(lane * 128, lane * 128 + 128)
-                acc[lane, 0 : 2 * step, :] = out[:, cols]
-                rows = slice(i * padded, i * padded + step)
-                own_ref[rows, cols] = acc[lane, pl.ds(g, step, stride=2), :]
-                other_ref[rows, cols] = acc[lane, pl.ds(1 - g, step, stride=2), :]
+        w = w_ref[...].reshape(2 * pair * step, depth)
+        out = lax.dot_general(w, x_ref[...], (((1,), (1,)), ((), ())), preferred_element_type=F32)
+        for lane in range(tokens // 128):
+            cols = slice(lane * 128, lane * 128 + 128)
+            acc[lane, 0 : 2 * pair * step, :] = out[:, cols]
+            for i in range(pair):
+                to = slice(i * padded, i * padded + step)
+                start = i * 2 * step
+                own_ref[to, cols] = acc[lane, pl.ds(start + g, step, stride=2), :]
+                other_ref[to, cols] = acc[lane, pl.ds(start + 1 - g, step, stride=2), :]
 
     out = jax.ShapeDtypeStruct((count * padded, tokens), F32)
-    return call(
-        kernel,
-        [out, out],
-        ids,
-        head,
-        rows,
-        in_specs=[SMEM, pl.BlockSpec(memory_space=pl.ANY), VMEM],
-        scratch=[
-            pltpu.VMEM((count, step, 2, depth), BF16),
-            pltpu.VMEM((tokens // 128, 2 * step + 18, 128), F32),
-            pltpu.SemaphoreType.DMA((count,)),
-        ],
-        mib=50,
-    )
+    block = pl.BlockSpec((pair * padded, tokens), lambda i, r: (i, 0))
+    return pl.pallas_call(
+        kernel,
+        grid_spec=pltpu.PrefetchScalarGridSpec(
+            num_scalar_prefetch=1,
+            grid=(count // pair,),
+            in_specs=[
+                pl.BlockSpec((pair * step, 2, depth), place),
+                pl.BlockSpec((tokens, depth), lambda i, r: (0, 0)),
+            ],
+            out_specs=[block, block],
+            scratch_shapes=[pltpu.VMEM((tokens // 128, 2 * pair * step + 20, 128), F32)],
+        ),
+        out_shape=[out, out],
+        compiler_params=params(50),
+        cost_estimate=TINY,
+    )(ids, head, rows)
 
 
 def student_product(head, own, other, ids):
@@ -246,6 +251,26 @@
     )
 
 
+def add_parts(own, other, blocks):
+    tokens, depth = own.shape
+
+    def kernel(own_ref, other_ref, out_ref):
+        total = own_ref[...] + other_ref[...].astype(F32)
+        out_ref[...] = total.reshape(out_ref.shape).astype(BF16)
+
+    return call(kernel, jax.ShapeDtypeStruct((blocks, tokens // blocks, depth), BF16), own, other)
+
+
+def sum_parts(parts):
+    def kernel(in_ref, out_ref):
+        total = in_ref[0].astype(F32)
+        for i in range(1, in_ref.shape[0]):
+            total += in_ref[i].astype(F32)
+        out_ref[...] = total.astype(BF16)
+
+    return call(kernel, jax.ShapeDtypeStruct(parts.shape[1:], BF16), parts)
+
+
 def body(teacher_rows, student_rows, teacher_head, student_head, targets, loss_grad):
     t_head = jnp.transpose(teacher_head, (2, 1, 0))
     s_head = jnp.transpose(student_head, (1, 0))
@@ -253,49 +278,46 @@
     grp, vocab, seq = lax.axis_index("grp"), lax.axis_index("vocab"), lax.axis_index("seq")
     shard = (grp * lax.axis_size("vocab") + vocab) * lax.axis_size("seq") + seq
     ids = jnp.stack([grp, seq, (vocab // 4) % 4, vocab % 4, shard * width]).astype(jnp.int32)
-    lower = vocab < 16
     targets2, loss_grad2 = targets.reshape(1, -1), loss_grad.reshape(1, -1)
 
-    def pair(a):
-        b = swap_xhi(a)
-        return jnp.where(lower, jnp.stack([a, b]), jnp.stack([b, a]))
-
     after = lax.optimization_barrier
-    a = jnp.broadcast_to(teacher_rows[None], (32,) + teacher_rows.shape)
+
+    near_b = swap_xhi(student_rows)
+    pair = [jnp.where(vocab < 16, p, q) for p, q in ((student_rows, near_b), (near_b, student_rows))]
+    b = spread_rows(jnp.stack(pair), 16)
+    a = spread_rows(teacher_rows, lax.axis_size("vocab"))
     a = lax.all_to_all(a, "vocab", 0, 0, tiled=True).reshape(-1, teacher_rows.shape[1])
+    a, b = after((a, b))
     planes = [[x * 16 + i for i in range(16)] for x in range(2)]
-    b = pair(student_rows)
-    b = jnp.broadcast_to(b[None], (16,) + b.shape)
-    a, b = after((a, b))
     b = lax.all_to_all(b, "vocab", 0, 0, axis_index_groups=planes, tiled=True)
 
-    def send(first, count):
-        own, other = teacher_part(t_head, a, ids, False, first, count)
-        return own, swap_core(other)
-
-    own0, got0 = send(0, 4)
-    a, own0 = after((a, own0))
-    own1, other1 = teacher_part(t_head, a, ids, False, 4, 2)
-    a, own1, other1, sum0 = after((a, own1, other1, own0 + got0))
+    own0, other0 = teacher_part(t_head, a, ids, False, 0, 2)
+    a, sum0 = after((a, own0 + swap_core(other0)))
     near0 = swap_seq(sum0)
-    sum1 = own1 + swap_core(other1)
+    own1, other1 = teacher_part(t_head, a, ids, False, 2, 4)
+    a, own1, other1, near0, b = after((a, own1, other1, near0, b))
+    got1 = swap_core(other1)
+    b = place(b)
+    b_other = swap_core(b)
+    half = sum0.shape[0]
+    sum1, sum2 = own1[:half] + got1[:half], own1[half:] + got1[half:]
+    a, b, b_other, sum1, sum2 = after((a, b, b_other, sum1, sum2))
+    near1 = swap_seq(sum1)
     mine, other = teacher_part(t_head, a, ids, True, 0, BLOCKS)
-    mine, other, b, sum1, near0 = after((mine, other, b, sum1, near0))
-    near1 = swap_seq(sum1)
+    mine, other, b, b_other, sum2, near1 = after((mine, other, b, b_other, sum2, near1))
+    near2 = swap_seq(sum2)
     core = swap_core(other)
-    b = place(b)
-    student = student_product(s_head, b, swap_core(b), ids)
-    near = [near0, near1]
+    student = student_product(s_head, b, b_other, ids)
+    near = [near0, near1, near2]
     teacher, stats = local_stats(mine, core, near, student, targets2, ids)
     stats = merge([stats, swap_core(stats)])
     stats = jnp.broadcast_to(stats[None], (64,) + stats.shape)
     stats = merge_all(lax.all_to_all(stats, ("vocab", "seq"), 0, 0, tiled=True))
 
     own, other = hidden_part(s_head, teacher, student, stats, targets2, loss_grad2, ids)
-    part = (own + swap_core(other).astype(F32)).astype(BF16)
-    part = part.reshape(64, 2, -1)
+    part = add_parts(own, swap_core(other), 64)
     part = lax.all_to_all(part, ("vocab", "seq"), 0, 0, tiled=True)
-    hidden = jnp.sum(part.astype(F32), axis=0).astype(BF16)
+    hidden = sum_parts(part)
 
     t_norm = stats[0] + jnp.log(stats[1])
     s_norm = stats[3] + jnp.log(stats[4])

time: 140 us -> 136 us (0.971)
  local copies, waits for them, and re-layouts: 12.6 us -> 2.7 us
  waiting for transfers between devices: 47.9 us -> 53 us
  other arithmetic: 4.48 us -> 2.29 us
    pallas_call x0 -> x3, Pallas kernels: none -> 14.3 us  [teacher_part(): pl.pallas_call(kernel, grid_spec=pltpu.PrefetchScalarGridSpec(num_scalar_...]
    pallas_call x9 -> x10, Pallas kernels: 26.7 us -> 13.3 us  [call(): pl.pallas_call(kernel, out_shape=out_shape, in_specs=in_specs or [VMEM] *...]
    all_to_all x1, waiting for transfers between devices: 2.59 us -> 15.7 us  [body(): lax.all_to_all(a, 'vocab', 0, 0, tiled=True)]
    ppermute x1, waiting for transfers between devices: 12 us -> 0.01 us  [swap_xhi(): return lax.ppermute(a, 'vocab', [(i, i ^ 16) for i in range(32)])]
    unnamed x14, local copies, waits for them, and re-layouts: 7.65 us -> 2.58 us
    ppermute x2 -> x3, waiting for transfers between devices: 6.74 us -> 10.8 us  [swap_seq(): return lax.ppermute(a, 'seq', [(0, 1), (1, 0)])]
    all_to_all x1, waiting for transfers between devices: 3.53 us -> 0.01 us  [body(): b = lax.all_to_all(b, 'vocab', 0, 0, axis_index_groups=planes, tiled=True)]
    ppermute x6, waiting for transfers between devices: 5.37 us -> 8.79 us  [swap_core(): return lax.ppermute(a, 'grp', [(0, 1), (1, 0)])]
  transfers between devices with their start and end apart: 12 -> 13, of which waited for: 9 -> 9; matrix products, arithmetic and copies ran while one was open for 2% -> 2% of each run, Pallas kernels for 10% -> 14%
where the time goes in v3:
time: 136 us; the launch traced here: 135 us
  waiting for transfers between devices  53 us (39%)
  Pallas kernels  27.5 us (20%)
  starting transfers between devices  26.1 us (19%)
  blocking collectives  22.5 us (17%)
  local copies, waits for them, and re-layouts  2.7 us (2%)
  other arithmetic  2.29 us (2%)
    all_to_all x1, blocking collectives, body(): stats = merge_all(lax.all_to_all(stats, ('vocab', 'seq'), 0, 0, tiled=True))  22.5 us
    all_to_all x1, waiting for transfers between devices, body(): part = lax.all_to_all(part, ('vocab', 'seq'), 0, 0, tiled=True)  17.7 us
    all_to_all x1, waiting for transfers between devices, body(): lax.all_to_all(a, 'vocab', 0, 0, tiled=True)  15.7 us
    pallas_call x3, Pallas kernels, teacher_part(): pl.pallas_call(kernel, grid_spec=pltpu.PrefetchScalarGridSpec(num_scalar_...  14.3 us
    pallas_call x10, Pallas kernels, call(): pl.pallas_call(kernel, out_shape=out_shape, in_specs=in_specs or [VMEM] *...  13.3 us
    ppermute x3, waiting for transfers between devices, swap_seq(): return lax.ppermute(a, 'seq', [(0, 1), (1, 0)])  10.8 us
    ppermute x6, waiting for transfers between devices, swap_core(): return lax.ppermute(a, 'grp', [(0, 1), (1, 0)])  8.79 us
    all_to_all x1, starting transfers between devices, body(): lax.all_to_all(a, 'vocab', 0, 0, tiled=True)  8.33 us
  transfers between devices with their start and end apart: 13, of which 9 were waited for; matrix products, arithmetic and copies ran while one was open for 2% of the time, Pallas kernels for 14%

profile of v3, /device:TPU:0, one launch (start us, length us, event | category | flops | bytes accessed | tf_op | source)
XLA Modules:
  0.0 134.9 jit_solution(17834833958356494802)
XLA Ops:
  0.6 3.2 %collective-permute-start = (bf16[4,4096]{1,0:T(4,128)(2,1)}, bf16[4,4096]{1,0:T(4,128)(2,1)S(1)}, u32[]{:S(2)}, u32[]{:S(2)}) collective-permute-start(bf16[4,4096]{1,0:T(4,128)(2,1)} %param.7), channel_id=1, source_target_pairs={{0,32},{2,34},{4,36},{6,38},{8,40},{10,42},{12,44},{14,46},{16,48}... | collective-permute-start | bytes 98312 | tf_op jit(solution)/shard_map/ppermute | solution.py:35
  3.8 0.8 copy-done
  4.6 1.0 shard_map.77
  5.6 8.3 %all-to-all-start = ((bf16[32,8,2048]{2,1,0:T(8,128)(2,1)}), bf16[32,8,2048]{2,1,0:T(8,128)(2,1)S(1)}, u32[]{:S(2)}, u32[]{:S(2)}) async-start(bf16[32,8,2048]{2,1,0:T(8,128)(2,1)} %shard_map.77), calls=%async_computation | async-start | bytes 2097152 | tf_op jit(solution)/shard_map/all_to_all | solution.py:289
  14.0 0.0 collective-permute-done
  14.0 0.8 select_bitcast_fusion.1
  14.8 1.1 shard_map.78
  15.9 15.7 %all-to-all-done = bf16[32,8,2048]{2,1,0:T(8,128)(2,1)S(1)} async-done(((bf16[32,8,2048]{2,1,0:T(8,128)(2,1)}), bf16[32,8,2048]{2,1,0:T(8,128)(2,1)S(1)}, u32[]{:S(2)}, u32[]{:S(2)}) %all-to-all-start) | async-done | bytes 1048608 | tf_op jit(solution)/shard_map/all_to_all | solution.py:289
  31.6 4.1 %all-to-all-start.1 = ((bf16[16,2,4,4096]{3,2,1,0:T(4,128)(2,1)}), bf16[16,2,4,4096]{3,2,1,0:T(4,128)(2,1)S(1)}, u32[]{:S(2)}, u32[]{:S(2)}) async-start(bf16[16,2,4,4096]{3,2,1,0:T(4,128)(2,1)} %shard_map.78), calls=%async_computation.1 | async-start | bytes 2097152 | tf_op jit(solution)/shard_map/all_to_all | solution.py:292
  35.7 0.1 stack.32.ids_ref
  35.8 3.3 %shard_map.79 = (f32[336,256]{1,0:T(8,128)S(1)}, f32[336,256]{1,0:T(8,128)S(1)}) custom-call(s32[5]{0:T(128)S(1)} %stack.32.ids_ref, bf16[2004,2,2048]{2,1,0:T(2,128)(2,1)} %bitcast.25, bf16[256,2048]{1,0:T(8,128)(2,1)S(1)} %bitcast.19), custom_call_target="tpu_custom_call" | custom-call | flops 1000 | bytes 1000 | tf_op jit(solution)/shard_map/pallas_call | solution.py:90
  39.2 0.1 collective-permute-start.1
  39.3 1.6 %collective-permute-done.1 = f32[336,256]{1,0:T(8,128)S(1)} collective-permute-done((f32[336,256]{1,0:T(8,128)S(1)}, f32[336,256]{1,0:T(8,128)S(1)}, u32[]{:S(2)}, u32[]{:S(2)}) %collective-permute-start.1) | collective-permute-done | bytes 344096 | tf_op jit(solution)/shard_map/ppermute | solution.py:39
  40.9 1.5 %collective-permute-start.2 = (f32[336,256]{1,0:T(8,128)S(1)}, f32[336,256]{1,0:T(8,128)S(1)}, u32[]{:S(2)}, u32[]{:S(2)}) collective-permute-start(f32[336,256]{1,0:T(8,128)S(1)} %add.41), channel_id=1, source_target_pairs={{0,1},{1,0},{2,3},{3,2},{4,5},{5,4},{6,7},{7,6},{8,9},{9,8},{10,11... | collective-permute-start | bytes 1032200 | tf_op jit(solution)/shard_map/ppermute | solution.py:43
  42.5 4.4 %shard_map.80 = (f32[672,256]{1,0:T(8,128)S(1)}, f32[672,256]{1,0:T(8,128)S(1)}) custom-call(s32[5]{0:T(128)S(1)} %stack.32.ids_ref, bf16[2004,2,2048]{2,1,0:T(2,128)(2,1)} %bitcast.26, bf16[256,2048]{1,0:T(8,128)(2,1)S(1)} %bitcast.20), custom_call_target="tpu_custom_call" | custom-call | flops 1000 | bytes 1000 | tf_op jit(solution)/shard_map/pallas_call | solution.py:90
  46.8 0.0 copy-start.4
  46.8 0.8 copy-done.4
  47.7 3.4 %collective-permute-done.2.refs_0_ = f32[336,256]{1,0:T(8,128)S(1)} collective-permute-done((f32[336,256]{1,0:T(8,128)S(1)}, f32[336,256]{1,0:T(8,128)S(1)}, u32[]{:S(2)}, u32[]{:S(2)}) %collective-permute-start.2) | collective-permute-done | bytes 344096 | tf_op jit(solution)/shard_map/ppermute | solution.py:43
  51.1 0.0 all-to-all-done.1.in_ref
  51.1 0.1 shard_map.81.own_ref
  51.2 0.1 collective-permute-start.3
  51.3 0.5 collective-permute-start.4
  51.8 3.3 %collective-permute-done.4 = f32[672,256]{1,0:T(8,128)S(1)} collective-permute-done((f32[672,256]{1,0:T(8,128)}, f32[672,256]{1,0:T(8,128)S(1)}, u32[]{:S(2)}, u32[]{:S(2)}) %collective-permute-start.4) | collective-permute-done | bytes 688160 | tf_op jit(solution)/shard_map/ppermute | solution.py:39
  55.2 0.8 slice_add_fusion
  56.0 0.0 collective-permute-done.3.other_ref
  56.0 1.4 %collective-permute-start.5 = (f32[336,256]{1,0:T(8,128)S(1)}, f32[336,256]{1,0:T(8,128)S(1)}, u32[]{:S(2)}, u32[]{:S(2)}) collective-permute-start(f32[336,256]{1,0:T(8,128)S(1)} %get-tuple-element.50), channel_id=1, source_target_pairs={{0,1},{1,0},{2,3},{3,2},{4,5},{5,4},{6,7},{7,6},{8,9},{9,8},{10,11... | collective-permute-start | bytes 1032200 | tf_op jit(solution)/shard_map/ppermute | solution.py:43
  57.4 6.6 %shard_map.82 = (f32[1008,256]{1,0:T(8,128)S(1)}, f32[1008,256]{1,0:T(8,128)S(1)}) custom-call(s32[5]{0:T(128)S(1)} %stack.32.ids_ref, bf16[2004,2,2048]{2,1,0:T(2,128)(2,1)} %bitcast.27, bf16[256,2048]{1,0:T(8,128)(2,1)S(1)} %bitcast.21), custom_call_target="tpu_custom_call" | custom-call | flops 1000 | bytes 1000 | tf_op jit(solution)/shard_map/pallas_call | solution.py:90
  64.0 0.0 copy-start.3
  64.0 1.0 copy-done.3
  65.0 1.1 collective-permute-done.5.refs_1_
  66.1 0.0 collective-permute-start.6
  66.1 1.4 %collective-permute-start.7 = (f32[336,256]{1,0:T(8,128)}, f32[336,256]{1,0:T(8,128)S(1)}, u32[]{:S(2)}, u32[]{:S(2)}) collective-permute-start(f32[336,256]{1,0:T(8,128)} %get-tuple-element.55), channel_id=1, source_target_pairs={{0,1},{1,0},{2,3},{3,2},{4,5},{5,4},{6,7},{7,6},{8,9},{9,8},{10,11... | collective-permute-start | bytes 1032200 | tf_op jit(solution)/shard_map/ppermute | solution.py:43
  67.5 3.0 %shard_map.83.refs_3_.sl_ref = f32[1002,256]{1,0:T(8,128)S(1)} custom-call(s32[5]{0:T(128)S(1)} %stack.32.ids_ref, bf16[1002,4096]{1,0:T(8,128)(2,1)S(1)} %bitcast.17, bf16[128,4096]{1,0:T(8,128)(2,1)S(1)} %shard_map.81.own_ref, bf16[128,4096]{1,0:T(8,128)(2,1)S(1)} %collective-permute-done.3.other_ref), custom_call_target="tpu_custom_call" | custom-call | flops 1000 | bytes 1000 | tf_op jit(solution)/shard_map/pallas_call | solution.py:23
  70.6 6.2 %collective-permute-done.7.refs_2_ = f32[336,256]{1,0:T(8,128)S(1)} collective-permute-done((f32[336,256]{1,0:T(8,128)}, f32[336,256]{1,0:T(8,128)S(1)}, u32[]{:S(2)}, u32[]{:S(2)}) %collective-permute-start.7) | collective-permute-done | bytes 344096 | tf_op jit(solution)/shard_map/ppermute | solution.py:43
  76.8 0.0 collective-permute-done.6.core_ref
  76.8 1.5 %shard_map.84 = (f32[1002,256]{1,0:T(8,128)S(1)}, f32[8,256]{1,0:T(8,128)S(1)}) custom-call(s32[5]{0:T(128)S(1)} %stack.32.ids_ref, f32[1008,256]{1,0:T(8,128)S(1)} %get-tuple-element.51.mine_ref, f32[1008,256]{1,0:T(8,128)S(1)} %collective-permute-done.6.core_ref, f32[336,256]{1,0:T(8,128)S(1)} %collective-permute-done.2.refs_0_, ...), custom_call_target="tpu_custom_call" | custom-call | flops 1000 | bytes 1000 | tf_op jit(solution)/shard_map/pallas_call | solution.py:23
  78.3 0.1 collective-permute-start.8
  78.4 1.2 collective-permute-done.8.refs_1_
  79.6 22.5 %all_to_all.20.in_ref = f32[64,8,256]{2,1,0:T(8,128)S(1)} all-to-all(f32[64,8,256]{2,1,0:T(8,128)S(1)} %broadcast_in_dim.2), channel_id=1, replica_groups=mesh['grp'=2,'vocab'=32,'seq'=2] {'vocab','seq'}, dimensions={0} | all-to-all | bytes 1048576 | tf_op jit(solution)/shard_map/all_to_all | solution.py:315
  102.1 0.2 shard_map.86.st_ref
  102.3 3.4 %shard_map.87 = (f32[128,4096]{1,0:T(8,128)S(1)}, bf16[128,4096]{1,0:T(8,128)(2,1)S(1)}) custom-call(s32[5]{0:T(128)S(1)} %stack.32.ids_ref, bf16[1002,4096]{1,0:T(8,128)(2,1)S(1)} %bitcast.18, f32[1002,256]{1,0:T(8,128)S(1)} %get-tuple-element.58.tl_ref, f32[1002,256]{1,0:T(8,128)S(1)} %shard_map.83.refs_3_.sl_ref, f32[8,256]{1,0:T(8,128)S(1)} %shard_map.86.st_ref, ...), custom_call_target="tpu_custom_call" | custom-call | flops 1000 | bytes 1000 | tf_op jit(solution)/shard_map/pallas_call | solution.py:23
  105.7 0.1 collective-permute-start.9
  105.8 2.6 %collective-permute-done.9.other_ref = bf16[128,4096]{1,0:T(8,128)(2,1)S(1)} collective-permute-done((bf16[128,4096]{1,0:T(8,128)(2,1)S(1)}, bf16[128,4096]{1,0:T(8,128)(2,1)S(1)}, u32[]{:S(2)}, u32[]{:S(2)}) %collective-permute-start.9) | collective-permute-done | bytes 1048608 | tf_op jit(solution)/shard_map/ppermute | solution.py:39
  108.5 2.1 %shard_map.88 = bf16[64,2,4096]{2,1,0:T(2,128)(2,1)} custom-call(f32[128,4096]{1,0:T(8,128)S(1)} %get-tuple-element.60.own_ref, bf16[128,4096]{1,0:T(8,128)(2,1)S(1)} %collective-permute-done.9.other_ref), custom_call_target="tpu_custom_call" | custom-call | flops 1000 | bytes 1000 | tf_op jit(solution)/shard_map/pallas_call | solution.py:23
  110.6 5.3 %all-to-all-start.3 = ((bf16[64,2,4096]{2,1,0:T(2,128)(2,1)}), bf16[64,2,4096]{2,1,0:T(2,128)(2,1)S(1)}, u32[]{:S(2)}, u32[]{:S(2)}) async-start(bf16[64,2,4096]{2,1,0:T(2,128)(2,1)} %shard_map.88), calls=%async_computation.3 | async-start | bytes 2097152 | tf_op jit(solution)/shard_map/all_to_all | solution.py:319
  115.9 0.6 slice_subtract_fusion
  116.5 17.7 %all-to-all-done.3.in_ref = bf16[64,2,4096]{2,1,0:T(2,128)(2,1)S(1)} async-done(((bf16[64,2,4096]{2,1,0:T(2,128)(2,1)}), bf16[64,2,4096]{2,1,0:T(2,128)(2,1)S(1)}, u32[]{:S(2)}, u32[]{:S(2)}) %all-to-all-start.3) | async-done | bytes 1048608 | tf_op jit(solution)/shard_map/all_to_all | solution.py:319
  134.1 0.8 shard_map.89
  (14 shorter events, 0.2 us)
Async XLA Ops:
  0.6 13.3 %collective-permute-start = (bf16[4,4096]{1,0:T(4,128)(2,1)}, bf16[4,4096]{1,0:T(4,128)(2,1)S(1)}, u32[]{:S(2)}, u32[]{:S(2)}) collective-permute-start(bf16[4,4096]{1,0:T(4,128)(2,1)} %param.7), channel_id=1, source_target_pairs={{0,32},{2,34},{4,36},{6,38},{8,40},{10,42},{12,44},{14,46},{16,48}... | collective-permute-start | bytes 98312 | tf_op jit(solution)/shard_map/ppermute | solution.py:35
  3.8 0.8 copy-start
  5.6 26.0 %all-to-all-start = ((bf16[32,8,2048]{2,1,0:T(8,128)(2,1)}), bf16[32,8,2048]{2,1,0:T(8,128)(2,1)S(1)}, u32[]{:S(2)}, u32[]{:S(2)}) async-start(bf16[32,8,2048]{2,1,0:T(8,128)(2,1)} %shard_map.77), calls=%async_computation | async-start | bytes 2097152 | tf_op jit(solution)/shard_map/all_to_all | solution.py:289
  31.6 19.5 %all-to-all-start.1 = ((bf16[16,2,4,4096]{3,2,1,0:T(4,128)(2,1)}), bf16[16,2,4,4096]{3,2,1,0:T(4,128)(2,1)S(1)}, u32[]{:S(2)}, u32[]{:S(2)}) async-start(bf16[16,2,4,4096]{3,2,1,0:T(4,128)(2,1)} %shard_map.78), calls=%async_computation.1 | async-start | bytes 2097152 | tf_op jit(solution)/shard_map/all_to_all | solution.py:292
  39.2 1.7 %collective-permute-start.1 = (f32[336,256]{1,0:T(8,128)S(1)}, f32[336,256]{1,0:T(8,128)S(1)}, u32[]{:S(2)}, u32[]{:S(2)}) collective-permute-start(f32[336,256]{1,0:T(8,128)S(1)} %get-tuple-element.34), channel_id=1, source_target_pairs={{0,64},{64,0},{1,65},{65,1},{2,66},{66,2},{3,67},{67,3},{4,68},{68... | collective-permute-start | bytes 1032200 | tf_op jit(solution)/shard_map/ppermute | solution.py:39
  40.9 10.2 %collective-permute-start.2 = (f32[336,256]{1,0:T(8,128)S(1)}, f32[336,256]{1,0:T(8,128)S(1)}, u32[]{:S(2)}, u32[]{:S(2)}) collective-permute-start(f32[336,256]{1,0:T(8,128)S(1)} %add.41), channel_id=1, source_target_pairs={{0,1},{1,0},{2,3},{3,2},{4,5},{5,4},{6,7},{7,6},{8,9},{9,8},{10,11... | collective-permute-start | bytes 1032200 | tf_op jit(solution)/shard_map/ppermute | solution.py:43
  46.8 0.8 copy-start.4
  51.2 4.8 %collective-permute-start.3 = (bf16[128,4096]{1,0:T(8,128)(2,1)S(1)}, bf16[128,4096]{1,0:T(8,128)(2,1)S(1)}, u32[]{:S(2)}, u32[]{:S(2)}) collective-permute-start(bf16[128,4096]{1,0:T(8,128)(2,1)S(1)} %shard_map.81.own_ref), channel_id=1, source_target_pairs={{0,64},{64,0},{1,65},{65,1},{2,66},{66,2},{3,67},{67,3},{4,68},{68... | collective-permute-start | bytes 3145736 | tf_op jit(solution)/shard_map/ppermute | solution.py:39
  51.3 3.8 %collective-permute-start.4 = (f32[672,256]{1,0:T(8,128)}, f32[672,256]{1,0:T(8,128)S(1)}, u32[]{:S(2)}, u32[]{:S(2)}) collective-permute-start(f32[672,256]{1,0:T(8,128)} %copy-done.4), channel_id=1, source_target_pairs={{0,64},{64,0},{1,65},{65,1},{2,66},{66,2},{3,67},{67,3},{4,68},{68... | collective-permute-start | bytes 2064392 | tf_op jit(solution)/shard_map/ppermute | solution.py:39
  56.0 11.5 %slice-start = ((s8[8257536]{0:T(1024)(128)(4,1)}), s8[4194304]{0:T(1024)(128)(4,1)S(1)}, s32[]{:S(2)}) async-start(s8[8257536]{0:T(1024)(128)(4,1)} %bitcast.15), calls=%async_computation.4 | async-start | bytes 8388608
  56.0 11.5 %slice-start.1 = ((s8[8257536]{0:T(1024)(128)(4,1)}), s8[4063232]{0:T(1024)(128)(4,1)S(1)}, s32[]{:S(2)}) async-start(s8[8257536]{0:T(1024)(128)(4,1)} %bitcast.15), calls=%async_computation.5 | async-start | bytes 8126464
  56.0 10.1 %collective-permute-start.5 = (f32[336,256]{1,0:T(8,128)S(1)}, f32[336,256]{1,0:T(8,128)S(1)}, u32[]{:S(2)}, u32[]{:S(2)}) collective-permute-start(f32[336,256]{1,0:T(8,128)S(1)} %get-tuple-element.50), channel_id=1, source_target_pairs={{0,1},{1,0},{2,3},{3,2},{4,5},{5,4},{6,7},{7,6},{8,9},{9,8},{10,11... | collective-permute-start | bytes 1032200 | tf_op jit(solution)/shard_map/ppermute | solution.py:43
  64.0 1.0 copy-start.3
  65.0 11.8 %copy-start.1 = (s32[256]{0:T(256)S(1)}, s32[256]{0:T(256)}, u32[]{:S(2)}) copy-start(s32[256]{0:T(256)} %param.10) | copy-start | bytes 3076
  66.1 10.7 %collective-permute-start.6 = (f32[1008,256]{1,0:T(8,128)}, f32[1008,256]{1,0:T(8,128)S(1)}, u32[]{:S(2)}, u32[]{:S(2)}) collective-permute-start(f32[1008,256]{1,0:T(8,128)} %copy-done.3), channel_id=1, source_target_pairs={{0,64},{64,0},{1,65},{65,1},{2,66},{66,2},{3,67},{67,3},{4,68},{68... | collective-permute-start | bytes 3096584 | tf_op jit(solution)/shard_map/ppermute | solution.py:39
  66.1 10.7 %collective-permute-start.7 = (f32[336,256]{1,0:T(8,128)}, f32[336,256]{1,0:T(8,128)S(1)}, u32[]{:S(2)}, u32[]{:S(2)}) collective-permute-start(f32[336,256]{1,0:T(8,128)} %get-tuple-element.55), channel_id=1, source_target_pairs={{0,1},{1,0},{2,3},{3,2},{4,5},{5,4},{6,7},{7,6},{8,9},{9,8},{10,11... | collective-permute-start | bytes 1032200 | tf_op jit(solution)/shard_map/ppermute | solution.py:43
  67.5 34.8 %copy-start.2 = (f32[256]{0:T(256)S(1)}, f32[256]{0:T(256)}, u32[]{:S(2)}) copy-start(f32[256]{0:T(256)} %param.11) | copy-start | bytes 3076
  78.3 1.2 collective-permute-start.8
  105.7 2.7 %collective-permute-start.9 = (bf16[128,4096]{1,0:T(8,128)(2,1)S(1)}, bf16[128,4096]{1,0:T(8,128)(2,1)S(1)}, u32[]{:S(2)}, u32[]{:S(2)}) collective-permute-start(bf16[128,4096]{1,0:T(8,128)(2,1)S(1)} %get-tuple-element.61), channel_id=1, source_target_pairs={{0,64},{64,0},{1,65},{65,1},{2,66},{66,2},{3,67},{67,3},{4,68},{68... | collective-permute-start | bytes 3145736 | tf_op jit(solution)/shard_map/ppermute | solution.py:39
  110.6 23.6 %all-to-all-start.3 = ((bf16[64,2,4096]{2,1,0:T(2,128)(2,1)}), bf16[64,2,4096]{2,1,0:T(2,128)(2,1)S(1)}, u32[]{:S(2)}, u32[]{:S(2)}) async-start(bf16[64,2,4096]{2,1,0:T(2,128)(2,1)} %shard_map.88), calls=%async_computation.3 | async-start | bytes 2097152 | tf_op jit(solution)/shard_map/all_to_all | solution.py:319

commit v4 on v3

--- a/solution.py
+++ b/solution.py
@@ -66,7 +66,7 @@
     step = width // (2 * BLOCKS)
     tokens = rows.shape[0]
     padded = -(-step // 8) * 8
-    pair = 2
+    pair = min(count, 3)
 
     def place(i, ids_ref):
         part = ids_ref[1] if mine else 1 - ids_ref[1]
@@ -144,31 +144,34 @@
 
     def kernel(ids_ref, mine_ref, core_ref, *refs):
         near_refs = refs[: len(near)]
-        s_ref, t_ref, tl_ref, out_ref = refs[len(near) :]
+        s_ref, t_ref, te_ref, se_ref, out_ref = refs[len(near) :]
         b = 0
         for ref in near_refs:
             for i in range(ref.shape[0] // padded):
                 here = slice(b * padded, b * padded + step)
                 there = slice(i * padded, i * padded + step)
                 own = mine_ref[here, :] + core_ref[here, :]
-                tl_ref[b * step : (b + 1) * step, :] = own + ref[there, :]
+                te_ref[b * step : (b + 1) * step, :] = own + ref[there, :]
                 b += 1
-        t, s = tl_ref[...], s_ref[...]
+        t, s = te_ref[...], s_ref[...]
         t_top = jnp.max(t, axis=0, keepdims=True)
         s_top = jnp.max(s, axis=0, keepdims=True)
         e = jnp.exp(t - t_top)
+        te_ref[...] = e
         out_ref[0:1, :] = t_top
         out_ref[1:2, :] = jnp.sum(e, axis=0, keepdims=True)
         out_ref[2:3, :] = jnp.sum(e * (t - s), axis=0, keepdims=True)
         out_ref[3:4, :] = s_top
-        out_ref[4:5, :] = jnp.sum(jnp.exp(s - s_top), axis=0, keepdims=True)
+        e = jnp.exp(s - s_top)
+        se_ref[...] = e
+        out_ref[4:5, :] = jnp.sum(e, axis=0, keepdims=True)
         hit = hits(ids_ref, t_ref, s.shape)
         out_ref[5:6, :] = jnp.sum(jnp.where(hit, s, jnp.zeros_like(s)), axis=0, keepdims=True)
         out_ref[6:8, :] = jnp.zeros((2, tokens), F32)
 
     return call(
         kernel,
-        [jax.ShapeDtypeStruct((width, tokens), F32), jax.ShapeDtypeStruct((8, tokens), F32)],
+        [jax.ShapeDtypeStruct((width, tokens), F32)] * 2 + [jax.ShapeDtypeStruct((8, tokens), F32)],
         ids,
         mine,
         core,
@@ -214,16 +217,18 @@
     return call(kernel, jax.ShapeDtypeStruct(stats.shape[1:], F32), stats)
 
 
-def hidden_part(head, teacher, student, stats, targets, loss_grad, ids):
+def hidden_part(head, teacher, student, here, stats, targets, loss_grad, ids):
     width, depth = head.shape
     tokens = teacher.shape[1]
     half = tokens // 2
     block = 1024
 
-    def kernel(ids_ref, w_ref, tl_ref, sl_ref, st_ref, t_ref, g_ref, own_ref, other_ref, grad):
-        st = st_ref[...]
-        t_probs = jnp.exp(tl_ref[...] - st[0:1, :]) / st[1:2, :]
-        s_probs = jnp.exp(sl_ref[...] - st[3:4, :]) / st[4:5, :]
+    def kernel(
+        ids_ref, w_ref, te_ref, se_ref, here_ref, st_ref, t_ref, g_ref, own_ref, other_ref, grad
+    ):
+        st, here = st_ref[...], here_ref[...]
+        t_probs = te_ref[...] * (jnp.exp(here[0:1, :] - st[0:1, :]) / st[1:2, :])
+        s_probs = se_ref[...] * (jnp.exp(here[3:4, :] - st[3:4, :]) / st[4:5, :])
         hit = hits(ids_ref, t_ref, t_probs.shape)
         value = g_ref[...] * (2.0 * s_probs - t_probs - hit.astype(F32))
         first = ids_ref[0] == 0
@@ -243,10 +248,11 @@
         head,
         teacher,
         student,
+        here,
         stats,
         targets,
         loss_grad,
-        in_specs=[SMEM] + [VMEM] * 6,
+        in_specs=[SMEM] + [VMEM] * 7,
         scratch=[pltpu.VMEM((tokens, width), BF16)],
     )
 
@@ -292,29 +298,31 @@
     b = lax.all_to_all(b, "vocab", 0, 0, axis_index_groups=planes, tiled=True)
 
     own0, other0 = teacher_part(t_head, a, ids, False, 0, 2)
-    a, sum0 = after((a, own0 + swap_core(other0)))
+    got0 = swap_core(other0)
+    a, own0 = after((a, own0))
+    own1, other1 = teacher_part(t_head, a, ids, False, 2, 2)
+    a, own1, other1, sum0 = after((a, own1, other1, own0 + got0))
     near0 = swap_seq(sum0)
-    own1, other1 = teacher_part(t_head, a, ids, False, 2, 4)
-    a, own1, other1, near0, b = after((a, own1, other1, near0, b))
-    got1 = swap_core(other1)
+    sum1 = own1 + swap_core(other1)
+    own2, other2 = teacher_part(t_head, a, ids, False, 4, 2)
+    a, own2, other2, sum1, near0, b = after((a, own2, other2, sum1, near0, b))
     b = place(b)
+    a, own2, other2, sum1, b = after((a, own2, other2, sum1, b))
+    near1 = swap_seq(sum1)
+    sum2 = own2 + swap_core(other2)
     b_other = swap_core(b)
-    half = sum0.shape[0]
-    sum1, sum2 = own1[:half] + got1[:half], own1[half:] + got1[half:]
-    a, b, b_other, sum1, sum2 = after((a, b, b_other, sum1, sum2))
-    near1 = swap_seq(sum1)
     mine, other = teacher_part(t_head, a, ids, True, 0, BLOCKS)
     mine, other, b, b_other, sum2, near1 = after((mine, other, b, b_other, sum2, near1))
     near2 = swap_seq(sum2)
     core = swap_core(other)
     student = student_product(s_head, b, b_other, ids)
     near = [near0, near1, near2]
-    teacher, stats = local_stats(mine, core, near, student, targets2, ids)
-    stats = merge([stats, swap_core(stats)])
-    stats = jnp.broadcast_to(stats[None], (64,) + stats.shape)
+    teacher, student, here = local_stats(mine, core, near, student, targets2, ids)
+    stats = merge([here, swap_core(here)])
+    stats = spread_rows(stats, 64)
     stats = merge_all(lax.all_to_all(stats, ("vocab", "seq"), 0, 0, tiled=True))
 
-    own, other = hidden_part(s_head, teacher, student, stats, targets2, loss_grad2, ids)
+    own, other = hidden_part(s_head, teacher, student, here, stats, targets2, loss_grad2, ids)
     part = add_parts(own, swap_core(other), 64)
     part = lax.all_to_all(part, ("vocab", "seq"), 0, 0, tiled=True)
     hidden = sum_parts(part)

time: 136 us -> 134 us (0.985)
  waiting for transfers between devices: 53 us -> 49.1 us
  Pallas kernels: 27.5 us -> 29.8 us
  local copies, waits for them, and re-layouts: 2.7 us -> 0.86 us
    ppermute x6 -> x7, waiting for transfers between devices: 8.79 us -> 3.82 us  [swap_core(): return lax.ppermute(a, 'grp', [(0, 1), (1, 0)])]
    pallas_call x3 -> x4, Pallas kernels: 14.3 us -> 16.4 us  [teacher_part(): pl.pallas_call(kernel, grid_spec=pltpu.PrefetchScalarGridSpec(num_scalar_...]
    unnamed x14 -> x10, local copies, waits for them, and re-layouts: 2.58 us -> 0.78 us
    pallas_call x10 -> x11, Pallas kernels: 13.3 us -> 13.4 us  [call(): pl.pallas_call(kernel, out_shape=out_shape, in_specs=in_specs or [VMEM] *...]
  transfers between devices with their start and end apart: 13 -> 14, of which waited for: 9 -> 7; matrix products, arithmetic and copies ran while one was open for 2% -> 3% of each run, Pallas kernels for 14% -> 16%
where the time goes in v4:
time: 134 us; the launch traced here: 133 us
  waiting for transfers between devices  49.1 us (37%)
  Pallas kernels  29.8 us (22%)
  starting transfers between devices  26.6 us (20%)
  blocking collectives  22.5 us (17%)
  other arithmetic  3.27 us (2%)
    all_to_all x1, blocking collectives, body(): stats = merge_all(lax.all_to_all(stats, ('vocab', 'seq'), 0, 0, tiled=True))  22.5 us
    all_to_all x1, waiting for transfers between devices, body(): part = lax.all_to_all(part, ('vocab', 'seq'), 0, 0, tiled=True)  17.7 us
    pallas_call x4, Pallas kernels, teacher_part(): pl.pallas_call(kernel, grid_spec=pltpu.PrefetchScalarGridSpec(num_scalar_...  16.4 us
    all_to_all x1, waiting for transfers between devices, body(): lax.all_to_all(a, 'vocab', 0, 0, tiled=True)  15.7 us
    pallas_call x11, Pallas kernels, call(): pl.pallas_call(kernel, out_shape=out_shape, in_specs=in_specs or [VMEM] *...  13.4 us
    ppermute x3, waiting for transfers between devices, swap_seq(): return lax.ppermute(a, 'seq', [(0, 1), (1, 0)])  11.9 us
    all_to_all x1, starting transfers between devices, body(): lax.all_to_all(a, 'vocab', 0, 0, tiled=True)  8.33 us
    all_to_all x1, starting transfers between devices, body(): part = lax.all_to_all(part, ('vocab', 'seq'), 0, 0, tiled=True)  5.28 us
  transfers between devices with their start and end apart: 14, of which 7 were waited for; matrix products, arithmetic and copies ran while one was open for 3% of the time, Pallas kernels for 16%

profile of v4, /device:TPU:0, one launch (start us, length us, event | category | flops | bytes accessed | tf_op | source)
XLA Modules:
  0.0 133.0 jit_solution(14312052885877709837)
XLA Ops:
  0.6 3.2 %collective-permute-start = (bf16[4,4096]{1,0:T(4,128)(2,1)}, bf16[4,4096]{1,0:T(4,128)(2,1)S(1)}, u32[]{:S(2)}, u32[]{:S(2)}) collective-permute-start(bf16[4,4096]{1,0:T(4,128)(2,1)} %param.7), channel_id=1, source_target_pairs={{0,32},{2,34},{4,36},{6,38},{8,40},{10,42},{12,44},{14,46},{16,48}... | collective-permute-start | bytes 98312 | tf_op jit(solution)/shard_map/ppermute | solution.py:35
  3.8 0.8 copy-done
  4.6 1.0 shard_map.77
  5.6 8.3 %all-to-all-start = ((bf16[32,8,2048]{2,1,0:T(8,128)(2,1)}), bf16[32,8,2048]{2,1,0:T(8,128)(2,1)S(1)}, u32[]{:S(2)}, u32[]{:S(2)}) async-start(bf16[32,8,2048]{2,1,0:T(8,128)(2,1)} %shard_map.77), calls=%async_computation | async-start | bytes 2097152 | tf_op jit(solution)/shard_map/all_to_all | solution.py:295
  14.0 0.0 collective-permute-done
  14.0 0.8 select_bitcast_fusion.1
  14.8 1.1 shard_map.78
  15.9 15.7 %all-to-all-done = bf16[32,8,2048]{2,1,0:T(8,128)(2,1)S(1)} async-done(((bf16[32,8,2048]{2,1,0:T(8,128)(2,1)}), bf16[32,8,2048]{2,1,0:T(8,128)(2,1)S(1)}, u32[]{:S(2)}, u32[]{:S(2)}) %all-to-all-start) | async-done | bytes 1048608 | tf_op jit(solution)/shard_map/all_to_all | solution.py:295
  31.6 4.1 %all-to-all-start.1 = ((bf16[16,2,4,4096]{3,2,1,0:T(4,128)(2,1)}), bf16[16,2,4,4096]{3,2,1,0:T(4,128)(2,1)S(1)}, u32[]{:S(2)}, u32[]{:S(2)}) async-start(bf16[16,2,4,4096]{3,2,1,0:T(4,128)(2,1)} %shard_map.78), calls=%async_computation.1 | async-start | bytes 2097152 | tf_op jit(solution)/shard_map/all_to_all | solution.py:298
  35.8 0.1 stack.32.ids_ref
  35.8 3.4 %shard_map.79 = (f32[336,256]{1,0:T(8,128)S(1)}, f32[336,256]{1,0:T(8,128)S(1)}) custom-call(s32[5]{0:T(128)S(1)} %stack.32.ids_ref, bf16[2004,2,2048]{2,1,0:T(2,128)(2,1)} %bitcast.26, bf16[256,2048]{1,0:T(8,128)(2,1)S(1)} %bitcast.19), custom_call_target="tpu_custom_call" | custom-call | flops 1000 | bytes 1000 | tf_op jit(solution)/shard_map/pallas_call | solution.py:90
  39.2 0.1 collective-permute-start.1
  39.3 3.4 %shard_map.80 = (f32[336,256]{1,0:T(8,128)S(1)}, f32[336,256]{1,0:T(8,128)S(1)}) custom-call(s32[5]{0:T(128)S(1)} %stack.32.ids_ref, bf16[2004,2,2048]{2,1,0:T(2,128)(2,1)} %bitcast.27, bf16[256,2048]{1,0:T(8,128)(2,1)S(1)} %bitcast.20), custom_call_target="tpu_custom_call" | custom-call | flops 1000 | bytes 1000 | tf_op jit(solution)/shard_map/pallas_call | solution.py:90
  42.7 0.0 collective-permute-done.1
  42.7 0.6 collective-permute-start.2
  43.3 1.4 %collective-permute-start.3 = (f32[336,256]{1,0:T(8,128)S(1)}, f32[336,256]{1,0:T(8,128)S(1)}, u32[]{:S(2)}, u32[]{:S(2)}) collective-permute-start(f32[336,256]{1,0:T(8,128)S(1)} %add.41), channel_id=1, source_target_pairs={{0,1},{1,0},{2,3},{3,2},{4,5},{5,4},{6,7},{7,6},{8,9},{9,8},{10,11... | collective-permute-start | bytes 1032200 | tf_op jit(solution)/shard_map/ppermute | solution.py:43
  44.7 4.1 %shard_map.81 = (f32[336,256]{1,0:T(8,128)S(1)}, f32[336,256]{1,0:T(8,128)}) custom-call(s32[5]{0:T(128)S(1)} %stack.32.ids_ref, bf16[2004,2,2048]{2,1,0:T(2,128)(2,1)} %bitcast.28, bf16[256,2048]{1,0:T(8,128)(2,1)S(1)} %bitcast.21), custom_call_target="tpu_custom_call" | custom-call | flops 1000 | bytes 1000 | tf_op jit(solution)/shard_map/pallas_call | solution.py:90
  48.8 0.0 collective-permute-done.2
  48.8 0.8 add.42
  49.6 3.8 %collective-permute-done.3.refs_0_ = f32[336,256]{1,0:T(8,128)S(1)} collective-permute-done((f32[336,256]{1,0:T(8,128)S(1)}, f32[336,256]{1,0:T(8,128)S(1)}, u32[]{:S(2)}, u32[]{:S(2)}) %collective-permute-start.3) | collective-permute-done | bytes 344096 | tf_op jit(solution)/shard_map/ppermute | solution.py:43
  53.4 0.0 all-to-all-done.1.in_ref
  53.4 0.1 shard_map.82.own_ref
  53.5 0.0 slice-start.1
  53.5 0.1 collective-permute-start.4
  53.6 0.5 collective-permute-start.5
  54.1 1.4 %collective-permute-start.6 = (f32[336,256]{1,0:T(8,128)}, f32[336,256]{1,0:T(8,128)S(1)}, u32[]{:S(2)}, u32[]{:S(2)}) collective-permute-start(f32[336,256]{1,0:T(8,128)} %add.42), channel_id=1, source_target_pairs={{0,1},{1,0},{2,3},{3,2},{4,5},{5,4},{6,7},{7,6},{8,9},{9,8},{10,11... | collective-permute-start | bytes 1032200 | tf_op jit(solution)/shard_map/ppermute | solution.py:43
  55.5 5.6 %shard_map.83 = (f32[1008,256]{1,0:T(8,128)S(1)}, f32[1008,256]{1,0:T(8,128)S(1)}) custom-call(s32[5]{0:T(128)S(1)} %stack.32.ids_ref, bf16[2004,2,2048]{2,1,0:T(2,128)(2,1)} %bitcast.29, bf16[256,2048]{1,0:T(8,128)(2,1)S(1)} %bitcast.22), custom_call_target="tpu_custom_call" | custom-call | flops 1000 | bytes 1000 | tf_op jit(solution)/shard_map/pallas_call | solution.py:90
  61.1 0.0 copy-start.1
  61.1 0.0 collective-permute-done.5
  61.1 1.0 add.43
  62.2 2.2 %collective-permute-done.6.refs_1_ = f32[336,256]{1,0:T(8,128)S(1)} collective-permute-done((f32[336,256]{1,0:T(8,128)}, f32[336,256]{1,0:T(8,128)S(1)}, u32[]{:S(2)}, u32[]{:S(2)}) %collective-permute-start.6) | collective-permute-done | bytes 344096 | tf_op jit(solution)/shard_map/ppermute | solution.py:43
  64.3 1.4 %collective-permute-start.8 = (f32[336,256]{1,0:T(8,128)S(1)}, f32[336,256]{1,0:T(8,128)S(1)}, u32[]{:S(2)}, u32[]{:S(2)}) collective-permute-start(f32[336,256]{1,0:T(8,128)S(1)} %add.43), channel_id=1, source_target_pairs={{0,1},{1,0},{2,3},{3,2},{4,5},{5,4},{6,7},{7,6},{8,9},{9,8},{10,11... | collective-permute-start | bytes 1032200 | tf_op jit(solution)/shard_map/ppermute | solution.py:43
  65.8 3.1 %shard_map.84.refs_3_ = f32[1002,256]{1,0:T(8,128)S(1)} custom-call(s32[5]{0:T(128)S(1)} %stack.32.ids_ref, bf16[1002,4096]{1,0:T(8,128)(2,1)S(1)} %bitcast.17, bf16[128,4096]{1,0:T(8,128)(2,1)S(1)} %shard_map.82.own_ref, bf16[128,4096]{1,0:T(8,128)(2,1)S(1)} %collective-permute-done.4.other_ref), custom_call_target="tpu_custom_call" | custom-call | flops 1000 | bytes 1000 | tf_op jit(solution)/shard_map/pallas_call | solution.py:23
  68.8 6.0 %collective-permute-done.8.refs_2_ = f32[336,256]{1,0:T(8,128)S(1)} collective-permute-done((f32[336,256]{1,0:T(8,128)S(1)}, f32[336,256]{1,0:T(8,128)S(1)}, u32[]{:S(2)}, u32[]{:S(2)}) %collective-permute-start.8) | collective-permute-done | bytes 344096 | tf_op jit(solution)/shard_map/ppermute | solution.py:43
  74.8 0.0 collective-permute-done.7.core_ref
  74.8 1.7 %shard_map.85 = (f32[1002,256]{1,0:T(8,128)S(1)}, f32[1002,256]{1,0:T(8,128)S(1)}, f32[8,256]{1,0:T(8,128)S(1)}) custom-call(s32[5]{0:T(128)S(1)} %stack.32.ids_ref, f32[1008,256]{1,0:T(8,128)S(1)} %get-tuple-element.66.mine_ref, f32[1008,256]{1,0:T(8,128)S(1)} %collective-permute-done.7.core_ref, f32[336,256]{1,0:T(8,128)S(1)} %collective-permute-done.3.refs_0_, ...), custom_call_target="tpu_custom_call" | custom-call | flops 1000 | bytes 1000 | tf_op jit(solution)/shard_map/pallas_call | solution.py:23
  76.5 0.1 collective-permute-start.9
  76.6 1.2 collective-permute-done.9.refs_1_
  77.8 22.5 %all_to_all.20.in_ref = f32[64,8,256]{2,1,0:T(8,128)S(1)} all-to-all(f32[64,8,256]{2,1,0:T(8,128)S(1)} %shard_map.87), channel_id=1, replica_groups=mesh['grp'=2,'vocab'=32,'seq'=2] {'vocab','seq'}, dimensions={0} | all-to-all | bytes 1048576 | tf_op jit(solution)/shard_map/all_to_all | solution.py:323
  100.3 0.2 shard_map.88.st_ref
  100.6 3.2 %shard_map.89 = (f32[128,4096]{1,0:T(8,128)S(1)}, bf16[128,4096]{1,0:T(8,128)(2,1)S(1)}) custom-call(s32[5]{0:T(128)S(1)} %stack.32.ids_ref, bf16[1002,4096]{1,0:T(8,128)(2,1)S(1)} %bitcast.18, f32[1002,256]{1,0:T(8,128)S(1)} %get-tuple-element.73.te_ref, f32[1002,256]{1,0:T(8,128)S(1)} %get-tuple-element.74.se_ref, ...), custom_call_target="tpu_custom_call" | custom-call | flops 1000 | bytes 1000 | tf_op jit(solution)/shard_map/pallas_call | solution.py:23
  103.8 0.1 collective-permute-start.10
  103.9 2.6 %collective-permute-done.10.other_ref = bf16[128,4096]{1,0:T(8,128)(2,1)S(1)} collective-permute-done((bf16[128,4096]{1,0:T(8,128)(2,1)S(1)}, bf16[128,4096]{1,0:T(8,128)(2,1)S(1)}, u32[]{:S(2)}, u32[]{:S(2)}) %collective-permute-start.10) | collective-permute-done | bytes 1048608 | tf_op jit(solution)/shard_map/ppermute | solution.py:39
  106.5 2.1 %shard_map.90 = bf16[64,2,4096]{2,1,0:T(2,128)(2,1)} custom-call(f32[128,4096]{1,0:T(8,128)S(1)} %get-tuple-element.76.own_ref, bf16[128,4096]{1,0:T(8,128)(2,1)S(1)} %collective-permute-done.10.other_ref), custom_call_target="tpu_custom_call" | custom-call | flops 1000 | bytes 1000 | tf_op jit(solution)/shard_map/pallas_call | solution.py:23
  108.6 5.3 %all-to-all-start.3 = ((bf16[64,2,4096]{2,1,0:T(2,128)(2,1)}), bf16[64,2,4096]{2,1,0:T(2,128)(2,1)S(1)}, u32[]{:S(2)}, u32[]{:S(2)}) async-start(bf16[64,2,4096]{2,1,0:T(2,128)(2,1)} %shard_map.90), calls=%async_computation.3 | async-start | bytes 2097152 | tf_op jit(solution)/shard_map/all_to_all | solution.py:327
  113.9 0.6 slice_subtract_fusion
  114.5 17.7 %all-to-all-done.3.in_ref = bf16[64,2,4096]{2,1,0:T(2,128)(2,1)S(1)} async-done(((bf16[64,2,4096]{2,1,0:T(2,128)(2,1)}), bf16[64,2,4096]{2,1,0:T(2,128)(2,1)S(1)}, u32[]{:S(2)}, u32[]{:S(2)}) %all-to-all-start.3) | async-done | bytes 1048608 | tf_op jit(solution)/shard_map/all_to_all | solution.py:327
  132.2 0.8 shard_map.91
  (14 shorter events, 0.2 us)
Async XLA Ops:
  0.6 13.3 %collective-permute-start = (bf16[4,4096]{1,0:T(4,128)(2,1)}, bf16[4,4096]{1,0:T(4,128)(2,1)S(1)}, u32[]{:S(2)}, u32[]{:S(2)}) collective-permute-start(bf16[4,4096]{1,0:T(4,128)(2,1)} %param.7), channel_id=1, source_target_pairs={{0,32},{2,34},{4,36},{6,38},{8,40},{10,42},{12,44},{14,46},{16,48}... | collective-permute-start | bytes 98312 | tf_op jit(solution)/shard_map/ppermute | solution.py:35
  3.8 0.8 copy-start
  5.6 26.0 %all-to-all-start = ((bf16[32,8,2048]{2,1,0:T(8,128)(2,1)}), bf16[32,8,2048]{2,1,0:T(8,128)(2,1)S(1)}, u32[]{:S(2)}, u32[]{:S(2)}) async-start(bf16[32,8,2048]{2,1,0:T(8,128)(2,1)} %shard_map.77), calls=%async_computation | async-start | bytes 2097152 | tf_op jit(solution)/shard_map/all_to_all | solution.py:295
  31.6 21.8 %all-to-all-start.1 = ((bf16[16,2,4,4096]{3,2,1,0:T(4,128)(2,1)}), bf16[16,2,4,4096]{3,2,1,0:T(4,128)(2,1)S(1)}, u32[]{:S(2)}, u32[]{:S(2)}) async-start(bf16[16,2,4,4096]{3,2,1,0:T(4,128)(2,1)} %shard_map.78), calls=%async_computation.1 | async-start | bytes 2097152 | tf_op jit(solution)/shard_map/all_to_all | solution.py:298
  39.2 3.5 %collective-permute-start.1 = (f32[336,256]{1,0:T(8,128)S(1)}, f32[336,256]{1,0:T(8,128)S(1)}, u32[]{:S(2)}, u32[]{:S(2)}) collective-permute-start(f32[336,256]{1,0:T(8,128)S(1)} %get-tuple-element.46), channel_id=1, source_target_pairs={{0,64},{64,0},{1,65},{65,1},{2,66},{66,2},{3,67},{67,3},{4,68},{68... | collective-permute-start | bytes 1032200 | tf_op jit(solution)/shard_map/ppermute | solution.py:39
  42.7 6.1 %collective-permute-start.2 = (f32[336,256]{1,0:T(8,128)S(1)}, f32[336,256]{1,0:T(8,128)S(1)}, u32[]{:S(2)}, u32[]{:S(2)}) collective-permute-start(f32[336,256]{1,0:T(8,128)S(1)} %get-tuple-element.51), channel_id=1, source_target_pairs={{0,64},{64,0},{1,65},{65,1},{2,66},{66,2},{3,67},{67,3},{4,68},{68... | collective-permute-start | bytes 1032200 | tf_op jit(solution)/shard_map/ppermute | solution.py:39
  43.3 10.1 %collective-permute-start.3 = (f32[336,256]{1,0:T(8,128)S(1)}, f32[336,256]{1,0:T(8,128)S(1)}, u32[]{:S(2)}, u32[]{:S(2)}) collective-permute-start(f32[336,256]{1,0:T(8,128)S(1)} %add.41), channel_id=1, source_target_pairs={{0,1},{1,0},{2,3},{3,2},{4,5},{5,4},{6,7},{7,6},{8,9},{9,8},{10,11... | collective-permute-start | bytes 1032200 | tf_op jit(solution)/shard_map/ppermute | solution.py:43
  53.4 12.4 %slice-start = ((s8[8257536]{0:T(1024)(128)(4,1)}), s8[4194304]{0:T(1024)(128)(4,1)S(1)}, s32[]{:S(2)}) async-start(s8[8257536]{0:T(1024)(128)(4,1)} %bitcast.15), calls=%async_computation.4 | async-start | bytes 8388608
  53.5 12.3 %slice-start.1 = ((s8[8257536]{0:T(1024)(128)(4,1)}), s8[4063232]{0:T(1024)(128)(4,1)S(1)}, s32[]{:S(2)}) async-start(s8[8257536]{0:T(1024)(128)(4,1)} %bitcast.15), calls=%async_computation.5 | async-start | bytes 8126464
  53.5 10.9 %collective-permute-start.4 = (bf16[128,4096]{1,0:T(8,128)(2,1)S(1)}, bf16[128,4096]{1,0:T(8,128)(2,1)S(1)}, u32[]{:S(2)}, u32[]{:S(2)}) collective-permute-start(bf16[128,4096]{1,0:T(8,128)(2,1)S(1)} %shard_map.82.own_ref), channel_id=1, source_target_pairs={{0,64},{64,0},{1,65},{65,1},{2,66},{66,2},{3,67},{67,3},{4,68},{68... | collective-permute-start | bytes 3145736 | tf_op jit(solution)/shard_map/ppermute | solution.py:39
  53.6 7.6 %collective-permute-start.5 = (f32[336,256]{1,0:T(8,128)}, f32[336,256]{1,0:T(8,128)}, u32[]{:S(2)}, u32[]{:S(2)}) collective-permute-start(f32[336,256]{1,0:T(8,128)} %get-tuple-element.64), channel_id=1, source_target_pairs={{0,64},{64,0},{1,65},{65,1},{2,66},{66,2},{3,67},{67,3},{4,68},{68... | collective-permute-start | bytes 1032200 | tf_op jit(solution)/shard_map/ppermute | solution.py:39
  54.1 10.3 %collective-permute-start.6 = (f32[336,256]{1,0:T(8,128)}, f32[336,256]{1,0:T(8,128)S(1)}, u32[]{:S(2)}, u32[]{:S(2)}) collective-permute-start(f32[336,256]{1,0:T(8,128)} %add.42), channel_id=1, source_target_pairs={{0,1},{1,0},{2,3},{3,2},{4,5},{5,4},{6,7},{7,6},{8,9},{9,8},{10,11... | collective-permute-start | bytes 1032200 | tf_op jit(solution)/shard_map/ppermute | solution.py:43
  61.1 13.7 %copy-start.1 = (s32[256]{0:T(256)S(1)}, s32[256]{0:T(256)}, u32[]{:S(2)}) copy-start(s32[256]{0:T(256)} %param.10) | copy-start | bytes 3076
  64.3 10.5 %collective-permute-start.7 = (f32[1008,256]{1,0:T(8,128)S(1)}, f32[1008,256]{1,0:T(8,128)S(1)}, u32[]{:S(2)}, u32[]{:S(2)}) collective-permute-start(f32[1008,256]{1,0:T(8,128)S(1)} %get-tuple-element.67), channel_id=1, source_target_pairs={{0,64},{64,0},{1,65},{65,1},{2,66},{66,2},{3,67},{67,3},{4,68},{68... | collective-permute-start | bytes 3096584 | tf_op jit(solution)/shard_map/ppermute | solution.py:39
  64.3 10.5 %collective-permute-start.8 = (f32[336,256]{1,0:T(8,128)S(1)}, f32[336,256]{1,0:T(8,128)S(1)}, u32[]{:S(2)}, u32[]{:S(2)}) collective-permute-start(f32[336,256]{1,0:T(8,128)S(1)} %add.43), channel_id=1, source_target_pairs={{0,1},{1,0},{2,3},{3,2},{4,5},{5,4},{6,7},{7,6},{8,9},{9,8},{10,11... | collective-permute-start | bytes 1032200 | tf_op jit(solution)/shard_map/ppermute | solution.py:43
  65.8 34.8 %copy-start.2 = (f32[256]{0:T(256)S(1)}, f32[256]{0:T(256)}, u32[]{:S(2)}) copy-start(f32[256]{0:T(256)} %param.11) | copy-start | bytes 3076
  76.5 1.3 collective-permute-start.9
  103.8 2.7 %collective-permute-start.10 = (bf16[128,4096]{1,0:T(8,128)(2,1)S(1)}, bf16[128,4096]{1,0:T(8,128)(2,1)S(1)}, u32[]{:S(2)}, u32[]{:S(2)}) collective-permute-start(bf16[128,4096]{1,0:T(8,128)(2,1)S(1)} %get-tuple-element.77), channel_id=1, source_target_pairs={{0,64},{64,0},{1,65},{65,1},{2,66},{66,2},{3,67},{67,3},{4,68},{68... | collective-permute-start | bytes 3145736 | tf_op jit(solution)/shard_map/ppermute | solution.py:39
  108.6 23.6 %all-to-all-start.3 = ((bf16[64,2,4096]{2,1,0:T(2,128)(2,1)}), bf16[64,2,4096]{2,1,0:T(2,128)(2,1)S(1)}, u32[]{:S(2)}, u32[]{:S(2)}) async-start(bf16[64,2,4096]{2,1,0:T(2,128)(2,1)} %shard_map.90), calls=%async_computation.3 | async-start | bytes 2097152 | tf_op jit(solution)/shard_map/all_to_all | solution.py:327

commit v5 on v4

--- a/solution.py
+++ b/solution.py
@@ -105,46 +105,58 @@
     )(ids, head, rows)
 
 
-def student_product(head, own, other, ids):
+def hits(ids_ref, targets_ref, shape):
+    columns = ids_ref[4] + lax.broadcasted_iota(jnp.int32, shape, 0)
+    return columns == targets_ref[...]
+
+
+def student_product(head, own, other, targets, ids):
     width, depth = head.shape
     half = own.shape[0]
+    tokens = 2 * half
     block = 256
 
-    def kernel(ids_ref, w_ref, own_ref, other_ref, out_ref, xs):
+    def kernel(ids_ref, w_ref, own_ref, other_ref, t_ref, s_ref, e_ref, out_ref, xs):
         g = ids_ref[0]
         xs[pl.ds(pl.multiple_of(g * half, half), half), :] = own_ref[...]
         xs[pl.ds(pl.multiple_of((1 - g) * half, half), half), :] = other_ref[...]
         for start in range(0, width, block):
             rows = slice(start, min(start + block, width))
-            out_ref[rows, :] = lax.dot_general(
+            s_ref[rows, :] = lax.dot_general(
                 w_ref[rows, :], xs[...], (((1,), (1,)), ((), ())), preferred_element_type=F32
             )
-
+        s = s_ref[...]
+        top = jnp.max(s, axis=0, keepdims=True)
+        e = jnp.exp(s - top)
+        e_ref[...] = e
+        hit = hits(ids_ref, t_ref, s.shape)
+        out_ref[...] = jnp.zeros_like(out_ref)
+        out_ref[3:4, :] = top
+        out_ref[4:5, :] = jnp.sum(e, axis=0, keepdims=True)
+        out_ref[5:6, :] = jnp.sum(jnp.where(hit, s, jnp.zeros_like(s)), axis=0, keepdims=True)
+
+    logits = jax.ShapeDtypeStruct((width, tokens), F32)
     return call(
         kernel,
-        jax.ShapeDtypeStruct((width, 2 * half), F32),
+        [logits, logits, jax.ShapeDtypeStruct((8, tokens), F32)],
         ids,
         head,
         own,
         other,
-        in_specs=[SMEM, VMEM, VMEM, VMEM],
-        scratch=[pltpu.VMEM((2 * half, depth), BF16)],
+        targets,
+        in_specs=[SMEM] + [VMEM] * 4,
+        scratch=[pltpu.VMEM((tokens, depth), BF16)],
     )
 
 
-def hits(ids_ref, targets_ref, shape):
-    columns = ids_ref[4] + lax.broadcasted_iota(jnp.int32, shape, 0)
-    return columns == targets_ref[...]
-
-
-def local_stats(mine, core, near, student, targets, ids):
+def local_stats(mine, core, near, student, student_stats):
     width, tokens = student.shape
     step = width // BLOCKS
     padded = -(-step // 8) * 8
 
-    def kernel(ids_ref, mine_ref, core_ref, *refs):
+    def kernel(mine_ref, core_ref, *refs):
         near_refs = refs[: len(near)]
-        s_ref, t_ref, te_ref, se_ref, out_ref = refs[len(near) :]
+        s_ref, in_ref, te_ref, out_ref = refs[len(near) :]
         b = 0
         for ref in near_refs:
             for i in range(ref.shape[0] // padded):
@@ -153,32 +165,23 @@
                 own = mine_ref[here, :] + core_ref[here, :]
                 te_ref[b * step : (b + 1) * step, :] = own + ref[there, :]
                 b += 1
-        t, s = te_ref[...], s_ref[...]
-        t_top = jnp.max(t, axis=0, keepdims=True)
-        s_top = jnp.max(s, axis=0, keepdims=True)
-        e = jnp.exp(t - t_top)
+        t = te_ref[...]
+        top = jnp.max(t, axis=0, keepdims=True)
+        e = jnp.exp(t - top)
         te_ref[...] = e
-        out_ref[0:1, :] = t_top
+        out_ref[...] = in_ref[...]
+        out_ref[0:1, :] = top
         out_ref[1:2, :] = jnp.sum(e, axis=0, keepdims=True)
-        out_ref[2:3, :] = jnp.sum(e * (t - s), axis=0, keepdims=True)
-        out_ref[3:4, :] = s_top
-        e = jnp.exp(s - s_top)
-        se_ref[...] = e
-        out_ref[4:5, :] = jnp.sum(e, axis=0, keepdims=True)
-        hit = hits(ids_ref, t_ref, s.shape)
-        out_ref[5:6, :] = jnp.sum(jnp.where(hit, s, jnp.zeros_like(s)), axis=0, keepdims=True)
-        out_ref[6:8, :] = jnp.zeros((2, tokens), F32)
+        out_ref[2:3, :] = jnp.sum(e * (t - s_ref[...]), axis=0, keepdims=True)
 
     return call(
         kernel,
-        [jax.ShapeDtypeStruct((width, tokens), F32)] * 2 + [jax.ShapeDtypeStruct((8, tokens), F32)],
-        ids,
+        [jax.ShapeDtypeStruct((width, tokens), F32), jax.ShapeDtypeStruct((8, tokens), F32)],
         mine,
         core,
         *near,
         student,
-        targets,
-        in_specs=[SMEM] + [VMEM] * (4 + len(near)),
+        student_stats,
     )
 
 
@@ -261,8 +264,11 @@
     tokens, depth = own.shape
 
     def kernel(own_ref, other_ref, out_ref):
-        total = own_ref[...] + other_ref[...].astype(F32)
-        out_ref[...] = total.reshape(out_ref.shape).astype(BF16)
+        size = depth // 4
+        for start in range(0, depth, size):
+            cols = slice(start, start + size)
+            total = (own_ref[:, cols] + other_ref[:, cols].astype(F32)).astype(BF16)
+            out_ref[:, :, cols] = total.reshape(blocks, tokens // blocks, size)
 
     return call(kernel, jax.ShapeDtypeStruct((blocks, tokens // blocks, depth), BF16), own, other)
 
@@ -288,10 +294,11 @@
 
     after = lax.optimization_barrier
 
+    a = spread_rows(teacher_rows, lax.axis_size("vocab"))
+    a, student_rows = after((a, student_rows))
     near_b = swap_xhi(student_rows)
     pair = [jnp.where(vocab < 16, p, q) for p, q in ((student_rows, near_b), (near_b, student_rows))]
     b = spread_rows(jnp.stack(pair), 16)
-    a = spread_rows(teacher_rows, lax.axis_size("vocab"))
     a = lax.all_to_all(a, "vocab", 0, 0, tiled=True).reshape(-1, teacher_rows.shape[1])
     a, b = after((a, b))
     planes = [[x * 16 + i for i in range(16)] for x in range(2)]
@@ -315,9 +322,9 @@
     mine, other, b, b_other, sum2, near1 = after((mine, other, b, b_other, sum2, near1))
     near2 = swap_seq(sum2)
     core = swap_core(other)
-    student = student_product(s_head, b, b_other, ids)
+    logits, student, student_stats = student_product(s_head, b, b_other, targets2, ids)
     near = [near0, near1, near2]
-    teacher, student, here = local_stats(mine, core, near, student, targets2, ids)
+    teacher, here = local_stats(mine, core, near, logits, student_stats)
     stats = merge([here, swap_core(here)])
     stats = spread_rows(stats, 64)
     stats = merge_all(lax.all_to_all(stats, ("vocab", "seq"), 0, 0, tiled=True))

time: 134 us -> 132 us (0.985)
  Pallas kernels: 29.8 us -> 28.3 us
    pallas_call x11, Pallas kernels: 13.4 us -> 11.9 us  [call(): pl.pallas_call(kernel, out_shape=out_shape, in_specs=in_specs or [VMEM] *...]
where the time goes in v5:
time: 132 us; the launch traced here: 131 us
  waiting for transfers between devices  48.8 us (37%)
  Pallas kernels  28.3 us (21%)
  starting transfers between devices  26.5 us (20%)
  blocking collectives  22.5 us (17%)
  other arithmetic  3.26 us (2%)
    all_to_all x1, blocking collectives, body(): stats = merge_all(lax.all_to_all(stats, ('vocab', 'seq'), 0, 0, tiled=True))  22.5 us
    all_to_all x1, waiting for transfers between devices, body(): part = lax.all_to_all(part, ('vocab', 'seq'), 0, 0, tiled=True)  17.7 us
    pallas_call x4, Pallas kernels, teacher_part(): pl.pallas_call(kernel, grid_spec=pltpu.PrefetchScalarGridSpec(num_scalar_...  16.4 us
    all_to_all x1, waiting for transfers between devices, body(): lax.all_to_all(a, 'vocab', 0, 0, tiled=True)  15.7 us
    pallas_call x11, Pallas kernels, call(): pl.pallas_call(kernel, out_shape=out_shape, in_specs=in_specs or [VMEM] *...  11.9 us
    ppermute x3, waiting for transfers between devices, swap_seq(): return lax.ppermute(a, 'seq', [(0, 1), (1, 0)])  11.6 us
    all_to_all x1, starting transfers between devices, body(): lax.all_to_all(a, 'vocab', 0, 0, tiled=True)  8.33 us
    all_to_all x1, starting transfers between devices, body(): part = lax.all_to_all(part, ('vocab', 'seq'), 0, 0, tiled=True)  5.28 us
  transfers between devices with their start and end apart: 14, of which 7 were waited for; matrix products, arithmetic and copies ran while one was open for 3% of the time, Pallas kernels for 16%

profile of v5, /device:TPU:0, one launch (start us, length us, event | category | flops | bytes accessed | tf_op | source)
XLA Modules:
  0.0 131.2 jit_solution(877638634115748894)
XLA Ops:
  0.6 0.7 copy-done
  1.4 1.0 shard_map.77
  2.4 3.1 %collective-permute-start = (bf16[4,4096]{1,0:T(4,128)(2,1)}, bf16[4,4096]{1,0:T(4,128)(2,1)S(1)}, u32[]{:S(2)}, u32[]{:S(2)}) collective-permute-start(bf16[4,4096]{1,0:T(4,128)(2,1)} %param.7), channel_id=1, source_target_pairs={{0,32},{2,34},{4,36},{6,38},{8,40},{10,42},{12,44},{14,46},{16,48}... | collective-permute-start | bytes 98312 | tf_op jit(solution)/shard_map/ppermute | solution.py:35
  5.5 8.3 %all-to-all-start = ((bf16[32,8,2048]{2,1,0:T(8,128)(2,1)}), bf16[32,8,2048]{2,1,0:T(8,128)(2,1)S(1)}, u32[]{:S(2)}, u32[]{:S(2)}) async-start(bf16[32,8,2048]{2,1,0:T(8,128)(2,1)} %shard_map.77), calls=%async_computation | async-start | bytes 2097152 | tf_op jit(solution)/shard_map/all_to_all | solution.py:302
  13.9 0.0 collective-permute-done
  13.9 0.8 select_bitcast_fusion.1
  14.7 1.1 shard_map.78
  15.8 15.7 %all-to-all-done = bf16[32,8,2048]{2,1,0:T(8,128)(2,1)S(1)} async-done(((bf16[32,8,2048]{2,1,0:T(8,128)(2,1)}), bf16[32,8,2048]{2,1,0:T(8,128)(2,1)S(1)}, u32[]{:S(2)}, u32[]{:S(2)}) %all-to-all-start) | async-done | bytes 1048608 | tf_op jit(solution)/shard_map/all_to_all | solution.py:302
  31.5 4.1 %all-to-all-start.1 = ((bf16[16,2,4,4096]{3,2,1,0:T(4,128)(2,1)}), bf16[16,2,4,4096]{3,2,1,0:T(4,128)(2,1)S(1)}, u32[]{:S(2)}, u32[]{:S(2)}) async-start(bf16[16,2,4,4096]{3,2,1,0:T(4,128)(2,1)} %shard_map.78), calls=%async_computation.1 | async-start | bytes 2097152 | tf_op jit(solution)/shard_map/all_to_all | solution.py:305
  35.7 0.1 stack.32.ids_ref
  35.8 3.4 %shard_map.79 = (f32[336,256]{1,0:T(8,128)S(1)}, f32[336,256]{1,0:T(8,128)S(1)}) custom-call(s32[5]{0:T(128)S(1)} %stack.32.ids_ref, bf16[2004,2,2048]{2,1,0:T(2,128)(2,1)} %bitcast.26, bf16[256,2048]{1,0:T(8,128)(2,1)S(1)} %bitcast.19), custom_call_target="tpu_custom_call" | custom-call | flops 1000 | bytes 1000 | tf_op jit(solution)/shard_map/pallas_call | solution.py:90
  39.1 0.1 collective-permute-start.1
  39.2 3.4 %shard_map.80 = (f32[336,256]{1,0:T(8,128)S(1)}, f32[336,256]{1,0:T(8,128)S(1)}) custom-call(s32[5]{0:T(128)S(1)} %stack.32.ids_ref, bf16[2004,2,2048]{2,1,0:T(2,128)(2,1)} %bitcast.27, bf16[256,2048]{1,0:T(8,128)(2,1)S(1)} %bitcast.20), custom_call_target="tpu_custom_call" | custom-call | flops 1000 | bytes 1000 | tf_op jit(solution)/shard_map/pallas_call | solution.py:90
  42.6 0.0 collective-permute-done.1
  42.6 0.6 collective-permute-start.2
  43.2 1.4 %collective-permute-start.3 = (f32[336,256]{1,0:T(8,128)S(1)}, f32[336,256]{1,0:T(8,128)S(1)}, u32[]{:S(2)}, u32[]{:S(2)}) collective-permute-start(f32[336,256]{1,0:T(8,128)S(1)} %add.41), channel_id=1, source_target_pairs={{0,1},{1,0},{2,3},{3,2},{4,5},{5,4},{6,7},{7,6},{8,9},{9,8},{10,11... | collective-permute-start | bytes 1032200 | tf_op jit(solution)/shard_map/ppermute | solution.py:43
  44.6 4.1 %shard_map.81 = (f32[336,256]{1,0:T(8,128)S(1)}, f32[336,256]{1,0:T(8,128)}) custom-call(s32[5]{0:T(128)S(1)} %stack.32.ids_ref, bf16[2004,2,2048]{2,1,0:T(2,128)(2,1)} %bitcast.28, bf16[256,2048]{1,0:T(8,128)(2,1)S(1)} %bitcast.21), custom_call_target="tpu_custom_call" | custom-call | flops 1000 | bytes 1000 | tf_op jit(solution)/shard_map/pallas_call | solution.py:90
  48.7 0.0 collective-permute-done.2
  48.7 0.8 add.42
  49.5 3.8 %collective-permute-done.3.refs_0_ = f32[336,256]{1,0:T(8,128)S(1)} collective-permute-done((f32[336,256]{1,0:T(8,128)S(1)}, f32[336,256]{1,0:T(8,128)S(1)}, u32[]{:S(2)}, u32[]{:S(2)}) %collective-permute-start.3) | collective-permute-done | bytes 344096 | tf_op jit(solution)/shard_map/ppermute | solution.py:43
  53.3 0.0 all-to-all-done.1.in_ref
  53.3 0.1 shard_map.82.own_ref
  53.4 0.0 slice-start.1
  53.4 0.0 copy-start.1
  53.4 0.1 collective-permute-start.4
  53.5 0.5 collective-permute-start.5
  54.0 1.4 %collective-permute-start.6 = (f32[336,256]{1,0:T(8,128)}, f32[336,256]{1,0:T(8,128)S(1)}, u32[]{:S(2)}, u32[]{:S(2)}) collective-permute-start(f32[336,256]{1,0:T(8,128)} %add.42), channel_id=1, source_target_pairs={{0,1},{1,0},{2,3},{3,2},{4,5},{5,4},{6,7},{7,6},{8,9},{9,8},{10,11... | collective-permute-start | bytes 1032200 | tf_op jit(solution)/shard_map/ppermute | solution.py:43
  55.4 5.6 %shard_map.83 = (f32[1008,256]{1,0:T(8,128)S(1)}, f32[1008,256]{1,0:T(8,128)S(1)}) custom-call(s32[5]{0:T(128)S(1)} %stack.32.ids_ref, bf16[2004,2,2048]{2,1,0:T(2,128)(2,1)} %bitcast.29, bf16[256,2048]{1,0:T(8,128)(2,1)S(1)} %bitcast.22), custom_call_target="tpu_custom_call" | custom-call | flops 1000 | bytes 1000 | tf_op jit(solution)/shard_map/pallas_call | solution.py:90
  61.0 0.0 collective-permute-done.5
  61.1 1.0 add.43
  62.1 2.2 %collective-permute-done.6.refs_1_ = f32[336,256]{1,0:T(8,128)S(1)} collective-permute-done((f32[336,256]{1,0:T(8,128)}, f32[336,256]{1,0:T(8,128)S(1)}, u32[]{:S(2)}, u32[]{:S(2)}) %collective-permute-start.6) | collective-permute-done | bytes 344096 | tf_op jit(solution)/shard_map/ppermute | solution.py:43
  64.3 1.4 %collective-permute-start.8 = (f32[336,256]{1,0:T(8,128)S(1)}, f32[336,256]{1,0:T(8,128)S(1)}, u32[]{:S(2)}, u32[]{:S(2)}) collective-permute-start(f32[336,256]{1,0:T(8,128)S(1)} %add.43), channel_id=1, source_target_pairs={{0,1},{1,0},{2,3},{3,2},{4,5},{5,4},{6,7},{7,6},{8,9},{9,8},{10,11... | collective-permute-start | bytes 1032200 | tf_op jit(solution)/shard_map/ppermute | solution.py:43
  65.7 0.0 copy-start.2
  65.7 3.4 %shard_map.84 = (f32[1002,256]{1,0:T(8,128)S(1)}, f32[1002,256]{1,0:T(8,128)S(1)}, f32[8,256]{1,0:T(8,128)S(1)}) custom-call(s32[5]{0:T(128)S(1)} %stack.32.ids_ref, bf16[1002,4096]{1,0:T(8,128)(2,1)S(1)} %bitcast.17, bf16[128,4096]{1,0:T(8,128)(2,1)S(1)} %shard_map.82.own_ref, bf16[128,4096]{1,0:T(8,128)(2,1)S(1)} %collective-permute-done.4.other_ref, ...), custom_call_target="tpu_custom_call" | custom-call | flops 1000 | bytes 1000 | tf_op jit(solution)/shard_map/pallas_call | solution.py:23
  69.1 5.6 %collective-permute-done.8.refs_2_ = f32[336,256]{1,0:T(8,128)S(1)} collective-permute-done((f32[336,256]{1,0:T(8,128)S(1)}, f32[336,256]{1,0:T(8,128)S(1)}, u32[]{:S(2)}, u32[]{:S(2)}) %collective-permute-start.8) | collective-permute-done | bytes 344096 | tf_op jit(solution)/shard_map/ppermute | solution.py:43
  74.7 0.7 shard_map.85
  75.5 0.1 collective-permute-start.9
  75.6 1.2 collective-permute-done.9.refs_1_
  76.8 22.5 %all_to_all.20.in_ref = f32[64,8,256]{2,1,0:T(8,128)S(1)} all-to-all(f32[64,8,256]{2,1,0:T(8,128)S(1)} %shard_map.87), channel_id=1, replica_groups=mesh['grp'=2,'vocab'=32,'seq'=2] {'vocab','seq'}, dimensions={0} | all-to-all | bytes 1048576 | tf_op jit(solution)/shard_map/all_to_all | solution.py:330
  99.3 0.2 shard_map.88.st_ref
  99.5 3.2 %shard_map.89 = (f32[128,4096]{1,0:T(8,128)S(1)}, bf16[128,4096]{1,0:T(8,128)(2,1)S(1)}) custom-call(s32[5]{0:T(128)S(1)} %stack.32.ids_ref, bf16[1002,4096]{1,0:T(8,128)(2,1)S(1)} %bitcast.18, f32[1002,256]{1,0:T(8,128)S(1)} %get-tuple-element.81.te_ref, f32[1002,256]{1,0:T(8,128)S(1)} %get-tuple-element.82.se_ref, ...), custom_call_target="tpu_custom_call" | custom-call | flops 1000 | bytes 1000 | tf_op jit(solution)/shard_map/pallas_call | solution.py:23
  102.7 0.1 collective-permute-start.10
  102.8 2.6 %collective-permute-done.10.other_ref = bf16[128,4096]{1,0:T(8,128)(2,1)S(1)} collective-permute-done((bf16[128,4096]{1,0:T(8,128)(2,1)S(1)}, bf16[128,4096]{1,0:T(8,128)(2,1)S(1)}, u32[]{:S(2)}, u32[]{:S(2)}) %collective-permute-start.10) | collective-permute-done | bytes 1048608 | tf_op jit(solution)/shard_map/ppermute | solution.py:39
  105.5 1.3 %shard_map.90 = bf16[64,2,4096]{2,1,0:T(2,128)(2,1)} custom-call(f32[128,4096]{1,0:T(8,128)S(1)} %get-tuple-element.84.own_ref, bf16[128,4096]{1,0:T(8,128)(2,1)S(1)} %collective-permute-done.10.other_ref), custom_call_target="tpu_custom_call" | custom-call | flops 1000 | bytes 1000 | tf_op jit(solution)/shard_map/pallas_call | solution.py:23
  106.8 5.3 %all-to-all-start.3 = ((bf16[64,2,4096]{2,1,0:T(2,128)(2,1)}), bf16[64,2,4096]{2,1,0:T(2,128)(2,1)S(1)}, u32[]{:S(2)}, u32[]{:S(2)}) async-start(bf16[64,2,4096]{2,1,0:T(2,128)(2,1)} %shard_map.90), calls=%async_computation.3 | async-start | bytes 2097152 | tf_op jit(solution)/shard_map/all_to_all | solution.py:334
  112.1 0.6 slice_subtract_fusion
  112.7 17.7 %all-to-all-done.3.in_ref = bf16[64,2,4096]{2,1,0:T(2,128)(2,1)S(1)} async-done(((bf16[64,2,4096]{2,1,0:T(2,128)(2,1)}), bf16[64,2,4096]{2,1,0:T(2,128)(2,1)S(1)}, u32[]{:S(2)}, u32[]{:S(2)}) %all-to-all-start.3) | async-done | bytes 1048608 | tf_op jit(solution)/shard_map/all_to_all | solution.py:334
  130.4 0.8 shard_map.91
  (14 shorter events, 0.2 us)
Async XLA Ops:
  0.6 0.8 copy-start
  2.4 11.5 %collective-permute-start = (bf16[4,4096]{1,0:T(4,128)(2,1)}, bf16[4,4096]{1,0:T(4,128)(2,1)S(1)}, u32[]{:S(2)}, u32[]{:S(2)}) collective-permute-start(bf16[4,4096]{1,0:T(4,128)(2,1)} %param.7), channel_id=1, source_target_pairs={{0,32},{2,34},{4,36},{6,38},{8,40},{10,42},{12,44},{14,46},{16,48}... | collective-permute-start | bytes 98312 | tf_op jit(solution)/shard_map/ppermute | solution.py:35
  5.5 26.0 %all-to-all-start = ((bf16[32,8,2048]{2,1,0:T(8,128)(2,1)}), bf16[32,8,2048]{2,1,0:T(8,128)(2,1)S(1)}, u32[]{:S(2)}, u32[]{:S(2)}) async-start(bf16[32,8,2048]{2,1,0:T(8,128)(2,1)} %shard_map.77), calls=%async_computation | async-start | bytes 2097152 | tf_op jit(solution)/shard_map/all_to_all | solution.py:302
  31.5 21.8 %all-to-all-start.1 = ((bf16[16,2,4,4096]{3,2,1,0:T(4,128)(2,1)}), bf16[16,2,4,4096]{3,2,1,0:T(4,128)(2,1)S(1)}, u32[]{:S(2)}, u32[]{:S(2)}) async-start(bf16[16,2,4,4096]{3,2,1,0:T(4,128)(2,1)} %shard_map.78), calls=%async_computation.1 | async-start | bytes 2097152 | tf_op jit(solution)/shard_map/all_to_all | solution.py:305
  39.1 3.5 %collective-permute-start.1 = (f32[336,256]{1,0:T(8,128)S(1)}, f32[336,256]{1,0:T(8,128)S(1)}, u32[]{:S(2)}, u32[]{:S(2)}) collective-permute-start(f32[336,256]{1,0:T(8,128)S(1)} %get-tuple-element.52), channel_id=1, source_target_pairs={{0,64},{64,0},{1,65},{65,1},{2,66},{66,2},{3,67},{67,3},{4,68},{68... | collective-permute-start | bytes 1032200 | tf_op jit(solution)/shard_map/ppermute | solution.py:39
  42.6 6.1 %collective-permute-start.2 = (f32[336,256]{1,0:T(8,128)S(1)}, f32[336,256]{1,0:T(8,128)S(1)}, u32[]{:S(2)}, u32[]{:S(2)}) collective-permute-start(f32[336,256]{1,0:T(8,128)S(1)} %get-tuple-element.57), channel_id=1, source_target_pairs={{0,64},{64,0},{1,65},{65,1},{2,66},{66,2},{3,67},{67,3},{4,68},{68... | collective-permute-start | bytes 1032200 | tf_op jit(solution)/shard_map/ppermute | solution.py:39
  43.2 10.1 %collective-permute-start.3 = (f32[336,256]{1,0:T(8,128)S(1)}, f32[336,256]{1,0:T(8,128)S(1)}, u32[]{:S(2)}, u32[]{:S(2)}) collective-permute-start(f32[336,256]{1,0:T(8,128)S(1)} %add.41), channel_id=1, source_target_pairs={{0,1},{1,0},{2,3},{3,2},{4,5},{5,4},{6,7},{7,6},{8,9},{9,8},{10,11... | collective-permute-start | bytes 1032200 | tf_op jit(solution)/shard_map/ppermute | solution.py:43
  53.3 12.4 %slice-start = ((s8[8257536]{0:T(1024)(128)(4,1)}), s8[4194304]{0:T(1024)(128)(4,1)S(1)}, s32[]{:S(2)}) async-start(s8[8257536]{0:T(1024)(128)(4,1)} %bitcast.15), calls=%async_computation.4 | async-start | bytes 8388608
  53.4 12.3 %slice-start.1 = ((s8[8257536]{0:T(1024)(128)(4,1)}), s8[4063232]{0:T(1024)(128)(4,1)S(1)}, s32[]{:S(2)}) async-start(s8[8257536]{0:T(1024)(128)(4,1)} %bitcast.15), calls=%async_computation.5 | async-start | bytes 8126464
  53.4 12.3 %copy-start.1 = (s32[256]{0:T(256)S(1)}, s32[256]{0:T(256)}, u32[]{:S(2)}) copy-start(s32[256]{0:T(256)} %param.10) | copy-start | bytes 3076
  53.4 10.9 %collective-permute-start.4 = (bf16[128,4096]{1,0:T(8,128)(2,1)S(1)}, bf16[128,4096]{1,0:T(8,128)(2,1)S(1)}, u32[]{:S(2)}, u32[]{:S(2)}) collective-permute-start(bf16[128,4096]{1,0:T(8,128)(2,1)S(1)} %shard_map.82.own_ref), channel_id=1, source_target_pairs={{0,64},{64,0},{1,65},{65,1},{2,66},{66,2},{3,67},{67,3},{4,68},{68... | collective-permute-start | bytes 3145736 | tf_op jit(solution)/shard_map/ppermute | solution.py:39
  53.5 7.6 %collective-permute-start.5 = (f32[336,256]{1,0:T(8,128)}, f32[336,256]{1,0:T(8,128)}, u32[]{:S(2)}, u32[]{:S(2)}) collective-permute-start(f32[336,256]{1,0:T(8,128)} %get-tuple-element.70), channel_id=1, source_target_pairs={{0,64},{64,0},{1,65},{65,1},{2,66},{66,2},{3,67},{67,3},{4,68},{68... | collective-permute-start | bytes 1032200 | tf_op jit(solution)/shard_map/ppermute | solution.py:39
  54.0 10.3 %collective-permute-start.6 = (f32[336,256]{1,0:T(8,128)}, f32[336,256]{1,0:T(8,128)S(1)}, u32[]{:S(2)}, u32[]{:S(2)}) collective-permute-start(f32[336,256]{1,0:T(8,128)} %add.42), channel_id=1, source_target_pairs={{0,1},{1,0},{2,3},{3,2},{4,5},{5,4},{6,7},{7,6},{8,9},{9,8},{10,11... | collective-permute-start | bytes 1032200 | tf_op jit(solution)/shard_map/ppermute | solution.py:43
  64.3 10.5 %collective-permute-start.7 = (f32[1008,256]{1,0:T(8,128)S(1)}, f32[1008,256]{1,0:T(8,128)S(1)}, u32[]{:S(2)}, u32[]{:S(2)}) collective-permute-start(f32[1008,256]{1,0:T(8,128)S(1)} %get-tuple-element.73), channel_id=1, source_target_pairs={{0,64},{64,0},{1,65},{65,1},{2,66},{66,2},{3,67},{67,3},{4,68},{68... | collective-permute-start | bytes 3096584 | tf_op jit(solution)/shard_map/ppermute | solution.py:39
  64.3 10.5 %collective-permute-start.8 = (f32[336,256]{1,0:T(8,128)S(1)}, f32[336,256]{1,0:T(8,128)S(1)}, u32[]{:S(2)}, u32[]{:S(2)}) collective-permute-start(f32[336,256]{1,0:T(8,128)S(1)} %add.43), channel_id=1, source_target_pairs={{0,1},{1,0},{2,3},{3,2},{4,5},{5,4},{6,7},{7,6},{8,9},{9,8},{10,11... | collective-permute-start | bytes 1032200 | tf_op jit(solution)/shard_map/ppermute | solution.py:43
  65.7 33.8 %copy-start.2 = (f32[256]{0:T(256)S(1)}, f32[256]{0:T(256)}, u32[]{:S(2)}) copy-start(f32[256]{0:T(256)} %param.11) | copy-start | bytes 3076
  75.5 1.2 collective-permute-start.9
  102.7 2.7 %collective-permute-start.10 = (bf16[128,4096]{1,0:T(8,128)(2,1)S(1)}, bf16[128,4096]{1,0:T(8,128)(2,1)S(1)}, u32[]{:S(2)}, u32[]{:S(2)}) collective-permute-start(bf16[128,4096]{1,0:T(8,128)(2,1)S(1)} %get-tuple-element.85), channel_id=1, source_target_pairs={{0,64},{64,0},{1,65},{65,1},{2,66},{66,2},{3,67},{67,3},{4,68},{68... | collective-permute-start | bytes 3145736 | tf_op jit(solution)/shard_map/ppermute | solution.py:39
  106.8 23.6 %all-to-all-start.3 = ((bf16[64,2,4096]{2,1,0:T(2,128)(2,1)}), bf16[64,2,4096]{2,1,0:T(2,128)(2,1)S(1)}, u32[]{:S(2)}, u32[]{:S(2)}) async-start(bf16[64,2,4096]{2,1,0:T(2,128)(2,1)} %shard_map.90), calls=%async_computation.3 | async-start | bytes 2097152 | tf_op jit(solution)/shard_map/all_to_all | solution.py:334

commit v6 on v5

--- a/solution.py
+++ b/solution.py
@@ -61,45 +61,63 @@
     return call(kernel, jax.ShapeDtypeStruct((two * n * m, w), BF16), a)
 
 
-def teacher_part(head, rows, ids, mine, first, count):
+def teacher_part(head, rows, ids, mine, first, count, split=False):
     width, _, depth = head.shape
     step = width // (2 * BLOCKS)
     tokens = rows.shape[0]
     padded = -(-step // 8) * 8
-    pair = min(count, 3)
+    pair = 2 if split else min(count, 3)
+    steps = count // pair
 
     def place(i, ids_ref):
         part = ids_ref[1] if mine else 1 - ids_ref[1]
         return ((part * BLOCKS + first) // pair + i, 0, 0)
 
-    def kernel(ids_ref, w_ref, x_ref, own_ref, other_ref, acc):
+    def kernel(ids_ref, w_ref, x_ref, *refs):
+        acc = refs[-1]
         g = ids_ref[0]
         w = w_ref[...].reshape(2 * pair * step, depth)
         out = lax.dot_general(w, x_ref[...], (((1,), (1,)), ((), ())), preferred_element_type=F32)
         for lane in range(tokens // 128):
-            cols = slice(lane * 128, lane * 128 + 128)
-            acc[lane, 0 : 2 * pair * step, :] = out[:, cols]
-            for i in range(pair):
-                to = slice(i * padded, i * padded + step)
-                start = i * 2 * step
-                own_ref[to, cols] = acc[lane, pl.ds(start + g, step, stride=2), :]
-                other_ref[to, cols] = acc[lane, pl.ds(start + 1 - g, step, stride=2), :]
-
-    out = jax.ShapeDtypeStruct((count * padded, tokens), F32)
-    block = pl.BlockSpec((pair * padded, tokens), lambda i, r: (i, 0))
+            acc[lane, 0 : 2 * pair * step, :] = out[:, lane * 128 : lane * 128 + 128]
+
+        def store(own_ref, other_ref):
+            for lane in range(tokens // 128):
+                cols = slice(lane * 128, lane * 128 + 128)
+                for i in range(pair):
+                    to = slice(i * padded, i * padded + step)
+                    start = i * 2 * step
+                    own_ref[to, cols] = acc[lane, pl.ds(start + g, step, stride=2), :]
+                    other_ref[to, cols] = acc[lane, pl.ds(start + 1 - g, step, stride=2), :]
+
+        if split:
+            for j in range(steps):
+                pl.when(pl.program_id(0) == j)(
+                    functools.partial(store, refs[2 * j], refs[2 * j + 1])
+                )
+        else:
+            store(refs[0], refs[1])
+
+    if split:
+        out = jax.ShapeDtypeStruct((pair * padded, tokens), F32)
+        block = pl.BlockSpec((pair * padded, tokens), lambda i, r: (0, 0))
+    else:
+        out = jax.ShapeDtypeStruct((count * padded, tokens), F32)
+        block = pl.BlockSpec((pair * padded, tokens), lambda i, r: (i, 0))
+    outs = 2 * steps if split else 2
     return pl.pallas_call(
         kernel,
         grid_spec=pltpu.PrefetchScalarGridSpec(
             num_scalar_prefetch=1,
-            grid=(count // pair,),
+            grid=(steps,),
             in_specs=[
                 pl.BlockSpec((pair * step, 2, depth), place),
                 pl.BlockSpec((tokens, depth), lambda i, r: (0, 0)),
             ],
-            out_specs=[block, block],
+            out_specs=[block] * outs,
             scratch_shapes=[pltpu.VMEM((tokens // 128, 2 * pair * step + 20, 128), F32)],
         ),
-        out_shape=[out, out],
+        out_shape=[out] * outs,
         compiler_params=params(50),
         cost_estimate=TINY,
     )(ids, head, rows)
@@ -304,11 +322,9 @@
     planes = [[x * 16 + i for i in range(16)] for x in range(2)]
     b = lax.all_to_all(b, "vocab", 0, 0, axis_index_groups=planes, tiled=True)
 
-    own0, other0 = teacher_part(t_head, a, ids, False, 0, 2)
-    got0 = swap_core(other0)
-    a, own0 = after((a, own0))
-    own1, other1 = teacher_part(t_head, a, ids, False, 2, 2)
-    a, own1, other1, sum0 = after((a, own1, other1, own0 + got0))
+    own0, other0, own1, other1 = teacher_part(t_head, a, ids, False, 0, 4, split=True)
+    sum0 = own0 + swap_core(other0)
+    a, own1, other1, sum0 = after((a, own1, other1, sum0))
     near0 = swap_seq(sum0)
     sum1 = own1 + swap_core(other1)
     own2, other2 = teacher_part(t_head, a, ids, False, 4, 2)

time: 132 us -> 131 us (level)
  Pallas kernels: 28.3 us -> 25.9 us
  waiting for transfers between devices: 48.8 us -> 50.8 us
    pallas_call x4 -> x3, Pallas kernels: 16.4 us -> 14 us  [teacher_part(): pl.pallas_call(kernel, grid_spec=pltpu.PrefetchScalarGridSpec(num_scalar_...]
    ppermute x7, waiting for transfers between devices: 3.82 us -> 5.46 us  [swap_core(): return lax.ppermute(a, 'grp', [(0, 1), (1, 0)])]
  transfers between devices with their start and end apart: 14 -> 14, of which waited for: 7 -> 8; matrix products, arithmetic and copies ran while one was open for 3% -> 3% of each run, Pallas kernels for 16% -> 14%
where the time goes in v6:
time: 131 us; the launch traced here: 130 us
  waiting for transfers between devices  50.8 us (39%)
  starting transfers between devices  26.2 us (20%)
  Pallas kernels  25.9 us (20%)
  blocking collectives  22.5 us (17%)
  other arithmetic  3.27 us (2%)
    all_to_all x1, blocking collectives, body(): stats = merge_all(lax.all_to_all(stats, ('vocab', 'seq'), 0, 0, tiled=True))  22.5 us
    all_to_all x1, waiting for transfers between devices, body(): part = lax.all_to_all(part, ('vocab', 'seq'), 0, 0, tiled=True)  17.7 us
    all_to_all x1, waiting for transfers between devices, body(): lax.all_to_all(a, 'vocab', 0, 0, tiled=True)  15.7 us
    pallas_call x3, Pallas kernels, teacher_part(): pl.pallas_call(kernel, grid_spec=pltpu.PrefetchScalarGridSpec(num_scalar_...  14 us
    pallas_call x11, Pallas kernels, call(): pl.pallas_call(kernel, out_shape=out_shape, in_specs=in_specs or [VMEM] *...  11.9 us
    ppermute x3, waiting for transfers between devices, swap_seq(): return lax.ppermute(a, 'seq', [(0, 1), (1, 0)])  11.9 us
    all_to_all x1, starting transfers between devices, body(): lax.all_to_all(a, 'vocab', 0, 0, tiled=True)  8.33 us
    ppermute x7, waiting for transfers between devices, swap_core(): return lax.ppermute(a, 'grp', [(0, 1), (1, 0)])  5.46 us
  transfers between devices with their start and end apart: 14, of which 8 were waited for; matrix products, arithmetic and copies ran while one was open for 3% of the time, Pallas kernels for 14%

profile of v6, /device:TPU:0, one launch (start us, length us, event | category | flops | bytes accessed | tf_op | source)
XLA Modules:
  0.0 130.4 jit_solution(3974154768718389157)
XLA Ops:
  0.6 0.7 copy-done
  1.4 1.0 shard_map.77
  2.4 3.1 %collective-permute-start = (bf16[4,4096]{1,0:T(4,128)(2,1)}, bf16[4,4096]{1,0:T(4,128)(2,1)S(1)}, u32[]{:S(2)}, u32[]{:S(2)}) collective-permute-start(bf16[4,4096]{1,0:T(4,128)(2,1)} %param.7), channel_id=1, source_target_pairs={{0,32},{2,34},{4,36},{6,38},{8,40},{10,42},{12,44},{14,46},{16,48}... | collective-permute-start | bytes 98312 | tf_op jit(solution)/shard_map/ppermute | solution.py:35
  5.5 8.3 %all-to-all-start = ((bf16[32,8,2048]{2,1,0:T(8,128)(2,1)}), bf16[32,8,2048]{2,1,0:T(8,128)(2,1)S(1)}, u32[]{:S(2)}, u32[]{:S(2)}) async-start(bf16[32,8,2048]{2,1,0:T(8,128)(2,1)} %shard_map.77), calls=%async_computation | async-start | bytes 2097152 | tf_op jit(solution)/shard_map/all_to_all | solution.py:320
  13.9 0.0 collective-permute-done
  13.9 0.8 select_bitcast_fusion.1
  14.7 1.1 shard_map.78
  15.8 15.7 %all-to-all-done = bf16[32,8,2048]{2,1,0:T(8,128)(2,1)S(1)} async-done(((bf16[32,8,2048]{2,1,0:T(8,128)(2,1)}), bf16[32,8,2048]{2,1,0:T(8,128)(2,1)S(1)}, u32[]{:S(2)}, u32[]{:S(2)}) %all-to-all-start) | async-done | bytes 1048608 | tf_op jit(solution)/shard_map/all_to_all | solution.py:320
  31.5 4.1 %all-to-all-start.1 = ((bf16[16,2,4,4096]{3,2,1,0:T(4,128)(2,1)}), bf16[16,2,4,4096]{3,2,1,0:T(4,128)(2,1)S(1)}, u32[]{:S(2)}, u32[]{:S(2)}) async-start(bf16[16,2,4,4096]{3,2,1,0:T(4,128)(2,1)} %shard_map.78), calls=%async_computation.1 | async-start | bytes 2097152 | tf_op jit(solution)/shard_map/all_to_all | solution.py:323
  35.7 0.1 stack.32.ids_ref
  35.8 4.4 %shard_map.79 = (f32[336,256]{1,0:T(8,128)S(1)}, f32[336,256]{1,0:T(8,128)S(1)}, f32[336,256]{1,0:T(8,128)S(1)}, f32[336,256]{1,0:T(8,128)S(1)}) custom-call(s32[5]{0:T(128)S(1)} %stack.32.ids_ref, bf16[2004,2,2048]{2,1,0:T(2,128)(2,1)} %bitcast.25, bf16[256,2048]{1,0:T(8,128)(2,1)S(1)} %bitcast.19), custom_call_target="tpu_custom_call" | custom-call | flops 1000 | bytes 1000 | tf_op jit(solution)/shard_map/pallas_call | solution.py:108
  40.1 0.1 collective-permute-start.1
  40.2 1.6 %collective-permute-done.1 = f32[336,256]{1,0:T(8,128)S(1)} collective-permute-done((f32[336,256]{1,0:T(8,128)S(1)}, f32[336,256]{1,0:T(8,128)S(1)}, u32[]{:S(2)}, u32[]{:S(2)}) %collective-permute-start.1) | collective-permute-done | bytes 344096 | tf_op jit(solution)/shard_map/ppermute | solution.py:39
  41.9 0.2 collective-permute-start.2
  42.1 1.5 %collective-permute-start.3 = (f32[336,256]{1,0:T(8,128)S(1)}, f32[336,256]{1,0:T(8,128)S(1)}, u32[]{:S(2)}, u32[]{:S(2)}) collective-permute-start(f32[336,256]{1,0:T(8,128)S(1)} %add.41), channel_id=1, source_target_pairs={{0,1},{1,0},{2,3},{3,2},{4,5},{5,4},{6,7},{7,6},{8,9},{9,8},{10,11... | collective-permute-start | bytes 1032200 | tf_op jit(solution)/shard_map/ppermute | solution.py:43
  43.6 4.1 %shard_map.80 = (f32[336,256]{1,0:T(8,128)S(1)}, f32[336,256]{1,0:T(8,128)}) custom-call(s32[5]{0:T(128)S(1)} %stack.32.ids_ref, bf16[2004,2,2048]{2,1,0:T(2,128)(2,1)} %bitcast.26, bf16[256,2048]{1,0:T(8,128)(2,1)S(1)} %bitcast.20), custom_call_target="tpu_custom_call" | custom-call | flops 1000 | bytes 1000 | tf_op jit(solution)/shard_map/pallas_call | solution.py:108
  47.7 0.0 collective-permute-done.2
  47.7 0.8 add.42
  48.5 4.0 %collective-permute-done.3.refs_0_ = f32[336,256]{1,0:T(8,128)S(1)} collective-permute-done((f32[336,256]{1,0:T(8,128)S(1)}, f32[336,256]{1,0:T(8,128)S(1)}, u32[]{:S(2)}, u32[]{:S(2)}) %collective-permute-start.3) | collective-permute-done | bytes 344096 | tf_op jit(solution)/shard_map/ppermute | solution.py:43
  52.5 0.0 all-to-all-done.1.in_ref
  52.5 0.1 shard_map.81.own_ref
  52.6 0.0 slice-start.1
  52.6 0.0 copy-start.1
  52.6 0.1 collective-permute-start.4
  52.7 0.5 collective-permute-start.5
  53.2 1.4 %collective-permute-start.6 = (f32[336,256]{1,0:T(8,128)}, f32[336,256]{1,0:T(8,128)S(1)}, u32[]{:S(2)}, u32[]{:S(2)}) collective-permute-start(f32[336,256]{1,0:T(8,128)} %add.42), channel_id=1, source_target_pairs={{0,1},{1,0},{2,3},{3,2},{4,5},{5,4},{6,7},{7,6},{8,9},{9,8},{10,11... | collective-permute-start | bytes 1032200 | tf_op jit(solution)/shard_map/ppermute | solution.py:43
  54.6 5.6 %shard_map.82 = (f32[1008,256]{1,0:T(8,128)S(1)}, f32[1008,256]{1,0:T(8,128)S(1)}) custom-call(s32[5]{0:T(128)S(1)} %stack.32.ids_ref, bf16[2004,2,2048]{2,1,0:T(2,128)(2,1)} %bitcast.27, bf16[256,2048]{1,0:T(8,128)(2,1)S(1)} %bitcast.21), custom_call_target="tpu_custom_call" | custom-call | flops 1000 | bytes 1000 | tf_op jit(solution)/shard_map/pallas_call | solution.py:108
  60.2 1.0 add.43
  61.2 2.2 %collective-permute-done.6.refs_1_ = f32[336,256]{1,0:T(8,128)S(1)} collective-permute-done((f32[336,256]{1,0:T(8,128)}, f32[336,256]{1,0:T(8,128)S(1)}, u32[]{:S(2)}, u32[]{:S(2)}) %collective-permute-start.6) | collective-permute-done | bytes 344096 | tf_op jit(solution)/shard_map/ppermute | solution.py:43
  63.5 0.0 collective-permute-done.4.other_ref
  63.5 0.0 collective-permute-start.7
  63.5 1.4 %collective-permute-start.8 = (f32[336,256]{1,0:T(8,128)S(1)}, f32[336,256]{1,0:T(8,128)S(1)}, u32[]{:S(2)}, u32[]{:S(2)}) collective-permute-start(f32[336,256]{1,0:T(8,128)S(1)} %add.43), channel_id=1, source_target_pairs={{0,1},{1,0},{2,3},{3,2},{4,5},{5,4},{6,7},{7,6},{8,9},{9,8},{10,11... | collective-permute-start | bytes 1032200 | tf_op jit(solution)/shard_map/ppermute | solution.py:43
  64.9 0.0 copy-start.2
  64.9 3.4 %shard_map.83 = (f32[1002,256]{1,0:T(8,128)S(1)}, f32[1002,256]{1,0:T(8,128)S(1)}, f32[8,256]{1,0:T(8,128)S(1)}) custom-call(s32[5]{0:T(128)S(1)} %stack.32.ids_ref, bf16[1002,4096]{1,0:T(8,128)(2,1)S(1)} %bitcast.17, bf16[128,4096]{1,0:T(8,128)(2,1)S(1)} %shard_map.81.own_ref, bf16[128,4096]{1,0:T(8,128)(2,1)S(1)} %collective-permute-done.4.other_ref, ...), custom_call_target="tpu_custom_call" | custom-call | flops 1000 | bytes 1000 | tf_op jit(solution)/shard_map/pallas_call | solution.py:23
  68.3 5.6 %collective-permute-done.8.refs_2_ = f32[336,256]{1,0:T(8,128)S(1)} collective-permute-done((f32[336,256]{1,0:T(8,128)S(1)}, f32[336,256]{1,0:T(8,128)S(1)}, u32[]{:S(2)}, u32[]{:S(2)}) %collective-permute-start.8) | collective-permute-done | bytes 344096 | tf_op jit(solution)/shard_map/ppermute | solution.py:43
  74.0 0.7 shard_map.84
  74.7 0.1 collective-permute-start.9
  74.8 1.2 collective-permute-done.9.refs_1_
  76.0 22.5 %all_to_all.20.in_ref = f32[64,8,256]{2,1,0:T(8,128)S(1)} all-to-all(f32[64,8,256]{2,1,0:T(8,128)S(1)} %shard_map.86), channel_id=1, replica_groups=mesh['grp'=2,'vocab'=32,'seq'=2] {'vocab','seq'}, dimensions={0} | all-to-all | bytes 1048576 | tf_op jit(solution)/shard_map/all_to_all | solution.py:346
  98.5 0.2 shard_map.87.st_ref
  98.7 3.2 %shard_map.88 = (f32[128,4096]{1,0:T(8,128)S(1)}, bf16[128,4096]{1,0:T(8,128)(2,1)S(1)}) custom-call(s32[5]{0:T(128)S(1)} %stack.32.ids_ref, bf16[1002,4096]{1,0:T(8,128)(2,1)S(1)} %bitcast.18, f32[1002,256]{1,0:T(8,128)S(1)} %get-tuple-element.77.te_ref, f32[1002,256]{1,0:T(8,128)S(1)} %get-tuple-element.78.se_ref, ...), custom_call_target="tpu_custom_call" | custom-call | flops 1000 | bytes 1000 | tf_op jit(solution)/shard_map/pallas_call | solution.py:23
  102.0 0.1 collective-permute-start.10
  102.1 2.6 %collective-permute-done.10.other_ref = bf16[128,4096]{1,0:T(8,128)(2,1)S(1)} collective-permute-done((bf16[128,4096]{1,0:T(8,128)(2,1)S(1)}, bf16[128,4096]{1,0:T(8,128)(2,1)S(1)}, u32[]{:S(2)}, u32[]{:S(2)}) %collective-permute-start.10) | collective-permute-done | bytes 1048608 | tf_op jit(solution)/shard_map/ppermute | solution.py:39
  104.7 1.3 %shard_map.89 = bf16[64,2,4096]{2,1,0:T(2,128)(2,1)} custom-call(f32[128,4096]{1,0:T(8,128)S(1)} %get-tuple-element.80.own_ref, bf16[128,4096]{1,0:T(8,128)(2,1)S(1)} %collective-permute-done.10.other_ref), custom_call_target="tpu_custom_call" | custom-call | flops 1000 | bytes 1000 | tf_op jit(solution)/shard_map/pallas_call | solution.py:23
  106.0 5.3 %all-to-all-start.3 = ((bf16[64,2,4096]{2,1,0:T(2,128)(2,1)}), bf16[64,2,4096]{2,1,0:T(2,128)(2,1)S(1)}, u32[]{:S(2)}, u32[]{:S(2)}) async-start(bf16[64,2,4096]{2,1,0:T(2,128)(2,1)} %shard_map.89), calls=%async_computation.3 | async-start | bytes 2097152 | tf_op jit(solution)/shard_map/all_to_all | solution.py:350
  111.3 0.6 slice_subtract_fusion
  111.9 17.7 %all-to-all-done.3.in_ref = bf16[64,2,4096]{2,1,0:T(2,128)(2,1)S(1)} async-done(((bf16[64,2,4096]{2,1,0:T(2,128)(2,1)}), bf16[64,2,4096]{2,1,0:T(2,128)(2,1)S(1)}, u32[]{:S(2)}, u32[]{:S(2)}) %all-to-all-start.3) | async-done | bytes 1048608 | tf_op jit(solution)/shard_map/all_to_all | solution.py:350
  129.6 0.8 shard_map.90
  (13 shorter events, 0.2 us)
Async XLA Ops:
  0.6 0.8 copy-start
  2.4 11.5 %collective-permute-start = (bf16[4,4096]{1,0:T(4,128)(2,1)}, bf16[4,4096]{1,0:T(4,128)(2,1)S(1)}, u32[]{:S(2)}, u32[]{:S(2)}) collective-permute-start(bf16[4,4096]{1,0:T(4,128)(2,1)} %param.7), channel_id=1, source_target_pairs={{0,32},{2,34},{4,36},{6,38},{8,40},{10,42},{12,44},{14,46},{16,48}... | collective-permute-start | bytes 98312 | tf_op jit(solution)/shard_map/ppermute | solution.py:35
  5.5 26.0 %all-to-all-start = ((bf16[32,8,2048]{2,1,0:T(8,128)(2,1)}), bf16[32,8,2048]{2,1,0:T(8,128)(2,1)S(1)}, u32[]{:S(2)}, u32[]{:S(2)}) async-start(bf16[32,8,2048]{2,1,0:T(8,128)(2,1)} %shard_map.77), calls=%async_computation | async-start | bytes 2097152 | tf_op jit(solution)/shard_map/all_to_all | solution.py:320
  31.5 21.0 %all-to-all-start.1 = ((bf16[16,2,4,4096]{3,2,1,0:T(4,128)(2,1)}), bf16[16,2,4,4096]{3,2,1,0:T(4,128)(2,1)S(1)}, u32[]{:S(2)}, u32[]{:S(2)}) async-start(bf16[16,2,4,4096]{3,2,1,0:T(4,128)(2,1)} %shard_map.78), calls=%async_computation.1 | async-start | bytes 2097152 | tf_op jit(solution)/shard_map/all_to_all | solution.py:323
  40.1 1.7 %collective-permute-start.1 = (f32[336,256]{1,0:T(8,128)S(1)}, f32[336,256]{1,0:T(8,128)S(1)}, u32[]{:S(2)}, u32[]{:S(2)}) collective-permute-start(f32[336,256]{1,0:T(8,128)S(1)} %get-tuple-element.48), channel_id=1, source_target_pairs={{0,64},{64,0},{1,65},{65,1},{2,66},{66,2},{3,67},{67,3},{4,68},{68... | collective-permute-start | bytes 1032200 | tf_op jit(solution)/shard_map/ppermute | solution.py:39
  41.9 5.7 %collective-permute-start.2 = (f32[336,256]{1,0:T(8,128)S(1)}, f32[336,256]{1,0:T(8,128)S(1)}, u32[]{:S(2)}, u32[]{:S(2)}) collective-permute-start(f32[336,256]{1,0:T(8,128)S(1)} %get-tuple-element.53), channel_id=1, source_target_pairs={{0,64},{64,0},{1,65},{65,1},{2,66},{66,2},{3,67},{67,3},{4,68},{68... | collective-permute-start | bytes 1032200 | tf_op jit(solution)/shard_map/ppermute | solution.py:39
  42.1 10.3 %collective-permute-start.3 = (f32[336,256]{1,0:T(8,128)S(1)}, f32[336,256]{1,0:T(8,128)S(1)}, u32[]{:S(2)}, u32[]{:S(2)}) collective-permute-start(f32[336,256]{1,0:T(8,128)S(1)} %add.41), channel_id=1, source_target_pairs={{0,1},{1,0},{2,3},{3,2},{4,5},{5,4},{6,7},{7,6},{8,9},{9,8},{10,11... | collective-permute-start | bytes 1032200 | tf_op jit(solution)/shard_map/ppermute | solution.py:43
  52.5 12.4 %slice-start = ((s8[8257536]{0:T(1024)(128)(4,1)}), s8[4194304]{0:T(1024)(128)(4,1)S(1)}, s32[]{:S(2)}) async-start(s8[8257536]{0:T(1024)(128)(4,1)} %bitcast.15), calls=%async_computation.4 | async-start | bytes 8388608
  52.6 12.3 %slice-start.1 = ((s8[8257536]{0:T(1024)(128)(4,1)}), s8[4063232]{0:T(1024)(128)(4,1)S(1)}, s32[]{:S(2)}) async-start(s8[8257536]{0:T(1024)(128)(4,1)} %bitcast.15), calls=%async_computation.5 | async-start | bytes 8126464
  52.6 12.3 %copy-start.1 = (s32[256]{0:T(256)S(1)}, s32[256]{0:T(256)}, u32[]{:S(2)}) copy-start(s32[256]{0:T(256)} %param.10) | copy-start | bytes 3076
  52.6 10.9 %collective-permute-start.4 = (bf16[128,4096]{1,0:T(8,128)(2,1)S(1)}, bf16[128,4096]{1,0:T(8,128)(2,1)S(1)}, u32[]{:S(2)}, u32[]{:S(2)}) collective-permute-start(bf16[128,4096]{1,0:T(8,128)(2,1)S(1)} %shard_map.81.own_ref), channel_id=1, source_target_pairs={{0,64},{64,0},{1,65},{65,1},{2,66},{66,2},{3,67},{67,3},{4,68},{68... | collective-permute-start | bytes 3145736 | tf_op jit(solution)/shard_map/ppermute | solution.py:39
  52.7 7.5 %collective-permute-start.5 = (f32[336,256]{1,0:T(8,128)}, f32[336,256]{1,0:T(8,128)}, u32[]{:S(2)}, u32[]{:S(2)}) collective-permute-start(f32[336,256]{1,0:T(8,128)} %get-tuple-element.66), channel_id=1, source_target_pairs={{0,64},{64,0},{1,65},{65,1},{2,66},{66,2},{3,67},{67,3},{4,68},{68... | collective-permute-start | bytes 1032200 | tf_op jit(solution)/shard_map/ppermute | solution.py:39
  53.2 10.3 %collective-permute-start.6 = (f32[336,256]{1,0:T(8,128)}, f32[336,256]{1,0:T(8,128)S(1)}, u32[]{:S(2)}, u32[]{:S(2)}) collective-permute-start(f32[336,256]{1,0:T(8,128)} %add.42), channel_id=1, source_target_pairs={{0,1},{1,0},{2,3},{3,2},{4,5},{5,4},{6,7},{7,6},{8,9},{9,8},{10,11... | collective-permute-start | bytes 1032200 | tf_op jit(solution)/shard_map/ppermute | solution.py:43
  63.5 10.5 %collective-permute-start.7 = (f32[1008,256]{1,0:T(8,128)S(1)}, f32[1008,256]{1,0:T(8,128)S(1)}, u32[]{:S(2)}, u32[]{:S(2)}) collective-permute-start(f32[1008,256]{1,0:T(8,128)S(1)} %get-tuple-element.69), channel_id=1, source_target_pairs={{0,64},{64,0},{1,65},{65,1},{2,66},{66,2},{3,67},{67,3},{4,68},{68... | collective-permute-start | bytes 3096584 | tf_op jit(solution)/shard_map/ppermute | solution.py:39
  63.5 10.5 %collective-permute-start.8 = (f32[336,256]{1,0:T(8,128)S(1)}, f32[336,256]{1,0:T(8,128)S(1)}, u32[]{:S(2)}, u32[]{:S(2)}) collective-permute-start(f32[336,256]{1,0:T(8,128)S(1)} %add.43), channel_id=1, source_target_pairs={{0,1},{1,0},{2,3},{3,2},{4,5},{5,4},{6,7},{7,6},{8,9},{9,8},{10,11... | collective-permute-start | bytes 1032200 | tf_op jit(solution)/shard_map/ppermute | solution.py:43
  64.9 33.8 %copy-start.2 = (f32[256]{0:T(256)S(1)}, f32[256]{0:T(256)}, u32[]{:S(2)}) copy-start(f32[256]{0:T(256)} %param.11) | copy-start | bytes 3076
  74.7 1.2 collective-permute-start.9
  102.0 2.7 %collective-permute-start.10 = (bf16[128,4096]{1,0:T(8,128)(2,1)S(1)}, bf16[128,4096]{1,0:T(8,128)(2,1)S(1)}, u32[]{:S(2)}, u32[]{:S(2)}) collective-permute-start(bf16[128,4096]{1,0:T(8,128)(2,1)S(1)} %get-tuple-element.81), channel_id=1, source_target_pairs={{0,64},{64,0},{1,65},{65,1},{2,66},{66,2},{3,67},{67,3},{4,68},{68... | collective-permute-start | bytes 3145736 | tf_op jit(solution)/shard_map/ppermute | solution.py:39
  106.0 23.6 %all-to-all-start.3 = ((bf16[64,2,4096]{2,1,0:T(2,128)(2,1)}), bf16[64,2,4096]{2,1,0:T(2,128)(2,1)S(1)}, u32[]{:S(2)}, u32[]{:S(2)}) async-start(bf16[64,2,4096]{2,1,0:T(2,128)(2,1)} %shard_map.89), calls=%async_computation.3 | async-start | bytes 2097152 | tf_op jit(solution)/shard_map/all_to_all | solution.py:350

commit v7 on v6

--- a/solution.py
+++ b/solution.py
@@ -203,9 +203,9 @@
     )
 
 
-def merge(stats):
+def merge(stats, copies):
     def kernel(*refs):
-        out_ref = refs[-1]
+        out_ref = refs[-1].at[0]
         values = [r[...] for r in refs[:-1]]
 
         def row(v, i):
@@ -219,8 +219,11 @@
                 out_ref[i : i + 1, :] = sum(c * row(v, i) for c, v in zip(scale, values))
         out_ref[5:6, :] = sum(row(v, 5) for v in values)
         out_ref[6:8, :] = values[0][6:8, :]
-
-    return call(kernel, jax.ShapeDtypeStruct(stats[0].shape, F32), *stats)
+        merged = out_ref[...]
+        for i in range(1, copies):
+            refs[-1][i] = merged
+
+    return call(kernel, jax.ShapeDtypeStruct((copies,) + stats[0].shape, F32), *stats)
 
 
 def merge_all(stats):
@@ -341,8 +344,7 @@
     logits, student, student_stats = student_product(s_head, b, b_other, targets2, ids)
     near = [near0, near1, near2]
     teacher, here = local_stats(mine, core, near, logits, student_stats)
-    stats = merge([here, swap_core(here)])
-    stats = spread_rows(stats, 64)
+    stats = merge([here, swap_core(here)], 64)
     stats = merge_all(lax.all_to_all(stats, ("vocab", "seq"), 0, 0, tiled=True))
 
     own, other = hidden_part(s_head, teacher, student, here, stats, targets2, loss_grad2, ids)

time: 131 us -> 131 us (level)
    pallas_call x11 -> x10, Pallas kernels: 11.9 us -> 11.9 us  [call(): pl.pallas_call(kernel, out_shape=out_shape, in_specs=in_specs or [VMEM] *...]
where the time goes in v7:
time: 131 us; the launch traced here: 130 us
  waiting for transfers between devices  50.8 us (39%)
  starting transfers between devices  26.2 us (20%)
  Pallas kernels  25.9 us (20%)
  blocking collectives  22.5 us (17%)
  other arithmetic  3.27 us (2%)
    all_to_all x1, blocking collectives, body(): stats = merge_all(lax.all_to_all(stats, ('vocab', 'seq'), 0, 0, tiled=True))  22.5 us
    all_to_all x1, waiting for transfers between devices, body(): part = lax.all_to_all(part, ('vocab', 'seq'), 0, 0, tiled=True)  17.7 us
    all_to_all x1, waiting for transfers between devices, body(): lax.all_to_all(a, 'vocab', 0, 0, tiled=True)  15.7 us
    pallas_call x3, Pallas kernels, teacher_part(): pl.pallas_call(kernel, grid_spec=pltpu.PrefetchScalarGridSpec(num_scalar_...  14 us
    pallas_call x10, Pallas kernels, call(): pl.pallas_call(kernel, out_shape=out_shape, in_specs=in_specs or [VMEM] *...  11.9 us
    ppermute x3, waiting for transfers between devices, swap_seq(): return lax.ppermute(a, 'seq', [(0, 1), (1, 0)])  11.9 us
    all_to_all x1, starting transfers between devices, body(): lax.all_to_all(a, 'vocab', 0, 0, tiled=True)  8.33 us
    ppermute x7, waiting for transfers between devices, swap_core(): return lax.ppermute(a, 'grp', [(0, 1), (1, 0)])  5.46 us
  transfers between devices with their start and end apart: 14, of which 8 were waited for; matrix products, arithmetic and copies ran while one was open for 3% of the time, Pallas kernels for 14%

profile of v7, /device:TPU:0, one launch (start us, length us, event | category | flops | bytes accessed | tf_op | source)
XLA Modules:
  0.0 130.4 jit_solution(12859892158888321958)
XLA Ops:
  0.6 0.7 copy-done
  1.4 1.0 shard_map.77
  2.4 3.1 %collective-permute-start = (bf16[4,4096]{1,0:T(4,128)(2,1)}, bf16[4,4096]{1,0:T(4,128)(2,1)S(1)}, u32[]{:S(2)}, u32[]{:S(2)}) collective-permute-start(bf16[4,4096]{1,0:T(4,128)(2,1)} %param.7), channel_id=1, source_target_pairs={{0,32},{2,34},{4,36},{6,38},{8,40},{10,42},{12,44},{14,46},{16,48}... | collective-permute-start | bytes 98312 | tf_op jit(solution)/shard_map/ppermute | solution.py:35
  5.5 8.3 %all-to-all-start = ((bf16[32,8,2048]{2,1,0:T(8,128)(2,1)}), bf16[32,8,2048]{2,1,0:T(8,128)(2,1)S(1)}, u32[]{:S(2)}, u32[]{:S(2)}) async-start(bf16[32,8,2048]{2,1,0:T(8,128)(2,1)} %shard_map.77), calls=%async_computation | async-start | bytes 2097152 | tf_op jit(solution)/shard_map/all_to_all | solution.py:323
  13.9 0.0 collective-permute-done
  13.9 0.8 select_bitcast_fusion.1
  14.7 1.1 shard_map.78
  15.8 15.7 %all-to-all-done = bf16[32,8,2048]{2,1,0:T(8,128)(2,1)S(1)} async-done(((bf16[32,8,2048]{2,1,0:T(8,128)(2,1)}), bf16[32,8,2048]{2,1,0:T(8,128)(2,1)S(1)}, u32[]{:S(2)}, u32[]{:S(2)}) %all-to-all-start) | async-done | bytes 1048608 | tf_op jit(solution)/shard_map/all_to_all | solution.py:323
  31.5 4.1 %all-to-all-start.1 = ((bf16[16,2,4,4096]{3,2,1,0:T(4,128)(2,1)}), bf16[16,2,4,4096]{3,2,1,0:T(4,128)(2,1)S(1)}, u32[]{:S(2)}, u32[]{:S(2)}) async-start(bf16[16,2,4,4096]{3,2,1,0:T(4,128)(2,1)} %shard_map.78), calls=%async_computation.1 | async-start | bytes 2097152 | tf_op jit(solution)/shard_map/all_to_all | solution.py:326
  35.7 0.1 stack.32.ids_ref
  35.8 4.4 %shard_map.79 = (f32[336,256]{1,0:T(8,128)S(1)}, f32[336,256]{1,0:T(8,128)S(1)}, f32[336,256]{1,0:T(8,128)S(1)}, f32[336,256]{1,0:T(8,128)S(1)}) custom-call(s32[5]{0:T(128)S(1)} %stack.32.ids_ref, bf16[2004,2,2048]{2,1,0:T(2,128)(2,1)} %bitcast.25, bf16[256,2048]{1,0:T(8,128)(2,1)S(1)} %bitcast.19), custom_call_target="tpu_custom_call" | custom-call | flops 1000 | bytes 1000 | tf_op jit(solution)/shard_map/pallas_call | solution.py:108
  40.1 0.1 collective-permute-start.1
  40.2 1.6 %collective-permute-done.1 = f32[336,256]{1,0:T(8,128)S(1)} collective-permute-done((f32[336,256]{1,0:T(8,128)S(1)}, f32[336,256]{1,0:T(8,128)S(1)}, u32[]{:S(2)}, u32[]{:S(2)}) %collective-permute-start.1) | collective-permute-done | bytes 344096 | tf_op jit(solution)/shard_map/ppermute | solution.py:39
  41.9 0.2 collective-permute-start.2
  42.1 1.5 %collective-permute-start.3 = (f32[336,256]{1,0:T(8,128)S(1)}, f32[336,256]{1,0:T(8,128)S(1)}, u32[]{:S(2)}, u32[]{:S(2)}) collective-permute-start(f32[336,256]{1,0:T(8,128)S(1)} %add.41), channel_id=1, source_target_pairs={{0,1},{1,0},{2,3},{3,2},{4,5},{5,4},{6,7},{7,6},{8,9},{9,8},{10,11... | collective-permute-start | bytes 1032200 | tf_op jit(solution)/shard_map/ppermute | solution.py:43
  43.6 4.1 %shard_map.80 = (f32[336,256]{1,0:T(8,128)S(1)}, f32[336,256]{1,0:T(8,128)}) custom-call(s32[5]{0:T(128)S(1)} %stack.32.ids_ref, bf16[2004,2,2048]{2,1,0:T(2,128)(2,1)} %bitcast.26, bf16[256,2048]{1,0:T(8,128)(2,1)S(1)} %bitcast.20), custom_call_target="tpu_custom_call" | custom-call | flops 1000 | bytes 1000 | tf_op jit(solution)/shard_map/pallas_call | solution.py:108
  47.7 0.0 collective-permute-done.2
  47.7 0.8 add.42
  48.5 4.0 %collective-permute-done.3.refs_0_ = f32[336,256]{1,0:T(8,128)S(1)} collective-permute-done((f32[336,256]{1,0:T(8,128)S(1)}, f32[336,256]{1,0:T(8,128)S(1)}, u32[]{:S(2)}, u32[]{:S(2)}) %collective-permute-start.3) | collective-permute-done | bytes 344096 | tf_op jit(solution)/shard_map/ppermute | solution.py:43
  52.5 0.0 all-to-all-done.1.in_ref
  52.5 0.1 shard_map.81.own_ref
  52.6 0.0 slice-start.1
  52.6 0.0 copy-start.1
  52.6 0.1 collective-permute-start.4
  52.7 0.5 collective-permute-start.5
  53.2 1.4 %collective-permute-start.6 = (f32[336,256]{1,0:T(8,128)}, f32[336,256]{1,0:T(8,128)S(1)}, u32[]{:S(2)}, u32[]{:S(2)}) collective-permute-start(f32[336,256]{1,0:T(8,128)} %add.42), channel_id=1, source_target_pairs={{0,1},{1,0},{2,3},{3,2},{4,5},{5,4},{6,7},{7,6},{8,9},{9,8},{10,11... | collective-permute-start | bytes 1032200 | tf_op jit(solution)/shard_map/ppermute | solution.py:43
  54.6 5.6 %shard_map.82 = (f32[1008,256]{1,0:T(8,128)S(1)}, f32[1008,256]{1,0:T(8,128)S(1)}) custom-call(s32[5]{0:T(128)S(1)} %stack.32.ids_ref, bf16[2004,2,2048]{2,1,0:T(2,128)(2,1)} %bitcast.27, bf16[256,2048]{1,0:T(8,128)(2,1)S(1)} %bitcast.21), custom_call_target="tpu_custom_call" | custom-call | flops 1000 | bytes 1000 | tf_op jit(solution)/shard_map/pallas_call | solution.py:108
  60.2 1.0 add.43
  61.2 2.2 %collective-permute-done.6.refs_1_ = f32[336,256]{1,0:T(8,128)S(1)} collective-permute-done((f32[336,256]{1,0:T(8,128)}, f32[336,256]{1,0:T(8,128)S(1)}, u32[]{:S(2)}, u32[]{:S(2)}) %collective-permute-start.6) | collective-permute-done | bytes 344096 | tf_op jit(solution)/shard_map/ppermute | solution.py:43
  63.5 0.0 collective-permute-done.4.other_ref
  63.5 1.4 %collective-permute-start.8 = (f32[336,256]{1,0:T(8,128)S(1)}, f32[336,256]{1,0:T(8,128)S(1)}, u32[]{:S(2)}, u32[]{:S(2)}) collective-permute-start(f32[336,256]{1,0:T(8,128)S(1)} %add.43), channel_id=1, source_target_pairs={{0,1},{1,0},{2,3},{3,2},{4,5},{5,4},{6,7},{7,6},{8,9},{9,8},{10,11... | collective-permute-start | bytes 1032200 | tf_op jit(solution)/shard_map/ppermute | solution.py:43
  64.9 0.0 copy-start.2
  64.9 3.4 %shard_map.83 = (f32[1002,256]{1,0:T(8,128)S(1)}, f32[1002,256]{1,0:T(8,128)S(1)}, f32[8,256]{1,0:T(8,128)S(1)}) custom-call(s32[5]{0:T(128)S(1)} %stack.32.ids_ref, bf16[1002,4096]{1,0:T(8,128)(2,1)S(1)} %bitcast.17, bf16[128,4096]{1,0:T(8,128)(2,1)S(1)} %shard_map.81.own_ref, bf16[128,4096]{1,0:T(8,128)(2,1)S(1)} %collective-permute-done.4.other_ref, ...), custom_call_target="tpu_custom_call" | custom-call | flops 1000 | bytes 1000 | tf_op jit(solution)/shard_map/pallas_call | solution.py:23
  68.3 5.6 %collective-permute-done.8.refs_2_ = f32[336,256]{1,0:T(8,128)S(1)} collective-permute-done((f32[336,256]{1,0:T(8,128)S(1)}, f32[336,256]{1,0:T(8,128)S(1)}, u32[]{:S(2)}, u32[]{:S(2)}) %collective-permute-start.8) | collective-permute-done | bytes 344096 | tf_op jit(solution)/shard_map/ppermute | solution.py:43
  74.0 0.7 shard_map.84
  74.7 0.1 collective-permute-start.9
  74.8 1.2 collective-permute-done.9.refs_1_
  76.0 0.1 shard_map.85
  76.0 22.5 %all_to_all.20.in_ref = f32[64,8,256]{2,1,0:T(8,128)S(1)} all-to-all(f32[64,8,256]{2,1,0:T(8,128)S(1)} %shard_map.85), channel_id=1, replica_groups=mesh['grp'=2,'vocab'=32,'seq'=2] {'vocab','seq'}, dimensions={0} | all-to-all | bytes 1048576 | tf_op jit(solution)/shard_map/all_to_all | solution.py:348
  98.5 0.2 shard_map.86.st_ref
  98.7 3.2 %shard_map.87 = (f32[128,4096]{1,0:T(8,128)S(1)}, bf16[128,4096]{1,0:T(8,128)(2,1)S(1)}) custom-call(s32[5]{0:T(128)S(1)} %stack.32.ids_ref, bf16[1002,4096]{1,0:T(8,128)(2,1)S(1)} %bitcast.18, f32[1002,256]{1,0:T(8,128)S(1)} %get-tuple-element.77.te_ref, f32[1002,256]{1,0:T(8,128)S(1)} %get-tuple-element.78.se_ref, ...), custom_call_target="tpu_custom_call" | custom-call | flops 1000 | bytes 1000 | tf_op jit(solution)/shard_map/pallas_call | solution.py:23
  102.0 0.1 collective-permute-start.10
  102.1 2.6 %collective-permute-done.10.other_ref = bf16[128,4096]{1,0:T(8,128)(2,1)S(1)} collective-permute-done((bf16[128,4096]{1,0:T(8,128)(2,1)S(1)}, bf16[128,4096]{1,0:T(8,128)(2,1)S(1)}, u32[]{:S(2)}, u32[]{:S(2)}) %collective-permute-start.10) | collective-permute-done | bytes 1048608 | tf_op jit(solution)/shard_map/ppermute | solution.py:39
  104.7 1.3 %shard_map.88 = bf16[64,2,4096]{2,1,0:T(2,128)(2,1)} custom-call(f32[128,4096]{1,0:T(8,128)S(1)} %get-tuple-element.80.own_ref, bf16[128,4096]{1,0:T(8,128)(2,1)S(1)} %collective-permute-done.10.other_ref), custom_call_target="tpu_custom_call" | custom-call | flops 1000 | bytes 1000 | tf_op jit(solution)/shard_map/pallas_call | solution.py:23
  106.0 5.3 %all-to-all-start.3 = ((bf16[64,2,4096]{2,1,0:T(2,128)(2,1)}), bf16[64,2,4096]{2,1,0:T(2,128)(2,1)S(1)}, u32[]{:S(2)}, u32[]{:S(2)}) async-start(bf16[64,2,4096]{2,1,0:T(2,128)(2,1)} %shard_map.88), calls=%async_computation.3 | async-start | bytes 2097152 | tf_op jit(solution)/shard_map/all_to_all | solution.py:352
  111.3 0.6 slice_subtract_fusion
  111.9 17.7 %all-to-all-done.3.in_ref = bf16[64,2,4096]{2,1,0:T(2,128)(2,1)S(1)} async-done(((bf16[64,2,4096]{2,1,0:T(2,128)(2,1)}), bf16[64,2,4096]{2,1,0:T(2,128)(2,1)S(1)}, u32[]{:S(2)}, u32[]{:S(2)}) %all-to-all-start.3) | async-done | bytes 1048608 | tf_op jit(solution)/shard_map/all_to_all | solution.py:352
  129.6 0.8 shard_map.89
  (12 shorter events, 0.1 us)
Async XLA Ops:
  0.6 0.8 copy-start
  2.4 11.5 %collective-permute-start = (bf16[4,4096]{1,0:T(4,128)(2,1)}, bf16[4,4096]{1,0:T(4,128)(2,1)S(1)}, u32[]{:S(2)}, u32[]{:S(2)}) collective-permute-start(bf16[4,4096]{1,0:T(4,128)(2,1)} %param.7), channel_id=1, source_target_pairs={{0,32},{2,34},{4,36},{6,38},{8,40},{10,42},{12,44},{14,46},{16,48}... | collective-permute-start | bytes 98312 | tf_op jit(solution)/shard_map/ppermute | solution.py:35
  5.5 26.0 %all-to-all-start = ((bf16[32,8,2048]{2,1,0:T(8,128)(2,1)}), bf16[32,8,2048]{2,1,0:T(8,128)(2,1)S(1)}, u32[]{:S(2)}, u32[]{:S(2)}) async-start(bf16[32,8,2048]{2,1,0:T(8,128)(2,1)} %shard_map.77), calls=%async_computation | async-start | bytes 2097152 | tf_op jit(solution)/shard_map/all_to_all | solution.py:323
  31.5 21.0 %all-to-all-start.1 = ((bf16[16,2,4,4096]{3,2,1,0:T(4,128)(2,1)}), bf16[16,2,4,4096]{3,2,1,0:T(4,128)(2,1)S(1)}, u32[]{:S(2)}, u32[]{:S(2)}) async-start(bf16[16,2,4,4096]{3,2,1,0:T(4,128)(2,1)} %shard_map.78), calls=%async_computation.1 | async-start | bytes 2097152 | tf_op jit(solution)/shard_map/all_to_all | solution.py:326
  40.1 1.7 %collective-permute-start.1 = (f32[336,256]{1,0:T(8,128)S(1)}, f32[336,256]{1,0:T(8,128)S(1)}, u32[]{:S(2)}, u32[]{:S(2)}) collective-permute-start(f32[336,256]{1,0:T(8,128)S(1)} %get-tuple-element.48), channel_id=1, source_target_pairs={{0,64},{64,0},{1,65},{65,1},{2,66},{66,2},{3,67},{67,3},{4,68},{68... | collective-permute-start | bytes 1032200 | tf_op jit(solution)/shard_map/ppermute | solution.py:39
  41.9 5.7 %collective-permute-start.2 = (f32[336,256]{1,0:T(8,128)S(1)}, f32[336,256]{1,0:T(8,128)S(1)}, u32[]{:S(2)}, u32[]{:S(2)}) collective-permute-start(f32[336,256]{1,0:T(8,128)S(1)} %get-tuple-element.53), channel_id=1, source_target_pairs={{0,64},{64,0},{1,65},{65,1},{2,66},{66,2},{3,67},{67,3},{4,68},{68... | collective-permute-start | bytes 1032200 | tf_op jit(solution)/shard_map/ppermute | solution.py:39
  42.1 10.3 %collective-permute-start.3 = (f32[336,256]{1,0:T(8,128)S(1)}, f32[336,256]{1,0:T(8,128)S(1)}, u32[]{:S(2)}, u32[]{:S(2)}) collective-permute-start(f32[336,256]{1,0:T(8,128)S(1)} %add.41), channel_id=1, source_target_pairs={{0,1},{1,0},{2,3},{3,2},{4,5},{5,4},{6,7},{7,6},{8,9},{9,8},{10,11... | collective-permute-start | bytes 1032200 | tf_op jit(solution)/shard_map/ppermute | solution.py:43
  52.5 12.4 %slice-start = ((s8[8257536]{0:T(1024)(128)(4,1)}), s8[4194304]{0:T(1024)(128)(4,1)S(1)}, s32[]{:S(2)}) async-start(s8[8257536]{0:T(1024)(128)(4,1)} %bitcast.15), calls=%async_computation.4 | async-start | bytes 8388608
  52.6 12.3 %slice-start.1 = ((s8[8257536]{0:T(1024)(128)(4,1)}), s8[4063232]{0:T(1024)(128)(4,1)S(1)}, s32[]{:S(2)}) async-start(s8[8257536]{0:T(1024)(128)(4,1)} %bitcast.15), calls=%async_computation.5 | async-start | bytes 8126464
  52.6 12.3 %copy-start.1 = (s32[256]{0:T(256)S(1)}, s32[256]{0:T(256)}, u32[]{:S(2)}) copy-start(s32[256]{0:T(256)} %param.10) | copy-start | bytes 3076
  52.6 10.9 %collective-permute-start.4 = (bf16[128,4096]{1,0:T(8,128)(2,1)S(1)}, bf16[128,4096]{1,0:T(8,128)(2,1)S(1)}, u32[]{:S(2)}, u32[]{:S(2)}) collective-permute-start(bf16[128,4096]{1,0:T(8,128)(2,1)S(1)} %shard_map.81.own_ref), channel_id=1, source_target_pairs={{0,64},{64,0},{1,65},{65,1},{2,66},{66,2},{3,67},{67,3},{4,68},{68... | collective-permute-start | bytes 3145736 | tf_op jit(solution)/shard_map/ppermute | solution.py:39
  52.7 7.5 %collective-permute-start.5 = (f32[336,256]{1,0:T(8,128)}, f32[336,256]{1,0:T(8,128)}, u32[]{:S(2)}, u32[]{:S(2)}) collective-permute-start(f32[336,256]{1,0:T(8,128)} %get-tuple-element.66), channel_id=1, source_target_pairs={{0,64},{64,0},{1,65},{65,1},{2,66},{66,2},{3,67},{67,3},{4,68},{68... | collective-permute-start | bytes 1032200 | tf_op jit(solution)/shard_map/ppermute | solution.py:39
  53.2 10.3 %collective-permute-start.6 = (f32[336,256]{1,0:T(8,128)}, f32[336,256]{1,0:T(8,128)S(1)}, u32[]{:S(2)}, u32[]{:S(2)}) collective-permute-start(f32[336,256]{1,0:T(8,128)} %add.42), channel_id=1, source_target_pairs={{0,1},{1,0},{2,3},{3,2},{4,5},{5,4},{6,7},{7,6},{8,9},{9,8},{10,11... | collective-permute-start | bytes 1032200 | tf_op jit(solution)/shard_map/ppermute | solution.py:43
  63.5 10.5 %collective-permute-start.7 = (f32[1008,256]{1,0:T(8,128)S(1)}, f32[1008,256]{1,0:T(8,128)S(1)}, u32[]{:S(2)}, u32[]{:S(2)}) collective-permute-start(f32[1008,256]{1,0:T(8,128)S(1)} %get-tuple-element.69), channel_id=1, source_target_pairs={{0,64},{64,0},{1,65},{65,1},{2,66},{66,2},{3,67},{67,3},{4,68},{68... | collective-permute-start | bytes 3096584 | tf_op jit(solution)/shard_map/ppermute | solution.py:39
  63.5 10.5 %collective-permute-start.8 = (f32[336,256]{1,0:T(8,128)S(1)}, f32[336,256]{1,0:T(8,128)S(1)}, u32[]{:S(2)}, u32[]{:S(2)}) collective-permute-start(f32[336,256]{1,0:T(8,128)S(1)} %add.43), channel_id=1, source_target_pairs={{0,1},{1,0},{2,3},{3,2},{4,5},{5,4},{6,7},{7,6},{8,9},{9,8},{10,11... | collective-permute-start | bytes 1032200 | tf_op jit(solution)/shard_map/ppermute | solution.py:43
  64.9 33.8 %copy-start.2 = (f32[256]{0:T(256)S(1)}, f32[256]{0:T(256)}, u32[]{:S(2)}) copy-start(f32[256]{0:T(256)} %param.11) | copy-start | bytes 3076
  74.7 1.2 collective-permute-start.9
  102.0 2.7 %collective-permute-start.10 = (bf16[128,4096]{1,0:T(8,128)(2,1)S(1)}, bf16[128,4096]{1,0:T(8,128)(2,1)S(1)}, u32[]{:S(2)}, u32[]{:S(2)}) collective-permute-start(bf16[128,4096]{1,0:T(8,128)(2,1)S(1)} %get-tuple-element.81), channel_id=1, source_target_pairs={{0,64},{64,0},{1,65},{65,1},{2,66},{66,2},{3,67},{67,3},{4,68},{68... | collective-permute-start | bytes 3145736 | tf_op jit(solution)/shard_map/ppermute | solution.py:39
  106.0 23.6 %all-to-all-start.3 = ((bf16[64,2,4096]{2,1,0:T(2,128)(2,1)}), bf16[64,2,4096]{2,1,0:T(2,128)(2,1)S(1)}, u32[]{:S(2)}, u32[]{:S(2)}) async-start(bf16[64,2,4096]{2,1,0:T(2,128)(2,1)} %shard_map.88), calls=%async_computation.3 | async-start | bytes 2097152 | tf_op jit(solution)/shard_map/all_to_all | solution.py:352
